TPU v7x, 32 devices: a whole 2x2x4 slice. The times are simulated.
32 devices in a mesh: event: 2 (over x), phi: 16 (over z, y, core).
Axes of the slice: x: 2, y: 2, z: 4, core: 2. Of those that a mesh axis runs over, the one named last changes fastest.
Arguments:
- hit_feats: bfloat16 [12, 131072], P(None, ('event', 'phi')), parts along dimension 1, may hold values from -6 to 6
- layer_ids: int32 [131072], P(('event', 'phi')), parts along dimension 0, may hold values from 0 to 15
- edge_tiles: bfloat16 [1024, 8, 128, 128], P(('event', 'phi')), parts along dimension 0
- src_blocks: int32 [1024, 8], P(('event', 'phi')), parts along dimension 0, may hold values from 0 to 159
- live_slots: int32 [1024], P(('event', 'phi')), parts along dimension 0, may hold values from 1 to 8, as said below
- anchor_hits: int32 [32768], P(('event', 'phi')), parts along dimension 0, may hold values from 0 to 4095
- positive_hits: int32 [32768], P(('event', 'phi')), parts along dimension 0, may hold values from 0 to 20479
- negative_hits: int32 [32768], P(('event', 'phi')), parts along dimension 0, may hold values from 0 to 20479
- w_enc: bfloat16 [12, 128], replicated, may hold values from -1.75 to 1.75
- layer_table: bfloat16 [16, 128], replicated, may hold values from -3 to 3
- w_self: bfloat16 [2, 128, 128], replicated, may hold values from -0.5 to 0.5
- w_agg: bfloat16 [2, 128, 128], replicated, may hold values from -0.5 to 0.5
- w_out: bfloat16 [2, 128, 128], replicated, may hold values from -0.5 to 0.5
Outputs:
- loss: float32 [2], P('event'), parts along dimension 0
- grad_enc: float32 [24, 128], P('event'), parts along dimension 0
- grad_table: float32 [32, 128], P('event'), parts along dimension 0
- grad_self: float32 [4, 128, 128], P('event'), parts along dimension 0
- grad_agg: float32 [4, 128, 128], P('event'), parts along dimension 0
- grad_out: float32 [4, 128, 128], P('event'), parts along dimension 0
There are 2 independent parts, one for each index of `event`. A program takes and returns all parts, laid end to end along the dimension named above; an argument that names none is the same for every part. Nothing has to cross between parts.
Inputs may be any that keep to these rules, and one draw needn't show every extreme that they name: `live_slots`: in every draw some node block has all 8 slots live.
All inputs are finite; a program needn't handle non-finite values.
Results may differ from a plain program's by a relative error of at most 0.0022.
Values may be sent and summed in bfloat16 or wider, within the bound.
No kernel may reach another device: no remote copies, remote signals or barrier semaphores. Data moves between devices by JAX's collectives and lax.ppermute only.
A program may use at most 128 MiB of HBM per device.

v0:
```python
import math

import jax
import jax.numpy as jnp
from jax import lax
from jax.sharding import PartitionSpec as P

loss_divisor = 64.0


def shifted(value, axis, steps):
    count = lax.axis_size(axis)
    pairs = [(source, (source + steps) % count) for source in range(count)]
    return lax.ppermute(value, axis, pairs)


def contract_rows(left_side, right_side):
    return lax.dot_general(
        left_side, right_side, (((0,), (0,)), ((), ())), preferred_element_type=jnp.float32
    )


def contract_cols(left_side, right_side):
    return lax.dot_general(
        left_side, right_side, (((1,), (1,)), ((), ())), preferred_element_type=jnp.float32
    )


def contract_inner(left_side, right_side):
    return lax.dot_general(
        left_side, right_side, (((1,), (0,)), ((), ())), preferred_element_type=jnp.float32
    )


def contrast_terms(window, anchor_here, positive_here, negative_here, centre, latent_width):
    anchor = window[centre + anchor_here].astype(jnp.float32)
    positive = window[positive_here].astype(jnp.float32)
    negative = window[negative_here].astype(jnp.float32)
    inv_root = 1.0 / math.sqrt(latent_width)
    score_gap = (jnp.sum(anchor * negative, axis=1) - jnp.sum(anchor * positive, axis=1)) * inv_root
    return (score_gap, anchor, positive, negative)


def contrast_grad(
    score_gap,
    anchor,
    positive,
    negative,
    anchor_here,
    positive_here,
    negative_here,
    centre,
    window_shape,
    latent_width,
):
    weight_coef = (jax.nn.sigmoid(score_gap) * (1.0 / (loss_divisor * math.sqrt(latent_width))))[
        :, None
    ]
    gradient = jnp.zeros(window_shape, jnp.float32)
    gradient = gradient.at[centre + anchor_here].add(weight_coef * (negative - positive))
    gradient = gradient.at[positive_here].add(-weight_coef * anchor)
    gradient = gradient.at[negative_here].add(weight_coef * anchor)
    return gradient


def neighbour_window(latents):
    ahead_near = shifted(latents, "phi", -1)
    ahead_far = shifted(latents, "phi", -2)
    behind_near = shifted(latents, "phi", 1)
    behind_far = shifted(latents, "phi", 2)
    return jnp.concatenate([behind_far, behind_near, latents, ahead_near, ahead_far], axis=0)


def return_window(window_grad, hit_count):
    pieces = window_grad.reshape(5, hit_count, window_grad.shape[1])
    lower_far = pieces[0].astype(jnp.bfloat16)
    lower_near = pieces[1].astype(jnp.bfloat16)
    upper_near = pieces[3].astype(jnp.bfloat16)
    upper_far = pieces[4].astype(jnp.bfloat16)
    below_far = shifted(upper_far, "phi", 2)
    below_near = shifted(upper_near, "phi", 1)
    above_near = shifted(lower_near, "phi", -1)
    above_far = shifted(lower_far, "phi", -2)
    received = below_far.astype(jnp.float32) + below_near.astype(jnp.float32)
    received = received + above_near.astype(jnp.float32) + above_far.astype(jnp.float32)
    return pieces[2] + received


def block_product(edge_tiles, src_blocks, live_mask, window):
    block_rows = edge_tiles.shape[2]
    latent_width = window.shape[1]
    blocks = window.reshape(-1, block_rows, latent_width)
    chosen = jnp.where(live_mask[:, :, None, None], blocks[src_blocks], jnp.zeros((), blocks.dtype))
    return jnp.einsum("bsij,bsjw->biw", edge_tiles, chosen, preferred_element_type=jnp.float32)


def block_transpose(edge_tiles, src_blocks, live_mask, agg_grad):
    block_count, slot_count, block_rows = (
        edge_tiles.shape[0],
        edge_tiles.shape[1],
        edge_tiles.shape[2],
    )
    latent_width = agg_grad.shape[2]
    contrib = jnp.einsum("bsij,biw->bsjw", edge_tiles, agg_grad, preferred_element_type=jnp.float32)
    contrib = jnp.where(live_mask[:, :, None, None], contrib, 0.0)
    return jax.ops.segment_sum(
        contrib.reshape(block_count * slot_count, block_rows, latent_width),
        src_blocks.reshape(block_count * slot_count),
        num_segments=5 * block_count,
    )


def body(
    hit_feats,
    layer_ids,
    edge_tiles,
    src_blocks,
    live_slots,
    anchor_hits,
    positive_hits,
    negative_hits,
    w_enc,
    layer_table,
    w_self,
    w_agg,
    w_out,
):
    block_count, slot_count, block_rows = (
        edge_tiles.shape[0],
        edge_tiles.shape[1],
        edge_tiles.shape[2],
    )
    latent_width = w_enc.shape[1]
    hit_count = block_count * block_rows
    layer_total = w_self.shape[0]
    live_mask = jnp.arange(slot_count, dtype=jnp.int32)[None, :] < live_slots[:, None]
    onehot = (
        jnp.arange(layer_table.shape[0], dtype=jnp.int32)[:, None] == layer_ids[None, :]
    ).astype(jnp.bfloat16)
    encoded = contract_rows(hit_feats, w_enc) + contract_rows(onehot, layer_table)
    squashed = jnp.tanh(encoded)
    latents = squashed.astype(jnp.bfloat16)
    stored = []
    for layer_index in range(layer_total):
        window = neighbour_window(latents)
        aggregated = (
            block_product(edge_tiles, src_blocks, live_mask, window)
            .reshape(hit_count, latent_width)
            .astype(jnp.bfloat16)
        )
        activation = jnp.dot(
            latents, w_self[layer_index], preferred_element_type=jnp.float32
        ) + jnp.dot(aggregated, w_agg[layer_index], preferred_element_type=jnp.float32)
        hidden = jax.nn.relu(activation).astype(jnp.bfloat16)
        updated = (
            latents.astype(jnp.float32)
            + jnp.dot(hidden, w_out[layer_index], preferred_element_type=jnp.float32)
        ).astype(jnp.bfloat16)
        stored.append((latents, aggregated, activation, hidden))
        latents = updated
    window = neighbour_window(latents)
    centre = 2 * hit_count
    score_gap, anchor, positive, negative = contrast_terms(
        window, anchor_hits, positive_hits, negative_hits, centre, latent_width
    )
    loss_part = jnp.sum(jax.nn.softplus(score_gap))
    window_grad = contrast_grad(
        score_gap,
        anchor,
        positive,
        negative,
        anchor_hits,
        positive_hits,
        negative_hits,
        centre,
        window.shape,
        latent_width,
    )
    gradient = return_window(window_grad, hit_count)
    self_grads = [None] * layer_total
    agg_grads = [None] * layer_total
    out_grads = [None] * layer_total
    for layer_index in range(layer_total - 1, -1, -1):
        before, aggregated, activation, hidden = stored[layer_index]
        upstream = gradient.astype(jnp.bfloat16)
        out_grads[layer_index] = contract_rows(hidden, upstream)
        hidden_grad = contract_cols(upstream, w_out[layer_index])
        act_grad = jnp.where(activation > 0, hidden_grad, 0.0).astype(jnp.bfloat16)
        self_grads[layer_index] = contract_rows(before, act_grad)
        agg_grads[layer_index] = contract_rows(aggregated, act_grad)
        agg_grad = contract_cols(act_grad, w_agg[layer_index]).astype(jnp.bfloat16)
        direct = gradient + contract_cols(act_grad, w_self[layer_index])
        spread = block_transpose(
            edge_tiles,
            src_blocks,
            live_mask,
            agg_grad.reshape(block_count, block_rows, latent_width),
        )
        gradient = direct + return_window(spread.reshape(5 * hit_count, latent_width), hit_count)
    encoded_grad = (gradient * (1.0 - squashed * squashed)).astype(jnp.bfloat16)
    grad_enc = contract_inner(hit_feats, encoded_grad)
    grad_table = contract_inner(onehot, encoded_grad)
    summed = lax.psum(
        (
            grad_enc,
            grad_table,
            jnp.stack(self_grads),
            jnp.stack(agg_grads),
            jnp.stack(out_grads),
            loss_part,
        ),
        "phi",
    )
    triplet_total = anchor_hits.shape[0] * lax.axis_size("phi")
    loss = (summed[5] / triplet_total).reshape(1)
    return (loss, summed[0], summed[1], summed[2], summed[3], summed[4])


def solution(mesh):
    in_specs = (
        P(None, ("event", "phi")),
        P(("event", "phi")),
        P(("event", "phi"), None, None, None),
        P(("event", "phi"), None),
        P(("event", "phi")),
        P(("event", "phi")),
        P(("event", "phi")),
        P(("event", "phi")),
        P(),
        P(),
        P(),
        P(),
        P(),
    )
    out_specs = (
        P("event"),
        P("event", None),
        P("event", None),
        P("event", None, None),
        P("event", None, None),
        P("event", None, None),
    )
    return jax.shard_map(body, mesh=mesh, in_specs=in_specs, out_specs=out_specs, check_vma=False)
```

profile of v0, /device:TPU:0, one launch (start us, length us, event | category | flops | bytes accessed | tf_op | source)
XLA Modules:
  0.0 818.2 jit_solution(6428048118215018878)
XLA Ops:
  21.9 50.4 %collective-permute-done = bf16[4096,128]{1,0:T(8,128)(2,1)} collective-permute-done((bf16[4096,128]{1,0:T(8,128)(2,1)S(1)}, bf16[4096,128]{1,0:T(8,128)(2,1)}, u32[]{:S(2)}, u32[]{:S(2)}) %collective-permute-start) | collective-permute-done | bytes 1048608 | tf_op jit(solution)/shard_map/ppermute | solution.py:14
  87.2 11.2 %gather_fusion = bf16[256,128,128]{2,1,0:T(8,128)(2,1)} fusion(bf16[160,128,128]{2,1,0:T(8,128)(2,1)} %bitcast.1, s32[1024]{0:T(1024)S(1)} %pad_clamp_fusion), kind=kCustom, calls=%fused_computation | custom fusion | bytes 16778240 | tf_op jit(solution)/shard_map/gather | solution.py:93
  98.4 8.3 %bitcast_convert_fusion.1 = bf16[32,128,128]{1,2,0:T(8,128)(2,1)S(1)} fusion(bf16[32,8,128,128]{3,2,1,0:T(8,128)(2,1)} %param.15, bf16[32,8,128,128]{3,2,1,0:T(8,128)(2,1)} %bitcast.122, pred[32,8]{1,0:T(8,128)(4,1)S(1)} %iota_compare_fusion.3), kind=kOutput, calls=%fused_computation.46 | convolution fusion | flops 1078460416 | bytes 17826048 | tf_op jit(solution)/shard_map/bsij,bsjw->biw/dot_general | solution.py:94
  118.1 50.6 %collective-permute-done.4 = bf16[4096,128]{1,0:T(8,128)(2,1)S(1)} collective-permute-done((bf16[4096,128]{1,0:T(8,128)(2,1)S(1)}, bf16[4096,128]{1,0:T(8,128)(2,1)S(1)}, u32[]{:S(2)}, u32[]{:S(2)}) %collective-permute-start.4) | collective-permute-done | bytes 1048608 | tf_op jit(solution)/shard_map/ppermute | solution.py:14
  172.9 8.7 %collective-permute-done.7 = bf16[4096,128]{1,0:T(8,128)(2,1)S(1)} collective-permute-done((bf16[4096,128]{1,0:T(8,128)(2,1)S(1)}, bf16[4096,128]{1,0:T(8,128)(2,1)S(1)}, u32[]{:S(2)}, u32[]{:S(2)}) %collective-permute-start.7) | collective-permute-done | bytes 1048608 | tf_op jit(solution)/shard_map/ppermute | solution.py:14
  182.6 11.2 %gather_fusion.1 = bf16[256,128,128]{2,1,0:T(8,128)(2,1)} fusion(bf16[160,128,128]{2,1,0:T(8,128)(2,1)} %bitcast.10, s32[1024]{0:T(1024)S(1)} %pad_clamp_fusion), kind=kCustom, calls=%fused_computation.1 | custom fusion | bytes 16778240 | tf_op jit(solution)/shard_map/gather | solution.py:93
  193.8 8.3 %bitcast_convert_fusion = bf16[32,128,128]{1,2,0:T(8,128)(2,1)S(1)} fusion(bf16[32,8,128,128]{3,2,1,0:T(8,128)(2,1)} %param.15, bf16[32,8,128,128]{3,2,1,0:T(8,128)(2,1)} %bitcast.121, pred[32,8]{1,0:T(8,128)(4,1)S(1)} %iota_compare_fusion.3), kind=kOutput, calls=%fused_computation.45 | convolution fusion | flops 1078460416 | bytes 17826048 | tf_op jit(solution)/shard_map/bsij,bsjw->biw/dot_general | solution.py:94
  211.0 51.3 %collective-permute-done.8 = bf16[4096,128]{1,0:T(8,128)(2,1)S(1)} collective-permute-done((bf16[4096,128]{1,0:T(8,128)(2,1)S(1)}, bf16[4096,128]{1,0:T(8,128)(2,1)S(1)}, u32[]{:S(2)}, u32[]{:S(2)}) %collective-permute-start.8) | collective-permute-done | bytes 1048608 | tf_op jit(solution)/shard_map/ppermute | solution.py:14
  266.6 8.8 %collective-permute-done.11 = bf16[4096,128]{1,0:T(8,128)(2,1)S(1)} collective-permute-done((bf16[4096,128]{1,0:T(8,128)(2,1)S(1)}, bf16[4096,128]{1,0:T(8,128)(2,1)S(1)}, u32[]{:S(2)}, u32[]{:S(2)}) %collective-permute-start.11) | collective-permute-done | bytes 1048608 | tf_op jit(solution)/shard_map/ppermute | solution.py:14
  295.5 11.2 %scatter_custom_fusion = f32[20480,128]{1,0:T(8,128)} fusion(s32[1024]{0:T(1024)S(1)} %get-tuple-element.33, f32[]{:T(128)} %constant.14.clone.1, bf16[1024,128]{1,0:T(8,128)(2,1)S(1)} %gather_fusion.4, bf16[1024,128]{1,0:T(8,128)(2,1)S(1)} %gather_fusion.3, f32[1024]{0:T(1024)S(1)} %get-tuple-element.15), kind=kCustom, calls=%fused_computation.18 | custom fusion | flops 655360 | bytes 11014148 | tf_op jit(solution)/shard_map/scatter-add | solution.py:60
  306.7 13.9 %scatter_custom_fusion.1 = f32[20480,128]{1,0:T(8,128)} fusion(f32[20480,128]{1,0:T(8,128)} %scatter_custom_fusion, s32[1024]{0:T(1024)S(1)} %get-tuple-element.31, bf16[1024,128]{1,0:T(8,128)(2,1)S(1)} %gather_fusion.2, f32[1024]{0:T(1024)S(1)} %get-tuple-element.14), kind=kCustom, calls=%fused_computation.64 | custom fusion | flops 393216 | bytes 10752000 | tf_op jit(solution)/shard_map/scatter-add | solution.py:61
  320.7 13.9 %scatter_custom_fusion.2 = f32[20480,128]{1,0:T(8,128)} fusion(f32[20480,128]{1,0:T(8,128)} %scatter_custom_fusion.1, s32[1024]{0:T(1024)S(1)} %get-tuple-element.38, bf16[1024,128]{1,0:T(8,128)(2,1)S(1)} %gather_fusion.2, f32[1024]{0:T(1024)S(1)} %get-tuple-element.15), kind=kCustom, calls=%fused_computation.65 | custom fusion | flops 393216 | bytes 10752000 | tf_op jit(solution)/shard_map/scatter-add | solution.py:62
  348.4 51.2 %collective-permute-done.12 = bf16[4096,128]{1,0:T(8,128)(2,1)S(1)} collective-permute-done((bf16[4096,128]{1,0:T(8,128)(2,1)}, bf16[4096,128]{1,0:T(8,128)(2,1)S(1)}, u32[]{:S(2)}, u32[]{:S(2)}) %collective-permute-start.12) | collective-permute-done | bytes 1048608 | tf_op jit(solution)/shard_map/ppermute | solution.py:14
  399.6 13.0 %collective-permute-done.15 = bf16[4096,128]{1,0:T(8,128)(2,1)} collective-permute-done((bf16[4096,128]{1,0:T(8,128)(2,1)}, bf16[4096,128]{1,0:T(8,128)(2,1)}, u32[]{:S(2)}, u32[]{:S(2)}) %collective-permute-start.15) | collective-permute-done | bytes 1048608 | tf_op jit(solution)/shard_map/ppermute | solution.py:14
  417.4 11.7 %convolution_select_fusion.1 = f32[32,128,8,128]{3,1,2,0:T(8,128)} fusion(bf16[32,128,128,1]{2,1,3,0:T(8,128)(2,1)S(1)} %bitcast.124, bf16[32,8,128,128]{3,2,1,0:T(8,128)(2,1)} %param.15, pred[32,8]{1,0:T(8,128)(4,1)S(1)} %iota_compare_fusion.3), kind=kOutput, calls=%fused_computation.11 | convolution fusion | flops 1077936128 | bytes 26214656 | tf_op jit(solution)/shard_map/bsij,biw->bsjw/dot_general | solution.py:104
  429.2 17.4 %copy.26 = f32[256,128,128]{2,1,0:T(8,128)} copy(f32[256,128,128]{1,2,0:T(8,128)} %bitcast.118) | data formatting | bytes 33554432 | tf_op jit(solution)/shard_map/reshape | solution.py:107
  451.9 52.5 %scatter_fusion = f32[160,128,128]{2,1,0:T(8,128)} fusion(f32[160,128,128]{2,1,0:T(8,128)} %broadcast.77.clone, s32[256]{0:T(256)S(1)} %reshape.190, f32[256,128,128]{2,1,0:T(8,128)} %copy.26), kind=kCustom, calls=%fused_computation.8 | custom fusion | flops 4194304 | bytes 50332672 | tf_op jit(solution)/shard_map/scatter-add | solution.py:106
  520.2 47.3 %collective-permute-done.16 = bf16[4096,128]{1,0:T(8,128)(2,1)S(1)} collective-permute-done((bf16[4096,128]{1,0:T(8,128)(2,1)S(1)}, bf16[4096,128]{1,0:T(8,128)(2,1)S(1)}, u32[]{:S(2)}, u32[]{:S(2)}) %collective-permute-start.16) | collective-permute-done | bytes 1048608 | tf_op jit(solution)/shard_map/ppermute | solution.py:14
  567.4 10.6 %collective-permute-done.19 = bf16[4096,128]{1,0:T(8,128)(2,1)S(1)} collective-permute-done((bf16[4096,128]{1,0:T(8,128)(2,1)S(1)}, bf16[4096,128]{1,0:T(8,128)(2,1)S(1)}, u32[]{:S(2)}, u32[]{:S(2)}) %collective-permute-start.19) | collective-permute-done | bytes 1048608 | tf_op jit(solution)/shard_map/ppermute | solution.py:14
  590.0 17.4 %copy.28 = f32[256,128,128]{2,1,0:T(8,128)} copy(f32[256,128,128]{1,2,0:T(8,128)} %bitcast.117) | data formatting | bytes 33554432 | tf_op jit(solution)/shard_map/reshape | solution.py:107
  612.7 52.5 %scatter_fusion.1 = f32[160,128,128]{2,1,0:T(8,128)} fusion(f32[160,128,128]{2,1,0:T(8,128)} %broadcast.77, s32[256]{0:T(256)S(1)} %reshape.190, f32[256,128,128]{2,1,0:T(8,128)} %copy.28), kind=kCustom, calls=%fused_computation.9 | custom fusion | flops 4194304 | bytes 50332672 | tf_op jit(solution)/shard_map/scatter-add | solution.py:106
  686.4 45.0 %collective-permute-done.20 = bf16[4096,128]{1,0:T(8,128)(2,1)} collective-permute-done((bf16[4096,128]{1,0:T(8,128)(2,1)}, bf16[4096,128]{1,0:T(8,128)(2,1)}, u32[]{:S(2)}, u32[]{:S(2)}) %collective-permute-start.20) | collective-permute-done | bytes 1048608 | tf_op jit(solution)/shard_map/ppermute | solution.py:14
  731.3 11.0 %collective-permute-done.23 = bf16[4096,128]{1,0:T(8,128)(2,1)} collective-permute-done((bf16[4096,128]{1,0:T(8,128)(2,1)}, bf16[4096,128]{1,0:T(8,128)(2,1)}, u32[]{:S(2)}, u32[]{:S(2)}) %collective-permute-start.23) | collective-permute-done | bytes 1048608 | tf_op jit(solution)/shard_map/ppermute | solution.py:14
  746.8 57.8 %all-reduce = (f32[]{:T(128)}, f32[12,128]{1,0:T(8,128)}, f32[16,128]{1,0:T(8,128)}) all-reduce(f32[]{:T(128)} %get-tuple-element.28, f32[12,128]{1,0:T(8,128)S(1)} %convolution_bitcast_fusion.6, f32[16,128]{1,0:T(8,128)S(1)} %fusion.36), channel_id=1, replica_groups=mesh['event'=2,'phi'=16] {'phi'}, use_global_device_ids=true, to_apply=%region_3.4 | all-reduce | flops 3585 | bytes 28680 | tf_op jit(solution)/shard_map/psum | solution.py:203
  (184 shorter events, 166.4 us)
Async XLA Ops:
  7.2 798.1 %all-reduce.4.cloned.1.call-start = ((), (), s32[]{:S(2)}) async-start(), calls=%async_computation | async-start | bytes 786432 | tf_op jit(solution)/shard_map/psum | solution.py:203
  12.1 60.2 %collective-permute-start = (bf16[4096,128]{1,0:T(8,128)(2,1)S(1)}, bf16[4096,128]{1,0:T(8,128)(2,1)}, u32[]{:S(2)}, u32[]{:S(2)}) collective-permute-start(bf16[4096,128]{1,0:T(8,128)(2,1)S(1)} %get-tuple-element.35), channel_id=1, source_target_pairs={{0,2},{1,3},{2,4},{3,5},{4,6},{5,7},{6,8},{7,9},{8,10},{9,11},{10,... | collective-permute-start | bytes 3145736 | tf_op jit(solution)/shard_map/ppermute | solution.py:14
  15.0 59.5 %collective-permute-start.1 = (bf16[4096,128]{1,0:T(8,128)(2,1)S(1)}, bf16[4096,128]{1,0:T(8,128)(2,1)}, u32[]{:S(2)}, u32[]{:S(2)}) collective-permute-start(bf16[4096,128]{1,0:T(8,128)(2,1)S(1)} %get-tuple-element.35), channel_id=1, source_target_pairs={{0,1},{1,2},{2,3},{3,4},{4,5},{5,6},{6,7},{7,8},{8,9},{9,10},{10,1... | collective-permute-start | bytes 3145736 | tf_op jit(solution)/shard_map/ppermute | solution.py:14
  15.0 62.8 %collective-permute-start.2 = (bf16[4096,128]{1,0:T(8,128)(2,1)S(1)}, bf16[4096,128]{1,0:T(8,128)(2,1)S(1)}, u32[]{:S(2)}, u32[]{:S(2)}) collective-permute-start(bf16[4096,128]{1,0:T(8,128)(2,1)S(1)} %get-tuple-element.35), channel_id=1, source_target_pairs={{0,15},{1,0},{2,1},{3,2},{4,3},{5,4},{6,5},{7,6},{8,7},{9,8},{10,9... | collective-permute-start | bytes 3145736 | tf_op jit(solution)/shard_map/ppermute | solution.py:14
  19.5 66.7 %collective-permute-start.3 = (bf16[4096,128]{1,0:T(8,128)(2,1)S(1)}, bf16[4096,128]{1,0:T(8,128)(2,1)S(1)}, u32[]{:S(2)}, u32[]{:S(2)}) collective-permute-start(bf16[4096,128]{1,0:T(8,128)(2,1)S(1)} %get-tuple-element.35), channel_id=1, source_target_pairs={{0,14},{1,15},{2,0},{3,1},{4,2},{5,3},{6,4},{7,5},{8,6},{9,7},{10,... | collective-permute-start | bytes 3145736 | tf_op jit(solution)/shard_map/ppermute | solution.py:14
  108.1 60.6 %collective-permute-start.4 = (bf16[4096,128]{1,0:T(8,128)(2,1)S(1)}, bf16[4096,128]{1,0:T(8,128)(2,1)S(1)}, u32[]{:S(2)}, u32[]{:S(2)}) collective-permute-start(bf16[4096,128]{1,0:T(8,128)(2,1)S(1)} %fusion.12), channel_id=1, source_target_pairs={{0,2},{1,3},{2,4},{3,5},{4,6},{5,7},{6,8},{7,9},{8,10},{9,11},{10,... | collective-permute-start | bytes 3145736 | tf_op jit(solution)/shard_map/ppermute | solution.py:14
  111.4 58.4 %collective-permute-start.5 = (bf16[4096,128]{1,0:T(8,128)(2,1)S(1)}, bf16[4096,128]{1,0:T(8,128)(2,1)S(1)}, u32[]{:S(2)}, u32[]{:S(2)}) collective-permute-start(bf16[4096,128]{1,0:T(8,128)(2,1)S(1)} %fusion.12), channel_id=1, source_target_pairs={{0,1},{1,2},{2,3},{3,4},{4,5},{5,6},{6,7},{7,8},{8,9},{9,10},{10,1... | collective-permute-start | bytes 3145736 | tf_op jit(solution)/shard_map/ppermute | solution.py:14
  111.4 60.4 %collective-permute-start.6 = (bf16[4096,128]{1,0:T(8,128)(2,1)S(1)}, bf16[4096,128]{1,0:T(8,128)(2,1)S(1)}, u32[]{:S(2)}, u32[]{:S(2)}) collective-permute-start(bf16[4096,128]{1,0:T(8,128)(2,1)S(1)} %fusion.12), channel_id=1, source_target_pairs={{0,15},{1,0},{2,1},{3,2},{4,3},{5,4},{6,5},{7,6},{8,7},{9,8},{10,9... | collective-permute-start | bytes 3145736 | tf_op jit(solution)/shard_map/ppermute | solution.py:14
  115.8 65.8 %collective-permute-start.7 = (bf16[4096,128]{1,0:T(8,128)(2,1)S(1)}, bf16[4096,128]{1,0:T(8,128)(2,1)S(1)}, u32[]{:S(2)}, u32[]{:S(2)}) collective-permute-start(bf16[4096,128]{1,0:T(8,128)(2,1)S(1)} %fusion.12), channel_id=1, source_target_pairs={{0,14},{1,15},{2,0},{3,1},{4,2},{5,3},{6,4},{7,5},{8,6},{9,7},{10,... | collective-permute-start | bytes 3145736 | tf_op jit(solution)/shard_map/ppermute | solution.py:14
  204.2 58.1 %collective-permute-start.8 = (bf16[4096,128]{1,0:T(8,128)(2,1)S(1)}, bf16[4096,128]{1,0:T(8,128)(2,1)S(1)}, u32[]{:S(2)}, u32[]{:S(2)}) collective-permute-start(bf16[4096,128]{1,0:T(8,128)(2,1)S(1)} %fusion.13), channel_id=1, source_target_pairs={{0,2},{1,3},{2,4},{3,5},{4,6},{5,7},{6,8},{7,9},{8,10},{9,11},{10,... | collective-permute-start | bytes 3145736 | tf_op jit(solution)/shard_map/ppermute | solution.py:14
  205.0 58.4 %collective-permute-start.9 = (bf16[4096,128]{1,0:T(8,128)(2,1)S(1)}, bf16[4096,128]{1,0:T(8,128)(2,1)S(1)}, u32[]{:S(2)}, u32[]{:S(2)}) collective-permute-start(bf16[4096,128]{1,0:T(8,128)(2,1)S(1)} %fusion.13), channel_id=1, source_target_pairs={{0,1},{1,2},{2,3},{3,4},{4,5},{5,6},{6,7},{7,8},{8,9},{9,10},{10,1... | collective-permute-start | bytes 3145736 | tf_op jit(solution)/shard_map/ppermute | solution.py:14
  205.1 60.4 %collective-permute-start.10 = (bf16[4096,128]{1,0:T(8,128)(2,1)S(1)}, bf16[4096,128]{1,0:T(8,128)(2,1)S(1)}, u32[]{:S(2)}, u32[]{:S(2)}) collective-permute-start(bf16[4096,128]{1,0:T(8,128)(2,1)S(1)} %fusion.13), channel_id=1, source_target_pairs={{0,15},{1,0},{2,1},{3,2},{4,3},{5,4},{6,5},{7,6},{8,7},{9,8},{10,9... | collective-permute-start | bytes 3145736 | tf_op jit(solution)/shard_map/ppermute | solution.py:14
  209.6 65.8 %collective-permute-start.11 = (bf16[4096,128]{1,0:T(8,128)(2,1)S(1)}, bf16[4096,128]{1,0:T(8,128)(2,1)S(1)}, u32[]{:S(2)}, u32[]{:S(2)}) collective-permute-start(bf16[4096,128]{1,0:T(8,128)(2,1)S(1)} %fusion.13), channel_id=1, source_target_pairs={{0,14},{1,15},{2,0},{3,1},{4,2},{5,3},{6,4},{7,5},{8,6},{9,7},{10,... | collective-permute-start | bytes 3145736 | tf_op jit(solution)/shard_map/ppermute | solution.py:14
  341.2 58.4 %collective-permute-start.12 = (bf16[4096,128]{1,0:T(8,128)(2,1)}, bf16[4096,128]{1,0:T(8,128)(2,1)S(1)}, u32[]{:S(2)}, u32[]{:S(2)}) collective-permute-start(bf16[4096,128]{1,0:T(8,128)(2,1)} %get-tuple-element.24), channel_id=1, source_target_pairs={{0,2},{1,3},{2,4},{3,5},{4,6},{5,7},{6,8},{7,9},{8,10},{9,11},{10,... | collective-permute-start | bytes 3145736 | tf_op jit(solution)/shard_map/ppermute | solution.py:14
  342.0 57.6 %collective-permute-start.13 = (bf16[4096,128]{1,0:T(8,128)(2,1)}, bf16[4096,128]{1,0:T(8,128)(2,1)}, u32[]{:S(2)}, u32[]{:S(2)}) collective-permute-start(bf16[4096,128]{1,0:T(8,128)(2,1)} %get-tuple-element.27), channel_id=1, source_target_pairs={{0,1},{1,2},{2,3},{3,4},{4,5},{5,6},{6,7},{7,8},{8,9},{9,10},{10,1... | collective-permute-start | bytes 3145736 | tf_op jit(solution)/shard_map/ppermute | solution.py:14
  346.9 65.7 %collective-permute-start.15 = (bf16[4096,128]{1,0:T(8,128)(2,1)}, bf16[4096,128]{1,0:T(8,128)(2,1)}, u32[]{:S(2)}, u32[]{:S(2)}) collective-permute-start(bf16[4096,128]{1,0:T(8,128)(2,1)} %get-tuple-element.25), channel_id=1, source_target_pairs={{0,14},{1,15},{2,0},{3,1},{4,2},{5,3},{6,4},{7,5},{8,6},{9,7},{10,... | collective-permute-start | bytes 3145736 | tf_op jit(solution)/shard_map/ppermute | solution.py:14
  510.1 57.4 %collective-permute-start.16 = (bf16[4096,128]{1,0:T(8,128)(2,1)S(1)}, bf16[4096,128]{1,0:T(8,128)(2,1)S(1)}, u32[]{:S(2)}, u32[]{:S(2)}) collective-permute-start(bf16[4096,128]{1,0:T(8,128)(2,1)S(1)} %bitcast.132), channel_id=1, source_target_pairs={{0,2},{1,3},{2,4},{3,5},{4,6},{5,7},{6,8},{7,9},{8,10},{9,11},{10,... | collective-permute-start | bytes 3145736 | tf_op jit(solution)/shard_map/ppermute | solution.py:14
  510.1 57.3 %collective-permute-start.17 = (bf16[4096,128]{1,0:T(8,128)(2,1)S(1)}, bf16[4096,128]{1,0:T(8,128)(2,1)S(1)}, u32[]{:S(2)}, u32[]{:S(2)}) collective-permute-start(bf16[4096,128]{1,0:T(8,128)(2,1)S(1)} %bitcast.131), channel_id=1, source_target_pairs={{0,1},{1,2},{2,3},{3,4},{4,5},{5,6},{6,7},{7,8},{8,9},{9,10},{10,1... | collective-permute-start | bytes 3145736 | tf_op jit(solution)/shard_map/ppermute | solution.py:14
  510.2 57.3 %collective-permute-start.18 = (bf16[4096,128]{1,0:T(8,128)(2,1)S(1)}, bf16[4096,128]{1,0:T(8,128)(2,1)S(1)}, u32[]{:S(2)}, u32[]{:S(2)}) collective-permute-start(bf16[4096,128]{1,0:T(8,128)(2,1)S(1)} %bitcast.130), channel_id=1, source_target_pairs={{0,15},{1,0},{2,1},{3,2},{4,3},{5,4},{6,5},{7,6},{8,7},{9,8},{10,9... | collective-permute-start | bytes 3145736 | tf_op jit(solution)/shard_map/ppermute | solution.py:14
  514.6 63.5 %collective-permute-start.19 = (bf16[4096,128]{1,0:T(8,128)(2,1)S(1)}, bf16[4096,128]{1,0:T(8,128)(2,1)S(1)}, u32[]{:S(2)}, u32[]{:S(2)}) collective-permute-start(bf16[4096,128]{1,0:T(8,128)(2,1)S(1)} %bitcast.129), channel_id=1, source_target_pairs={{0,14},{1,15},{2,0},{3,1},{4,2},{5,3},{6,4},{7,5},{8,6},{9,7},{10,... | collective-permute-start | bytes 3145736 | tf_op jit(solution)/shard_map/ppermute | solution.py:14
  672.6 58.8 %collective-permute-start.20 = (bf16[4096,128]{1,0:T(8,128)(2,1)}, bf16[4096,128]{1,0:T(8,128)(2,1)}, u32[]{:S(2)}, u32[]{:S(2)}) collective-permute-start(bf16[4096,128]{1,0:T(8,128)(2,1)} %bitcast.33), channel_id=1, source_target_pairs={{0,2},{1,3},{2,4},{3,5},{4,6},{5,7},{6,8},{7,9},{8,10},{9,11},{10,... | collective-permute-start | bytes 3145736 | tf_op jit(solution)/shard_map/ppermute | solution.py:14
  672.6 58.8 %collective-permute-start.21 = (bf16[4096,128]{1,0:T(8,128)(2,1)}, bf16[4096,128]{1,0:T(8,128)(2,1)}, u32[]{:S(2)}, u32[]{:S(2)}) collective-permute-start(bf16[4096,128]{1,0:T(8,128)(2,1)} %bitcast.34), channel_id=1, source_target_pairs={{0,1},{1,2},{2,3},{3,4},{4,5},{5,6},{6,7},{7,8},{8,9},{9,10},{10,1... | collective-permute-start | bytes 3145736 | tf_op jit(solution)/shard_map/ppermute | solution.py:14
  672.6 58.8 %collective-permute-start.22 = (bf16[4096,128]{1,0:T(8,128)(2,1)}, bf16[4096,128]{1,0:T(8,128)(2,1)}, u32[]{:S(2)}, u32[]{:S(2)}) collective-permute-start(bf16[4096,128]{1,0:T(8,128)(2,1)} %bitcast.35), channel_id=1, source_target_pairs={{0,15},{1,0},{2,1},{3,2},{4,3},{5,4},{6,5},{7,6},{8,7},{9,8},{10,9... | collective-permute-start | bytes 3145736 | tf_op jit(solution)/shard_map/ppermute | solution.py:14
  677.0 65.3 %collective-permute-start.23 = (bf16[4096,128]{1,0:T(8,128)(2,1)}, bf16[4096,128]{1,0:T(8,128)(2,1)}, u32[]{:S(2)}, u32[]{:S(2)}) collective-permute-start(bf16[4096,128]{1,0:T(8,128)(2,1)} %bitcast.36), channel_id=1, source_target_pairs={{0,14},{1,15},{2,0},{3,1},{4,2},{5,3},{6,4},{7,5},{8,6},{9,7},{10,... | collective-permute-start | bytes 3145736 | tf_op jit(solution)/shard_map/ppermute | solution.py:14
  (37 other events, 776.7 us)
Sparse Core Ops, SparseCore 0:
  686.5 107.2 all-reduce.3
where the time goes:
time: 827 us; the launch traced here: 818 us
  waiting for transfers between devices  355 us (43%)
  other arithmetic  169 us (20%)
  local copies, waits for them, and re-layouts  125 us (15%)
  blocking collectives  57.8 us (7%)
  matrix products  51.6 us (6%)
  starting transfers between devices  43 us (5%)
  between operations  16.6 us (2%)
    ppermute x24, waiting for transfers between devices, shifted(): return lax.ppermute(value, axis, pairs)  355 us
    scatter-add x2, other arithmetic, block_transpose(): jax.ops.segment_sum(contrib.reshape(block_count * slot_count, block_rows,...  105 us
    psum x1, blocking collectives, body(): lax.psum((grad_enc, grad_table, jnp.stack(self_grads), jnp.stack(agg_grad...  57.8 us
    ppermute x24, starting transfers between devices, shifted(): return lax.ppermute(value, axis, pairs)  43 us
    reshape x2, local copies, waits for them, and re-layouts, block_transpose(): contrib.reshape(block_count * slot_count, block_rows, latent_width)  34.9 us
    unnamed x88, local copies, waits for them, and re-layouts  26 us
    gather x2, local copies, waits for them, and re-layouts, block_product(): blocks[src_blocks]  22.3 us
    dot_general x2, matrix products, block_transpose(): jnp.einsum('bsij,biw->bsjw', edge_tiles, agg_grad, preferred_element_type...  18.9 us
  transfers between devices with their start and end apart: 25, of which 12 were waited for; matrix products, arithmetic and copies ran while one was open for 4% of the time, Pallas kernels for 0%

commit v1 on v0

v1 whole, which is shorter than its diff:
```python
import math

import jax
import jax.numpy as jnp
from jax import lax
from jax.experimental import pallas as pl
from jax.experimental.pallas import tpu as pltpu
from jax.sharding import PartitionSpec as P

loss_divisor = 64.0
F32 = jnp.float32
BF16 = jnp.bfloat16
VMEM_LIMIT = 56 * 1024 * 1024
PACK_ROWS = 16
GROUP = 4

PIECES = 5


def vmem():
    return pl.BlockSpec(memory_space=pltpu.VMEM)


def smem():
    return pl.BlockSpec(memory_space=pltpu.SMEM)


def in_hbm():
    return pl.BlockSpec(memory_space=pl.ANY)


def params():
    return pltpu.CompilerParams(vmem_limit_bytes=VMEM_LIMIT)


def dot_nn(left, right):
    return lax.dot_general(left, right, (((1,), (0,)), ((), ())), preferred_element_type=F32)


def dot_tn(left, right):
    return lax.dot_general(left, right, (((0,), (0,)), ((), ())), preferred_element_type=F32)


def dot_nt(left, right):
    return lax.dot_general(left, right, (((1,), (1,)), ((), ())), preferred_element_type=F32)


def far_pairs(count):
    return [((p + 2) % count if p % 2 == 0 else (p - 2) % count, p) for p in range(count)]


def near_pairs(count):
    return [((p - 2) % count if p % 2 == 0 else (p + 2) % count, p) for p in range(count)]


def core_pairs(count):
    return [(p ^ 1, p) for p in range(count)]


def send(value, pairs):
    return lax.ppermute(value, "phi", pairs)


def turned(pairs):
    return [(target, source) for source, target in pairs]


def gather_window(value):
    count = lax.axis_size("phi")
    far = send(value, far_pairs(count))
    near = send(value, near_pairs(count))
    other = send(value, core_pairs(count))
    passed = send(far, core_pairs(count))
    return (value, far, near, other, passed)


def return_pieces(far, near, other, passed):
    count = lax.axis_size("phi")
    from_core = send(passed, core_pairs(count))
    from_near = send(near, turned(near_pairs(count)))
    from_other = send(other, core_pairs(count))
    joined = (far.astype(F32) + from_core.astype(F32)).astype(BF16)
    from_far = send(joined, turned(far_pairs(count)))
    return (from_far, from_near, from_other)


def total_over_phi(value):
    count = lax.axis_size("phi")
    if count & (count - 1) or count < 4:
        return lax.psum(value, "phi")
    half = value.shape[0] // 2
    odd = lax.axis_index("phi") % 2
    kept = lax.dynamic_slice_in_dim(value, odd * half, half, 0)
    given = lax.dynamic_slice_in_dim(value, (1 - odd) * half, half, 0)
    part = kept + send(given, core_pairs(count))
    step = 2
    while step < count:
        part = part + send(part, [(p, p ^ step) for p in range(count)])
        step *= 2
    back = send(part, core_pairs(count))
    return jnp.where(odd == 0, jnp.concatenate([part, back]), jnp.concatenate([back, part]))


def fetch_tiles(tiles_hbm, tiles, sems, groups):
    for g in range(groups):
        pltpu.make_async_copy(
            tiles_hbm.at[pl.ds(g * GROUP, GROUP)], tiles.at[pl.ds(g * GROUP, GROUP)], sems.at[g]
        ).start()


def await_tiles(tiles_hbm, tiles, sems, g):
    first = pl.multiple_of(g * GROUP, GROUP)
    pltpu.make_async_copy(
        tiles_hbm.at[pl.ds(first, GROUP)], tiles.at[pl.ds(first, GROUP)], sems.at[g]
    ).wait()


def encode_operand(pack_ref, start, width):
    rows = pack_ref[:, pl.ds(start, width)]
    ids = rows.astype(F32)[12:13, :]
    layers = lax.broadcasted_iota(jnp.int32, (PACK_ROWS, width), 0).astype(F32)
    onehot = (layers == ids).astype(BF16)
    return jnp.concatenate([rows, onehot], axis=0)


def forward_group(g, src, tiles, window, w_self, w_agg, w_out, agg_ref, hidden_t_ref, new_ref):
    slots = tiles.shape[1]
    sums = []
    for q in range(GROUP):
        b = g * GROUP + q
        left = jnp.concatenate([tiles[b, s] for s in range(slots)], axis=1)
        right = jnp.concatenate([window[src[b * slots + s]] for s in range(slots)], axis=0)
        sums.append(dot_nn(left, right))
    first = pl.multiple_of(g * GROUP, GROUP)
    agg = jnp.concatenate(sums, axis=0).astype(BF16)
    rows, width = agg.shape
    here = window[pl.ds(first, GROUP)].reshape(rows, width)
    activation = dot_nn(here, w_self[...]) + dot_nn(agg, w_agg[...])
    hidden = jnp.maximum(activation, 0.0)
    hidden_b = hidden.astype(BF16)
    updated = (here.astype(F32) + dot_nn(hidden_b, w_out[...])).astype(BF16)
    agg_ref[pl.ds(first, GROUP)] = agg.reshape(GROUP, rows // GROUP, width)
    new_ref[pl.ds(first, GROUP)] = updated.reshape(GROUP, rows // GROUP, width)
    for q in range(GROUP):
        block = hidden[q * (rows // GROUP) : (q + 1) * (rows // GROUP)]
        hidden_t_ref[first + q] = block.T.astype(BF16)


def first_layer_kernel(
    src, tiles_hbm, p0, p1, p2, p3, p4, w_in, w_self, w_agg, w_out,
    own_ref, agg_ref, hidden_t_ref, new_ref, tiles, window, sems,
):
    blocks, block_rows = tiles.shape[0], tiles.shape[2]
    groups = blocks // GROUP
    fetch_tiles(tiles_hbm, tiles, sems, groups)
    span = GROUP * block_rows
    for k, pack in enumerate((p0, p1, p2, p3, p4)):

        def encode(g, carry, pack=pack, k=k):
            operand = encode_operand(pack, pl.multiple_of(g * span, span), span)
            latents = jnp.tanh(dot_tn(operand, w_in[...])).astype(BF16)
            first = k * blocks + g * GROUP
            window[pl.ds(first, GROUP)] = latents.reshape(GROUP, block_rows, latents.shape[1])
            return carry

        lax.fori_loop(0, groups, encode, 0)
    window[PIECES * blocks] = jnp.zeros(window.shape[1:], BF16)
    own_ref[...] = window[pl.ds(0, blocks)]

    def step(g, carry):
        await_tiles(tiles_hbm, tiles, sems, g)
        forward_group(g, src, tiles, window, w_self, w_agg, w_out, agg_ref, hidden_t_ref, new_ref)
        return carry

    lax.fori_loop(0, groups, step, 0)


def next_layer_kernel(
    src, tiles_hbm, l0, l1, l2, l3, l4, w_self, w_agg, w_out,
    agg_ref, hidden_t_ref, new_ref, tiles, window, sems, piece_sems,
):
    blocks = tiles.shape[0]
    groups = blocks // GROUP
    copies = [
        pltpu.make_async_copy(piece, window.at[pl.ds(k * blocks, blocks)], piece_sems.at[k])
        for k, piece in enumerate((l0, l1, l2, l3, l4))
    ]
    for copy in copies:
        copy.start()
    fetch_tiles(tiles_hbm, tiles, sems, groups)
    window[PIECES * blocks] = jnp.zeros(window.shape[1:], BF16)
    for copy in copies:
        copy.wait()

    def step(g, carry):
        await_tiles(tiles_hbm, tiles, sems, g)
        forward_group(g, src, tiles, window, w_self, w_agg, w_out, agg_ref, hidden_t_ref, new_ref)
        return carry

    lax.fori_loop(0, groups, step, 0)


def list_kernel(row_bits, triplets, part_of, indices, negative_list, positive_list, counts):
    low = (1 << row_bits) - 1
    dummy = (PIECES * triplets) << row_bits

    def scan(k, carry):
        part = part_of[k]
        base = k * 2 * triplets

        def one(t, tops):
            top_n, top_p = tops
            code = (k * triplets + t) << row_bits
            positive = indices[base + t]
            negative = indices[base + triplets + t]
            negative_list[top_n] = code | (negative & low)
            positive_list[top_p] = code | (positive & low)
            top_n = top_n + ((negative >> row_bits) == part).astype(jnp.int32)
            top_p = top_p + ((positive >> row_bits) == part).astype(jnp.int32)
            return top_n, top_p

        return lax.fori_loop(0, triplets, one, carry, unroll=8)

    top_n, top_p = lax.fori_loop(0, PIECES, scan, (jnp.int32(0), jnp.int32(0)))
    longest = ((jnp.maximum(top_n, top_p) + 7) >> 3) << 3

    def pad(values):
        def put(i, carry):
            values[i] = jnp.int32(dummy)
            return carry

        return put

    lax.fori_loop(top_n, longest, pad(negative_list), 0)
    lax.fori_loop(top_p, longest, pad(positive_list), 0)
    counts[0] = longest >> 3


def gather_kernel(
    row_bits, negative_list, positive_list, counts, anchors, latents,
    d0, d1, d2, d3, d4, anchor_ref, wide, negative, positive, anchor_rows,
):
    low = (1 << row_bits) - 1
    triplets = anchor_ref.shape[0]
    blocks, block_rows, width = latents.shape
    wide[...] = latents[...].reshape(blocks * block_rows, width).astype(F32)
    negative[...] = jnp.zeros(negative.shape, F32)
    positive[...] = jnp.zeros(positive.shape, F32)

    def pick(i, carry):
        for u in range(8):
            code_n = negative_list[i * 8 + u]
            code_p = positive_list[i * 8 + u]
            negative[pl.ds(code_n >> row_bits, 1), :] = wide[pl.ds(code_n & low, 1), :]
            positive[pl.ds(code_p >> row_bits, 1), :] = wide[pl.ds(code_p & low, 1), :]
        return carry

    lax.fori_loop(0, counts[0], pick, 0)

    def pick_anchor(i, carry):
        for u in range(8):
            anchor_rows[pl.ds(i * 8 + u, 1), :] = wide[pl.ds(anchors[i * 8 + u], 1), :]
        return carry

    lax.fori_loop(0, triplets // 8, pick_anchor, 0)
    anchor_ref[...] = anchor_rows[...].astype(BF16)
    for k, out in enumerate((d0, d1, d2, d3, d4)):
        here = pl.ds(k * triplets, triplets)
        out[...] = (negative[here, :] - positive[here, :]).astype(BF16)


def score_kernel(own, far, near, other, anchors, loss_ref, weighted_ref, weighted_b_ref, anchor_grad_ref):
    triplets, width = anchors.shape
    inv_root = 1.0 / math.sqrt(width)
    scale = 1.0 / (loss_divisor * math.sqrt(width))
    chunk = 128
    loss = jnp.zeros((chunk, 1), F32)
    for c in range(triplets // chunk):
        here = pl.ds(c * chunk, chunk)
        gap = own[here, :].astype(F32) + far[here, :].astype(F32)
        gap = gap + near[here, :].astype(F32) + other[here, :].astype(F32)
        anchor = anchors[here, :].astype(F32)
        score = jnp.sum(anchor * gap, axis=1, keepdims=True) * inv_root
        loss = loss + jnp.maximum(score, 0.0) + jnp.log1p(jnp.exp(-jnp.abs(score)))
        coef = scale / (1.0 + jnp.exp(-score))
        weighted = coef * anchor
        weighted_ref[here, :] = weighted
        weighted_b_ref[here, :] = weighted.astype(BF16)
        anchor_grad_ref[here, :] = coef * gap
    loss_ref[...] = jnp.broadcast_to(jnp.sum(loss, axis=0, keepdims=True), loss_ref.shape)


def backward_group(g, src, tiles, gradient, hidden_t, latents, agg, w_self, w_agg, w_out,
                   grads, spread):
    slots = tiles.shape[1]
    first = pl.multiple_of(g * GROUP, GROUP)
    rows, width = tiles.shape[2], latents.shape[2]
    upstream = gradient.astype(BF16)
    hidden = jnp.concatenate([hidden_t[first + q] for q in range(GROUP)], axis=1)
    grads[2] += dot_nt(hidden, upstream)
    hidden_grad = dot_nn(w_out[...], upstream)
    act_grad = jnp.where(hidden > 0, hidden_grad, 0.0).astype(BF16)
    grads[0] += dot_nn(act_grad, latents[pl.ds(first, GROUP)].reshape(GROUP * rows, width))
    grads[1] += dot_nn(act_grad, agg[pl.ds(first, GROUP)].reshape(GROUP * rows, width))
    agg_grad = dot_nn(w_agg[...], act_grad).astype(BF16)
    direct = gradient + dot_nn(w_self[...], act_grad)
    for q in range(GROUP):
        b = g * GROUP + q
        spread[b] += direct[:, q * rows : (q + 1) * rows]
        right = jnp.concatenate([tiles[b, s] for s in range(slots)], axis=1)
        parts = dot_nn(agg_grad[:, q * rows : (q + 1) * rows], right)
        for s in range(slots):
            spread[src[b * slots + s]] += parts[:, s * rows : (s + 1) * rows]


def contrast_layer_kernel(
    row_bits, src, negative_list, positive_list, counts, anchors, tiles_hbm,
    weighted, e1, e2, e3, e4, anchor_grad, hidden_t, latents, agg, w_self, w_agg, w_out,
    own_ref, far_ref, near_ref, other_ref, passed_ref, grads_ref,
    tiles, spread, all_weighted, rows_a, rows_b, rows_c, rows_d, sems,
):
    low = (1 << row_bits) - 1
    blocks, block_rows = tiles.shape[0], tiles.shape[2]
    groups = blocks // GROUP
    triplets = weighted.shape[0]
    fetch_tiles(tiles_hbm, tiles, sems, groups)
    held = (rows_a, rows_b, rows_c, rows_d)
    for rows in held:
        rows[...] = jnp.zeros(rows.shape, F32)
    spread[...] = jnp.zeros(spread.shape, F32)
    grads_ref[...] = jnp.zeros(grads_ref.shape, F32)
    all_weighted[pl.ds(0, triplets), :] = weighted[...]
    for k, piece in enumerate((e1, e2, e3, e4)):
        all_weighted[pl.ds((k + 1) * triplets, triplets), :] = piece[...].astype(F32)
    all_weighted[pl.ds(PIECES * triplets, 8), :] = jnp.zeros((8, weighted.shape[1]), F32)

    def put_anchor(i, carry):
        for u in range(8):
            here = pl.ds(anchors[i * 8 + u], 1)
            held[u % 4][here, :] += anchor_grad[pl.ds(i * 8 + u, 1), :]
        return carry

    lax.fori_loop(0, triplets // 8, put_anchor, 0)

    def put(i, carry):
        for u in range(8):
            code_n = negative_list[i * 8 + u]
            code_p = positive_list[i * 8 + u]
            held[u % 2][pl.ds(code_n & low, 1), :] += all_weighted[pl.ds(code_n >> row_bits, 1), :]
            held[2 + u % 2][pl.ds(code_p & low, 1), :] -= all_weighted[pl.ds(code_p >> row_bits, 1), :]
        return carry

    lax.fori_loop(0, counts[0], put, 0)

    def step(g, carry):
        pieces = []
        for q in range(GROUP):
            here = pl.ds(pl.multiple_of((g * GROUP + q) * block_rows, block_rows), block_rows)
            block = (rows_a[here, :] + rows_b[here, :]) + (rows_c[here, :] + rows_d[here, :])
            pieces.append(block.T)
        await_tiles(tiles_hbm, tiles, sems, g)
        backward_group(g, src, tiles, jnp.concatenate(pieces, axis=1), hidden_t, latents, agg,
                       w_self, w_agg, w_out, grads_ref, spread)
        return carry

    lax.fori_loop(0, groups, step, 0)
    own_ref[...] = spread[pl.ds(0, blocks)]
    for k, out in enumerate((far_ref, near_ref, other_ref, passed_ref)):
        out[...] = spread[pl.ds((k + 1) * blocks, blocks)].astype(BF16)


def last_layer_kernel(
    src, tiles_hbm, own, r1, r2, r3, hidden_t, latents, agg, w_self, w_agg, w_out, w_in_t,
    p0, p1, p2, p3, p4,
    grads_ref, grad_in_ref, tiles, spread, sems,
):
    blocks, block_rows = tiles.shape[0], tiles.shape[2]
    groups = blocks // GROUP
    fetch_tiles(tiles_hbm, tiles, sems, groups)
    spread[...] = jnp.zeros(spread.shape, F32)
    grads_ref[...] = jnp.zeros(grads_ref.shape, F32)
    grad_in_ref[...] = jnp.zeros(grad_in_ref.shape, F32)

    def step(g, carry):
        pieces = []
        for q in range(GROUP):
            b = g * GROUP + q
            received = r1[b].astype(F32) + r2[b].astype(F32) + r3[b].astype(F32)
            pieces.append(own[b] + received)
        await_tiles(tiles_hbm, tiles, sems, g)
        backward_group(g, src, tiles, jnp.concatenate(pieces, axis=1), hidden_t, latents, agg,
                       w_self, w_agg, w_out, grads_ref, spread)
        return carry

    lax.fori_loop(0, groups, step, 0)
    span = GROUP * block_rows
    for k, pack in enumerate((p0, p1, p2, p3, p4)):

        def finish(g, carry, pack=pack, k=k):
            operand = encode_operand(pack, pl.multiple_of(g * span, span), span)
            squashed = jnp.tanh(dot_nn(w_in_t[...], operand))
            first = k * blocks + g * GROUP
            gradient = jnp.concatenate([spread[first + q] for q in range(GROUP)], axis=1)
            encoded_grad = (gradient * (1.0 - squashed * squashed)).astype(BF16)
            grad_in_ref[...] += dot_nt(operand, encoded_grad)
            return carry

        lax.fori_loop(0, groups, finish, 0)


def body(
    hit_feats, layer_ids, edge_tiles, src_blocks, live_slots,
    anchor_hits, positive_hits, negative_hits, w_enc, layer_table, w_self, w_agg, w_out,
):
    blocks, slots, block_rows = edge_tiles.shape[0], edge_tiles.shape[1], edge_tiles.shape[2]
    feats, width = w_enc.shape
    kinds = layer_table.shape[0]
    hits = blocks * block_rows
    triplets = anchor_hits.shape[0]
    layers = w_self.shape[0]
    row_bits = hits.bit_length() - 1
    assert hits == 1 << row_bits and feats < PACK_ROWS and kinds == PACK_ROWS and layers == 2
    assert 4 * triplets == hits and blocks % GROUP == 0
    groups = blocks // GROUP
    odd = lax.axis_index("phi") % 2

    positive_high, positive_low = positive_hits // 128, positive_hits % 128
    negative_high, negative_low = negative_hits // 128, negative_hits % 128
    codes = jnp.concatenate([positive_high, negative_high, positive_low, negative_low])
    pack = jnp.concatenate(
        [
            hit_feats,
            layer_ids.astype(BF16)[None, :],
            codes.astype(BF16)[None, :],
            jnp.zeros((PACK_ROWS - feats - 2, hits), BF16),
        ]
    )
    packs = gather_window(pack)
    w_in = jnp.concatenate([w_enc, jnp.zeros((PACK_ROWS - feats, width), BF16), layer_table])

    piece_of_part = jnp.where(odd == 0, jnp.array([2, 4, 0, 3, 1]), jnp.array([1, 3, 0, 4, 2]))
    part_back = jnp.where(odd == 0, jnp.array([2, 0, 4, 1, 3]), jnp.array([2, 4, 0, 3, 1]))
    part = src_blocks // blocks
    piece = jnp.zeros_like(part)
    for j in range(PIECES):
        piece = jnp.where(part == j, piece_of_part[j], piece)
    live = jnp.arange(slots, dtype=jnp.int32)[None, :] < live_slots[:, None]
    src = jnp.where(live, piece * blocks + src_blocks % blocks, PIECES * blocks).reshape(-1)
    src = src.astype(jnp.int32)

    block_shape = (blocks, block_rows, width)
    tile_scratch = pltpu.VMEM(edge_tiles.shape, BF16)
    group_sems = pltpu.SemaphoreType.DMA((groups,))
    window_scratch = pltpu.VMEM((PIECES * blocks + 1, block_rows, width), BF16)
    blocked = jax.ShapeDtypeStruct(block_shape, BF16)

    latents_0, agg_0, hidden_0, latents_1 = pl.pallas_call(
        first_layer_kernel,
        out_shape=(blocked,) * 4,
        in_specs=[smem(), in_hbm()] + [vmem()] * 9,
        out_specs=(vmem(),) * 4,
        scratch_shapes=[tile_scratch, window_scratch, group_sems],
        compiler_params=params(),
        name="first_layer",
    )(src, edge_tiles, *packs, w_in, w_self[0], w_agg[0], w_out[0])

    indices = jnp.stack([each[feats + 1] for each in packs]).astype(jnp.int32)
    indices = indices.reshape(PIECES, 2, 2 * triplets)
    indices = (indices[:, 0] * 128 + indices[:, 1]).reshape(-1)
    capacity = PIECES * triplets + 16
    negative_list, positive_list, counts = pl.pallas_call(
        lambda *refs: list_kernel(row_bits, triplets, *refs),
        out_shape=(
            jax.ShapeDtypeStruct((capacity,), jnp.int32),
            jax.ShapeDtypeStruct((capacity,), jnp.int32),
            jax.ShapeDtypeStruct((8,), jnp.int32),
        ),
        in_specs=[smem(), smem()],
        out_specs=(smem(),) * 3,
        compiler_params=params(),
        name="row_lists",
    )(part_back.astype(jnp.int32), indices)

    window_1 = gather_window(latents_1)
    agg_1, hidden_1, latents_2 = pl.pallas_call(
        next_layer_kernel,
        out_shape=(blocked,) * 3,
        in_specs=[smem(), in_hbm()] + [in_hbm()] * 5 + [vmem()] * 3,
        out_specs=(vmem(),) * 3,
        scratch_shapes=[
            tile_scratch, window_scratch, group_sems, pltpu.SemaphoreType.DMA((PIECES,)),
        ],
        compiler_params=params(),
        name="next_layer",
    )(src, edge_tiles, *window_1, w_self[1], w_agg[1], w_out[1])

    triplet_rows = jax.ShapeDtypeStruct((triplets, width), BF16)
    wide_rows = jax.ShapeDtypeStruct((triplets, width), F32)
    gathered = pl.pallas_call(
        lambda *refs: gather_kernel(row_bits, *refs),
        out_shape=(triplet_rows,) * 6,
        in_specs=[smem()] * 4 + [vmem()],
        out_specs=(vmem(),) * 6,
        scratch_shapes=[
            pltpu.VMEM((hits, width), F32),
            pltpu.VMEM((PIECES * triplets + 8, width), F32),
            pltpu.VMEM((PIECES * triplets + 8, width), F32),
            pltpu.VMEM((triplets, width), F32),
        ],
        compiler_params=params(),
        name="gather_rows",
    )(negative_list, positive_list, counts, anchor_hits, latents_2)
    gap_own, gap_far, gap_near, gap_other, gap_passed, anchor_rows = gathered
    gaps = return_pieces(gap_far, gap_near, gap_other, gap_passed)

    loss_part, weighted, weighted_b, anchor_grad = pl.pallas_call(
        score_kernel,
        out_shape=(jax.ShapeDtypeStruct((8, width), F32), wide_rows, triplet_rows, wide_rows),
        in_specs=[vmem()] * 5,
        out_specs=(vmem(),) * 4,
        compiler_params=params(),
        name="scores",
    )(gap_own, *gaps, anchor_rows)
    weighted_window = gather_window(weighted_b)

    wide_blocked = jax.ShapeDtypeStruct(block_shape, F32)
    spread_scratch = pltpu.VMEM((PIECES * blocks + 1, width, block_rows), F32)
    grads_shape = jax.ShapeDtypeStruct((3, width, width), F32)
    own_1, far_1, near_1, other_1, passed_1, grads_1 = pl.pallas_call(
        lambda *refs: contrast_layer_kernel(row_bits, *refs),
        out_shape=(wide_blocked,) + (blocked,) * 4 + (grads_shape,),
        in_specs=[smem()] * 5 + [in_hbm()] + [vmem()] * 12,
        out_specs=(vmem(),) * 6,
        scratch_shapes=[
            tile_scratch, spread_scratch, pltpu.VMEM((PIECES * triplets + 8, width), F32),
        ]
        + [pltpu.VMEM((hits, width), F32)] * 4
        + [group_sems],
        compiler_params=params(),
        name="contrast_layer",
    )(
        src, negative_list, positive_list, counts, anchor_hits, edge_tiles,
        weighted, *weighted_window[1:], anchor_grad, hidden_1, latents_1, agg_1,
        w_self[1], w_agg[1], w_out[1],
    )
    returned = return_pieces(far_1, near_1, other_1, passed_1)
    summed_1 = total_over_phi(jnp.concatenate([grads_1.reshape(3 * width, width), loss_part]))

    grads_0, grad_in = pl.pallas_call(
        last_layer_kernel,
        out_shape=(grads_shape, jax.ShapeDtypeStruct((2 * PACK_ROWS, width), F32)),
        in_specs=[smem(), in_hbm()] + [vmem()] * 16,
        out_specs=(vmem(),) * 2,
        scratch_shapes=[tile_scratch, spread_scratch, group_sems],
        compiler_params=params(),
        name="last_layer",
    )(
        src, edge_tiles, own_1, *returned, hidden_0, latents_0, agg_0,
        w_self[0], w_agg[0], w_out[0], w_in.T, *packs,
    )
    summed_0 = total_over_phi(jnp.concatenate([grads_0.reshape(3 * width, width), grad_in]))

    grads_1 = summed_1[: 3 * width].reshape(3, width, width)
    grads_0 = summed_0[: 3 * width].reshape(3, width, width)
    grad_in = summed_0[3 * width :]
    loss = (summed_1[3 * width, 0] / (triplets * lax.axis_size("phi"))).reshape(1)
    grad_self = jnp.stack([grads_0[0].T, grads_1[0].T])
    grad_agg = jnp.stack([grads_0[1].T, grads_1[1].T])
    grad_out = jnp.stack([grads_0[2], grads_1[2]])
    return (loss, grad_in[:feats], grad_in[PACK_ROWS:], grad_self, grad_agg, grad_out)


def solution(mesh):
    both = ("event", "phi")
    in_specs = (
        P(None, both), P(both), P(both, None, None, None), P(both, None), P(both),
        P(both), P(both), P(both), P(), P(), P(), P(), P(),
    )
    out_specs = (
        P("event"), P("event", None), P("event", None),
        P("event", None, None), P("event", None, None), P("event", None, None),
    )
    return jax.shard_map(body, mesh=mesh, in_specs=in_specs, out_specs=out_specs, check_vma=False)
```

time: 827 us -> 316 us (0.38)
  waiting for transfers between devices: 355 us -> 114 us
  other arithmetic: 169 us -> 16.8 us
  Pallas kernels: 0 us -> 127 us
  local copies, waits for them, and re-layouts: 125 us -> 17.3 us
  blocking collectives: 57.8 us -> 0 us
  matrix products: 51.6 us -> 0 us
  between operations: 16.6 us -> 2.84 us
    ppermute x24 -> x30, waiting for transfers between devices: 355 us -> 114 us  [send(): return lax.ppermute(value, 'phi', pairs)]
    scatter-add x5 -> x0, other arithmetic: 144 us -> none  [the longest x2 105 us: block_transpose(): jax.ops.segment_sum(contrib.reshape(block_count * slot_count, block_rows,...]
    pallas_call x0 -> x7, Pallas kernels: none -> 127 us  [the longest x1 39 us: body(): pl.pallas_call(lambda *refs: list_kernel(row_bits, triplets, *refs), out_...]
    psum x1 -> x0, blocking collectives: 57.8 us -> none  [body(): lax.psum((grad_enc, grad_table, jnp.stack(self_grads), jnp.stack(agg_grad...]
    dot_general x26 -> x0, matrix products: 51.6 us -> none  [the longest x2 18.9 us: block_transpose(): jnp.einsum('bsij,biw->bsjw', edge_tiles, agg_grad, preferred_element_type...]
    gather x5 -> x0, local copies, waits for them, and re-layouts: 40.5 us -> none  [the longest x2 22.3 us: block_product(): blocks[src_blocks]]
    reshape x2 -> x1, local copies, waits for them, and re-layouts: 34.9 us -> 0.63 us  [body(): jnp.where(live, piece * blocks + src_blocks % blocks, PIECES * blocks)]
    unnamed x88 -> x48, local copies, waits for them, and re-layouts: 26 us -> 6.79 us
  transfers between devices with their start and end apart: 25 -> 30, of which waited for: 12 -> 12; matrix products, arithmetic and copies ran while one was open for 4% -> 7% of each run, Pallas kernels for 0% -> 20%
where the time goes in v1:
time: 316 us; the launch traced here: 315 us
  Pallas kernels  127 us (40%)
  waiting for transfers between devices  114 us (36%)
  starting transfers between devices  37 us (12%)
  local copies, waits for them, and re-layouts  17.3 us (5%)
  other arithmetic  16.8 us (5%)
    ppermute x30, waiting for transfers between devices, send(): return lax.ppermute(value, 'phi', pairs)  114 us
    pallas_call x1, Pallas kernels, body(): pl.pallas_call(lambda *refs: list_kernel(row_bits, triplets, *refs), out_...  39 us
    ppermute x30, starting transfers between devices, send(): return lax.ppermute(value, 'phi', pairs)  37 us
    pallas_call x1, Pallas kernels, body(): pl.pallas_call(last_layer_kernel, out_shape=(grads_shape, jax.ShapeDtypeS...  25.2 us
    pallas_call x1, Pallas kernels, body(): pl.pallas_call(lambda *refs: contrast_layer_kernel(row_bits, *refs), out_...  20.7 us
    pallas_call x1, Pallas kernels, body(): pl.pallas_call(first_layer_kernel, out_shape=(blocked,) * 4, in_specs=[sm...  18.1 us
    pallas_call x1, Pallas kernels, body(): pl.pallas_call(next_layer_kernel, out_shape=(blocked,) * 3, in_specs=[sme...  12.8 us
    pallas_call x1, Pallas kernels, body(): pl.pallas_call(lambda *refs: gather_kernel(row_bits, *refs), out_shape=(t...  8.26 us
  transfers between devices with their start and end apart: 30, of which 12 were waited for; matrix products, arithmetic and copies ran while one was open for 7% of the time, Pallas kernels for 20%

profile of v1, /device:TPU:0, one launch (start us, length us, event | category | flops | bytes accessed | tf_op | source)
XLA Modules:
  0.0 314.7 jit_solution(12366101658558441188)
XLA Ops:
  3.9 6.1 %collective-permute-start = (bf16[16,4096]{1,0:T(8,128)(2,1)S(1)}, bf16[16,4096]{1,0:T(8,128)(2,1)S(1)}, u32[]{:S(2)}, u32[]{:S(2)}) collective-permute-start(bf16[16,4096]{1,0:T(8,128)(2,1)S(1)} %maximum_maximum_fusion.p0), channel_id=1, source_target_pairs={{2,0},{15,1},{4,2},{1,3},{6,4},{3,5},{8,6},{5,7},{10,8},{7,9},{12,... | collective-permute-start | bytes 393224 | tf_op jit(solution)/shard_map/ppermute | solution.py:61
  11.8 3.9 %fusion.7 = s32[32,8]{0,1:T(8,128)S(1)} fusion(s32[32,8]{0,1:T(8,128)} %param.20, s32[]{:T(128)} %bitcast.4, s32[]{:T(128)} %bitcast.3, s32[]{:T(128)} %bitcast.2, s32[]{:T(128)} %bitcast.1, s32[]{:T(128)} %bitcast, s32[32]{0:T(128)} %param.21), kind=kLoop, calls=%fused_computation.63 | loop fusion | flops 8448 | bytes 2196 | tf_op jit(solution)/shard_map/jit(_where)/select_n | solution.py:448
  22.0 18.1 %first_layer.1 = (bf16[32,128,128]{2,1,0:T(8,128)(2,1)}, bf16[32,128,128]{2,1,0:T(8,128)(2,1)}, bf16[32,128,128]{2,1,0:T(8,128)(2,1)}, bf16[32,128,128]{2,1,0:T(8,128)(2,1)}) custom-call(s32[256]{0:T(256)} %reshape.115.src.refs_0_, bf16[32,8,128,128]{3,2,1,0:T(8,128)(2,1)} %tiles_hbm.5, bf16[16,4096]{1,0:T(8,128)(2,1)} %copy-done, ...), custom_call_target="tpu_custom_call" | custom-call | tf_op jit(solution)/shard_map/first_layer/pallas_call | solution.py:457
  40.1 4.8 %collective-permute-start.4 = (bf16[32,128,128]{2,1,0:T(8,128)(2,1)}, bf16[32,128,128]{2,1,0:T(8,128)(2,1)S(1)}, u32[]{:S(2)}, u32[]{:S(2)}) collective-permute-start(bf16[32,128,128]{2,1,0:T(8,128)(2,1)} %get-tuple-element.37.l0.refs_13_), channel_id=1, source_target_pairs={{2,0},{15,1},{4,2},{1,3},{6,4},{3,5},{8,6},{5,7},{10,8},{7,9},{12,... | collective-permute-start | bytes 3145736 | tf_op jit(solution)/shard_map/ppermute | solution.py:61
  46.9 41.0 %collective-permute-done.4.l1 = bf16[32,128,128]{2,1,0:T(8,128)(2,1)S(1)} collective-permute-done((bf16[32,128,128]{2,1,0:T(8,128)(2,1)}, bf16[32,128,128]{2,1,0:T(8,128)(2,1)S(1)}, u32[]{:S(2)}, u32[]{:S(2)}) %collective-permute-start.4) | collective-permute-done | bytes 1048608 | tf_op jit(solution)/shard_map/ppermute | solution.py:61
  90.5 39.0 %row_lists.1 = (s32[5136]{0:T(1024)}, s32[5136]{0:T(1024)}, s32[8]{0:T(128)}) custom-call(s32[5]{0:T(128)} %get-tuple-element.98.refs_0_, s32[10240]{0:T(1024)} %bitcast.50), custom_call_target="tpu_custom_call" | custom-call | tf_op jit(solution)/shard_map/row_lists/pallas_call | solution.py:471
  130.8 12.8 %next_layer.1 = (bf16[32,128,128]{2,1,0:T(8,128)(2,1)}, bf16[32,128,128]{2,1,0:T(8,128)(2,1)}, bf16[32,128,128]{2,1,0:T(8,128)(2,1)}) custom-call(s32[256]{0:T(256)} %reshape.115.src.refs_0_, bf16[32,8,128,128]{3,2,1,0:T(8,128)(2,1)} %tiles_hbm.5, bf16[32,128,128]{2,1,0:T(8,128)(2,1)} %get-tuple-element.37.l0.refs_13_, bf16[32,128,128]{2,1,0:T(8,128)(2,1)} %copy-done.4, ...), custom_call_target="tpu_custom_call" | custom-call | tf_op jit(solution)/shard_map/next_layer/pallas_call | solution.py:485
  143.6 8.3 %gather_rows.1 = (bf16[1024,128]{1,0:T(8,128)(2,1)}, bf16[1024,128]{1,0:T(8,128)(2,1)}, bf16[1024,128]{1,0:T(8,128)(2,1)}, bf16[1024,128]{1,0:T(8,128)(2,1)}, bf...) custom-call(s32[5136]{0:T(1024)} %get-tuple-element.34.refs_0_.refs_1_, s32[5136]{0:T(1024)} %get-tuple-element.35.refs_1_.refs_2_, ...), custom_call_target="tpu_custom_call" | custom-call | tf_op jit(solution)/shard_map/gather_rows/pallas_call | solution.py:499
  155.7 10.0 %collective-permute-done.10.near = bf16[1024,128]{1,0:T(8,128)(2,1)S(1)} collective-permute-done((bf16[1024,128]{1,0:T(8,128)(2,1)}, bf16[1024,128]{1,0:T(8,128)(2,1)S(1)}, u32[]{:S(2)}, u32[]{:S(2)}) %collective-permute-start.10) | collective-permute-done | bytes 262176 | tf_op jit(solution)/shard_map/ppermute | solution.py:61
  166.5 2.9 scores.1
  169.4 3.4 %collective-permute-start.12 = (bf16[1024,128]{1,0:T(8,128)(2,1)}, bf16[1024,128]{1,0:T(8,128)(2,1)S(1)}, u32[]{:S(2)}, u32[]{:S(2)}) collective-permute-start(bf16[1024,128]{1,0:T(8,128)(2,1)} %get-tuple-element.46), channel_id=1, source_target_pairs={{2,0},{15,1},{4,2},{1,3},{6,4},{3,5},{8,6},{5,7},{10,8},{7,9},{12,... | collective-permute-start | bytes 786440 | tf_op jit(solution)/shard_map/ppermute | solution.py:61
  172.8 2.3 collective-permute-start.14
  175.2 8.7 %collective-permute-done.12.refs_7_ = bf16[1024,128]{1,0:T(8,128)(2,1)S(1)} collective-permute-done((bf16[1024,128]{1,0:T(8,128)(2,1)}, bf16[1024,128]{1,0:T(8,128)(2,1)S(1)}, u32[]{:S(2)}, u32[]{:S(2)}) %collective-permute-start.12) | collective-permute-done | bytes 262176 | tf_op jit(solution)/shard_map/ppermute | solution.py:61
  186.1 20.7 %contrast_layer.1 = (f32[32,128,128]{2,1,0:T(8,128)}, bf16[32,128,128]{2,1,0:T(8,128)(2,1)}, bf16[32,128,128]{2,1,0:T(8,128)(2,1)}, bf16[32,128,128]{2,1,0:T(8,1...) custom-call(s32[256]{0:T(256)} %reshape.115.src.refs_0_, s32[5136]{0:T(1024)} %get-tuple-element.34.refs_0_.refs_1_, ...), custom_call_target="tpu_custom_call" | custom-call | tf_op jit(solution)/shard_map/contrast_layer/pallas_call | solution.py:529
  206.9 3.0 collective-permute-start.23
  209.9 2.6 add_convert_fusion
  213.7 2.2 collective-permute-start.16
  215.9 37.4 %collective-permute-done.23.r2 = bf16[32,128,128]{2,1,0:T(8,128)(2,1)S(1)} collective-permute-done((bf16[32,128,128]{2,1,0:T(8,128)(2,1)}, bf16[32,128,128]{2,1,0:T(8,128)(2,1)S(1)}, u32[]{:S(2)}, u32[]{:S(2)}) %collective-permute-start.23) | collective-permute-done | bytes 1048608 | tf_op jit(solution)/shard_map/ppermute | solution.py:61
  255.0 25.2 %last_layer.1 = (f32[3,128,128]{2,1,0:T(8,128)}, f32[32,128]{1,0:T(8,128)}) custom-call(s32[256]{0:T(256)} %reshape.115.src.refs_0_, bf16[32,8,128,128]{3,2,1,0:T(8,128)(2,1)} %tiles_hbm.5, f32[32,128,128]{2,1,0:T(8,128)} %get-tuple-element.52.own, bf16[32,128,128]{2,1,0:T(8,128)(2,1)} %copy-done.3, bf16[32,128,128]{2,1,0:T(8,128)(2,1)} %copy-done.1, ...), custom_call_target="tpu_custom_call" | custom-call | tf_op jit(solution)/shard_map/last_layer/pallas_call | solution.py:549
  282.8 4.8 %collective-permute-done.17 = f32[196,128]{1,0:T(8,128)S(1)} collective-permute-done((f32[196,128]{1,0:T(8,128)S(1)}, f32[196,128]{1,0:T(8,128)S(1)}, u32[]{:S(2)}, u32[]{:S(2)}) %collective-permute-start.17) | collective-permute-done | bytes 100384 | tf_op jit(solution)/shard_map/ppermute | solution.py:61
  287.6 3.0 collective-permute-start.18
  293.4 2.7 collective-permute-start.19
  301.1 2.2 collective-permute-start.28
  303.4 5.3 %collective-permute-done.28 = f32[208,128]{1,0:T(8,128)S(1)} collective-permute-done((f32[208,128]{1,0:T(8,128)S(1)}, f32[208,128]{1,0:T(8,128)S(1)}, u32[]{:S(2)}, u32[]{:S(2)}) %collective-permute-start.28) | collective-permute-done | bytes 106528 | tf_op jit(solution)/shard_map/ppermute | solution.py:61
  (144 shorter events, 41.6 us)
Async XLA Ops:
  3.9 15.5 %collective-permute-start = (bf16[16,4096]{1,0:T(8,128)(2,1)S(1)}, bf16[16,4096]{1,0:T(8,128)(2,1)S(1)}, u32[]{:S(2)}, u32[]{:S(2)}) collective-permute-start(bf16[16,4096]{1,0:T(8,128)(2,1)S(1)} %maximum_maximum_fusion.p0), channel_id=1, source_target_pairs={{2,0},{15,1},{4,2},{1,3},{6,4},{3,5},{8,6},{5,7},{10,8},{7,9},{12,... | collective-permute-start | bytes 393224 | tf_op jit(solution)/shard_map/ppermute | solution.py:61
  10.0 11.3 %collective-permute-start.1 = (bf16[16,4096]{1,0:T(8,128)(2,1)S(1)}, bf16[16,4096]{1,0:T(8,128)(2,1)S(1)}, u32[]{:S(2)}, u32[]{:S(2)}) collective-permute-start(bf16[16,4096]{1,0:T(8,128)(2,1)S(1)} %maximum_maximum_fusion.p0), channel_id=1, source_target_pairs={{14,0},{3,1},{0,2},{5,3},{2,4},{7,5},{4,6},{9,7},{6,8},{11,9},{8,1... | collective-permute-start | bytes 393224 | tf_op jit(solution)/shard_map/ppermute | solution.py:61
  10.0 11.3 %collective-permute-start.2 = (bf16[16,4096]{1,0:T(8,128)(2,1)S(1)}, bf16[16,4096]{1,0:T(8,128)(2,1)S(1)}, u32[]{:S(2)}, u32[]{:S(2)}) collective-permute-start(bf16[16,4096]{1,0:T(8,128)(2,1)S(1)} %maximum_maximum_fusion.p0), channel_id=1, source_target_pairs={{1,0},{0,1},{3,2},{2,3},{5,4},{4,5},{7,6},{6,7},{9,8},{8,9},{11,10... | collective-permute-start | bytes 393224 | tf_op jit(solution)/shard_map/ppermute | solution.py:61
  40.1 47.8 %collective-permute-start.4 = (bf16[32,128,128]{2,1,0:T(8,128)(2,1)}, bf16[32,128,128]{2,1,0:T(8,128)(2,1)S(1)}, u32[]{:S(2)}, u32[]{:S(2)}) collective-permute-start(bf16[32,128,128]{2,1,0:T(8,128)(2,1)} %get-tuple-element.37.l0.refs_13_), channel_id=1, source_target_pairs={{2,0},{15,1},{4,2},{1,3},{6,4},{3,5},{8,6},{5,7},{10,8},{7,9},{12,... | collective-permute-start | bytes 3145736 | tf_op jit(solution)/shard_map/ppermute | solution.py:61
  46.8 82.7 %collective-permute-start.5 = (bf16[32,128,128]{2,1,0:T(8,128)(2,1)}, bf16[32,128,128]{2,1,0:T(8,128)(2,1)S(1)}, u32[]{:S(2)}, u32[]{:S(2)}) collective-permute-start(bf16[32,128,128]{2,1,0:T(8,128)(2,1)} %get-tuple-element.37.l0.refs_13_), channel_id=1, source_target_pairs={{14,0},{3,1},{0,2},{5,3},{2,4},{7,5},{4,6},{9,7},{6,8},{11,9},{8,1... | collective-permute-start | bytes 3145736 | tf_op jit(solution)/shard_map/ppermute | solution.py:61
  46.8 82.7 %collective-permute-start.6 = (bf16[32,128,128]{2,1,0:T(8,128)(2,1)}, bf16[32,128,128]{2,1,0:T(8,128)(2,1)S(1)}, u32[]{:S(2)}, u32[]{:S(2)}) collective-permute-start(bf16[32,128,128]{2,1,0:T(8,128)(2,1)} %get-tuple-element.37.l0.refs_13_), channel_id=1, source_target_pairs={{1,0},{0,1},{3,2},{2,3},{5,4},{4,5},{7,6},{6,7},{9,8},{8,9},{11,10... | collective-permute-start | bytes 3145736 | tf_op jit(solution)/shard_map/ppermute | solution.py:61
  87.9 41.7 %collective-permute-start.7 = (bf16[32,128,128]{2,1,0:T(8,128)(2,1)S(1)}, bf16[32,128,128]{2,1,0:T(8,128)(2,1)}, u32[]{:S(2)}, u32[]{:S(2)}) collective-permute-start(bf16[32,128,128]{2,1,0:T(8,128)(2,1)S(1)} %collective-permute-done.4.l1), channel_id=1, source_target_pairs={{1,0},{0,1},{3,2},{2,3},{5,4},{4,5},{7,6},{6,7},{9,8},{8,9},{11,10... | collective-permute-start | bytes 3145736 | tf_op jit(solution)/shard_map/ppermute | solution.py:61
  152.6 13.1 %collective-permute-start.10 = (bf16[1024,128]{1,0:T(8,128)(2,1)}, bf16[1024,128]{1,0:T(8,128)(2,1)S(1)}, u32[]{:S(2)}, u32[]{:S(2)}) collective-permute-start(bf16[1024,128]{1,0:T(8,128)(2,1)} %get-tuple-element.42), channel_id=1, source_target_pairs={{0,14},{1,3},{2,0},{3,5},{4,2},{5,7},{6,4},{7,9},{8,6},{9,11},{10,... | collective-permute-start | bytes 786440 | tf_op jit(solution)/shard_map/ppermute | solution.py:61
  154.3 11.3 %collective-permute-start.11 = (bf16[1024,128]{1,0:T(8,128)(2,1)}, bf16[1024,128]{1,0:T(8,128)(2,1)S(1)}, u32[]{:S(2)}, u32[]{:S(2)}) collective-permute-start(bf16[1024,128]{1,0:T(8,128)(2,1)} %get-tuple-element.43), channel_id=1, source_target_pairs={{1,0},{0,1},{3,2},{2,3},{5,4},{4,5},{7,6},{6,7},{9,8},{8,9},{11,10... | collective-permute-start | bytes 786440 | tf_op jit(solution)/shard_map/ppermute | solution.py:61
  155.3 10.3 %collective-permute-start.9 = (bf16[1024,128]{1,0:T(8,128)(2,1)S(1)}, bf16[1024,128]{1,0:T(8,128)(2,1)S(1)}, u32[]{:S(2)}, u32[]{:S(2)}) collective-permute-start(bf16[1024,128]{1,0:T(8,128)(2,1)S(1)} %add_convert_fusion.1), channel_id=1, source_target_pairs={{0,2},{1,15},{2,4},{3,1},{4,6},{5,3},{6,8},{7,5},{8,10},{9,7},{10,... | collective-permute-start | bytes 786440 | tf_op jit(solution)/shard_map/ppermute | solution.py:61
  169.4 14.4 %collective-permute-start.12 = (bf16[1024,128]{1,0:T(8,128)(2,1)}, bf16[1024,128]{1,0:T(8,128)(2,1)S(1)}, u32[]{:S(2)}, u32[]{:S(2)}) collective-permute-start(bf16[1024,128]{1,0:T(8,128)(2,1)} %get-tuple-element.46), channel_id=1, source_target_pairs={{2,0},{15,1},{4,2},{1,3},{6,4},{3,5},{8,6},{5,7},{10,8},{7,9},{12,... | collective-permute-start | bytes 786440 | tf_op jit(solution)/shard_map/ppermute | solution.py:61
  172.8 11.0 %collective-permute-start.13 = (bf16[1024,128]{1,0:T(8,128)(2,1)}, bf16[1024,128]{1,0:T(8,128)(2,1)S(1)}, u32[]{:S(2)}, u32[]{:S(2)}) collective-permute-start(bf16[1024,128]{1,0:T(8,128)(2,1)} %get-tuple-element.46), channel_id=1, source_target_pairs={{14,0},{3,1},{0,2},{5,3},{2,4},{7,5},{4,6},{9,7},{6,8},{11,9},{8,1... | collective-permute-start | bytes 786440 | tf_op jit(solution)/shard_map/ppermute | solution.py:61
  172.8 11.0 %collective-permute-start.14 = (bf16[1024,128]{1,0:T(8,128)(2,1)}, bf16[1024,128]{1,0:T(8,128)(2,1)S(1)}, u32[]{:S(2)}, u32[]{:S(2)}) collective-permute-start(bf16[1024,128]{1,0:T(8,128)(2,1)} %get-tuple-element.46), channel_id=1, source_target_pairs={{1,0},{0,1},{3,2},{2,3},{5,4},{4,5},{7,6},{6,7},{9,8},{8,9},{11,10... | collective-permute-start | bytes 786440 | tf_op jit(solution)/shard_map/ppermute | solution.py:61
  206.9 46.4 %collective-permute-start.23 = (bf16[32,128,128]{2,1,0:T(8,128)(2,1)}, bf16[32,128,128]{2,1,0:T(8,128)(2,1)S(1)}, u32[]{:S(2)}, u32[]{:S(2)}) collective-permute-start(bf16[32,128,128]{2,1,0:T(8,128)(2,1)} %get-tuple-element.55), channel_id=1, source_target_pairs={{0,14},{1,3},{2,0},{3,5},{4,2},{5,7},{6,4},{7,9},{8,6},{9,11},{10,... | collective-permute-start | bytes 3145736 | tf_op jit(solution)/shard_map/ppermute | solution.py:61
  209.9 43.5 %collective-permute-start.24 = (bf16[32,128,128]{2,1,0:T(8,128)(2,1)}, bf16[32,128,128]{2,1,0:T(8,128)(2,1)S(1)}, u32[]{:S(2)}, u32[]{:S(2)}) collective-permute-start(bf16[32,128,128]{2,1,0:T(8,128)(2,1)} %get-tuple-element.56), channel_id=1, source_target_pairs={{1,0},{0,1},{3,2},{2,3},{5,4},{4,5},{7,6},{6,7},{9,8},{8,9},{11,10... | collective-permute-start | bytes 3145736 | tf_op jit(solution)/shard_map/ppermute | solution.py:61
  212.5 40.8 %collective-permute-start.22 = (bf16[32,128,128]{2,1,0:T(8,128)(2,1)}, bf16[32,128,128]{2,1,0:T(8,128)(2,1)S(1)}, u32[]{:S(2)}, u32[]{:S(2)}) collective-permute-start(bf16[32,128,128]{2,1,0:T(8,128)(2,1)} %add_convert_fusion), channel_id=1, source_target_pairs={{0,2},{1,15},{2,4},{3,1},{4,6},{5,3},{6,8},{7,5},{8,10},{9,7},{10,... | collective-permute-start | bytes 3145736 | tf_op jit(solution)/shard_map/ppermute | solution.py:61
  213.7 68.9 %collective-permute-start.16 = (f32[196,128]{1,0:T(8,128)S(1)}, f32[196,128]{1,0:T(8,128)S(1)}, u32[]{:S(2)}, u32[]{:S(2)}) collective-permute-start(f32[196,128]{1,0:T(8,128)S(1)} %fusion.3), channel_id=1, source_target_pairs={{1,0},{0,1},{3,2},{2,3},{5,4},{4,5},{7,6},{6,7},{9,8},{8,9},{11,10... | collective-permute-start | bytes 301064 | tf_op jit(solution)/shard_map/ppermute | solution.py:61
  281.2 9.5 %collective-permute-start.25 = (f32[208,128]{1,0:T(8,128)S(1)}, f32[208,128]{1,0:T(8,128)S(1)}, u32[]{:S(2)}, u32[]{:S(2)}) collective-permute-start(f32[208,128]{1,0:T(8,128)S(1)} %fusion), channel_id=1, source_target_pairs={{1,0},{0,1},{3,2},{2,3},{5,4},{4,5},{7,6},{6,7},{9,8},{8,9},{11,10... | collective-permute-start | bytes 319496 | tf_op jit(solution)/shard_map/ppermute | solution.py:61
  282.7 4.9 %collective-permute-start.17 = (f32[196,128]{1,0:T(8,128)S(1)}, f32[196,128]{1,0:T(8,128)S(1)}, u32[]{:S(2)}, u32[]{:S(2)}) collective-permute-start(f32[196,128]{1,0:T(8,128)S(1)} %fusion.5), channel_id=1, source_target_pairs={{0,2},{1,3},{2,0},{3,1},{4,6},{5,7},{6,4},{7,5},{8,10},{9,11},{10,... | collective-permute-start | bytes 301064 | tf_op jit(solution)/shard_map/ppermute | solution.py:61
  287.6 5.8 %collective-permute-start.18 = (f32[196,128]{1,0:T(8,128)S(1)}, f32[196,128]{1,0:T(8,128)S(1)}, u32[]{:S(2)}, u32[]{:S(2)}) collective-permute-start(f32[196,128]{1,0:T(8,128)S(1)} %add.88), channel_id=1, source_target_pairs={{0,4},{1,5},{2,6},{3,7},{4,0},{5,1},{6,2},{7,3},{8,12},{9,13},{10,... | collective-permute-start | bytes 301064 | tf_op jit(solution)/shard_map/ppermute | solution.py:61
  291.6 4.8 %collective-permute-start.26 = (f32[208,128]{1,0:T(8,128)S(1)}, f32[208,128]{1,0:T(8,128)S(1)}, u32[]{:S(2)}, u32[]{:S(2)}) collective-permute-start(f32[208,128]{1,0:T(8,128)S(1)} %fusion.2), channel_id=1, source_target_pairs={{0,2},{1,3},{2,0},{3,1},{4,6},{5,7},{6,4},{7,5},{8,10},{9,11},{10,... | collective-permute-start | bytes 319496 | tf_op jit(solution)/shard_map/ppermute | solution.py:61
  293.4 6.2 %collective-permute-start.19 = (f32[196,128]{1,0:T(8,128)S(1)}, f32[196,128]{1,0:T(8,128)S(1)}, u32[]{:S(2)}, u32[]{:S(2)}) collective-permute-start(f32[196,128]{1,0:T(8,128)S(1)} %add.89), channel_id=1, source_target_pairs={{0,8},{1,9},{2,10},{3,11},{4,12},{5,13},{6,14},{7,15},{8,0},{9,1},... | collective-permute-start | bytes 301064 | tf_op jit(solution)/shard_map/ppermute | solution.py:61
  296.3 4.8 %collective-permute-start.27 = (f32[208,128]{1,0:T(8,128)S(1)}, f32[208,128]{1,0:T(8,128)S(1)}, u32[]{:S(2)}, u32[]{:S(2)}) collective-permute-start(f32[208,128]{1,0:T(8,128)S(1)} %add.95), channel_id=1, source_target_pairs={{0,4},{1,5},{2,6},{3,7},{4,0},{5,1},{6,2},{7,3},{8,12},{9,13},{10,... | collective-permute-start | bytes 319496 | tf_op jit(solution)/shard_map/ppermute | solution.py:61
  301.1 7.6 %collective-permute-start.28 = (f32[208,128]{1,0:T(8,128)S(1)}, f32[208,128]{1,0:T(8,128)S(1)}, u32[]{:S(2)}, u32[]{:S(2)}) collective-permute-start(f32[208,128]{1,0:T(8,128)S(1)} %add.96), channel_id=1, source_target_pairs={{0,8},{1,9},{2,10},{3,11},{4,12},{5,13},{6,14},{7,15},{8,0},{9,1},... | collective-permute-start | bytes 319496 | tf_op jit(solution)/shard_map/ppermute | solution.py:61
  (27 other events, 111.2 us)

commit v2 on v1

--- a/solution.py
+++ b/solution.py
@@ -33,6 +33,10 @@
     return pltpu.CompilerParams(vmem_limit_bytes=VMEM_LIMIT)
 
 
+def cost(microseconds):
+    return pl.CostEstimate(flops=0, transcendentals=0, bytes_accessed=int(microseconds * 3.6e6))
+
+
 def dot_nn(left, right):
     return lax.dot_general(left, right, (((1,), (0,)), ((), ())), preferred_element_type=F32)
 
@@ -65,12 +69,16 @@
     return [(target, source) for source, target in pairs]
 
 
-def gather_window(value):
+def after(value, *earlier):
+    return lax.optimization_barrier((value, *earlier))[0]
+
+
+def gather_window(value, *meanwhile):
     count = lax.axis_size("phi")
     far = send(value, far_pairs(count))
     near = send(value, near_pairs(count))
     other = send(value, core_pairs(count))
-    passed = send(far, core_pairs(count))
+    passed = send(after(far, *meanwhile) if meanwhile else far, core_pairs(count))
     return (value, far, near, other, passed)
 
 
@@ -462,6 +470,7 @@
         scratch_shapes=[tile_scratch, window_scratch, group_sems],
         compiler_params=params(),
         name="first_layer",
+        cost_estimate=cost(18),
     )(src, edge_tiles, *packs, w_in, w_self[0], w_agg[0], w_out[0])
 
     indices = jnp.stack([each[feats + 1] for each in packs]).astype(jnp.int32)
@@ -479,9 +488,10 @@
         out_specs=(smem(),) * 3,
         compiler_params=params(),
         name="row_lists",
+        cost_estimate=cost(39),
     )(part_back.astype(jnp.int32), indices)
 
-    window_1 = gather_window(latents_1)
+    window_1 = gather_window(latents_1, counts)
     agg_1, hidden_1, latents_2 = pl.pallas_call(
         next_layer_kernel,
         out_shape=(blocked,) * 3,
@@ -492,6 +502,7 @@
         ],
         compiler_params=params(),
         name="next_layer",
+        cost_estimate=cost(13),
     )(src, edge_tiles, *window_1, w_self[1], w_agg[1], w_out[1])
 
     triplet_rows = jax.ShapeDtypeStruct((triplets, width), BF16)
@@ -509,6 +520,7 @@
         ],
         compiler_params=params(),
         name="gather_rows",
+        cost_estimate=cost(8),
     )(negative_list, positive_list, counts, anchor_hits, latents_2)
     gap_own, gap_far, gap_near, gap_other, gap_passed, anchor_rows = gathered
     gaps = return_pieces(gap_far, gap_near, gap_other, gap_passed)
@@ -520,6 +532,7 @@
         out_specs=(vmem(),) * 4,
         compiler_params=params(),
         name="scores",
+        cost_estimate=cost(3),
     )(gap_own, *gaps, anchor_rows)
     weighted_window = gather_window(weighted_b)
 
@@ -538,6 +551,7 @@
         + [group_sems],
         compiler_params=params(),
         name="contrast_layer",
+        cost_estimate=cost(20),
     )(
         src, negative_list, positive_list, counts, anchor_hits, edge_tiles,
         weighted, *weighted_window[1:], anchor_grad, hidden_1, latents_1, agg_1,
@@ -554,6 +568,7 @@
         scratch_shapes=[tile_scratch, spread_scratch, group_sems],
         compiler_params=params(),
         name="last_layer",
+        cost_estimate=cost(25),
     )(
         src, edge_tiles, own_1, *returned, hidden_0, latents_0, agg_0,
         w_self[0], w_agg[0], w_out[0], w_in.T, *packs,

time: 316 us -> 277 us (0.88)
  waiting for transfers between devices: 114 us -> 76.6 us
    ppermute x30, waiting for transfers between devices: 114 us -> 76.6 us  [send(): return lax.ppermute(value, 'phi', pairs)]
    unnamed x48 -> x50, local copies, waits for them, and re-layouts: 6.79 us -> 6.29 us
  transfers between devices with their start and end apart: 30 -> 30, of which waited for: 12 -> 14; matrix products, arithmetic and copies ran while one was open for 7% -> 7% of each run, Pallas kernels for 20% -> 23%
where the time goes in v2:
time: 277 us; the launch traced here: 276 us
  Pallas kernels  127 us (46%)
  waiting for transfers between devices  76.6 us (28%)
  starting transfers between devices  37.8 us (14%)
  other arithmetic  16.7 us (6%)
  local copies, waits for them, and re-layouts  15.1 us (5%)
  between operations  2.81 us (1%)
    ppermute x30, waiting for transfers between devices, send(): return lax.ppermute(value, 'phi', pairs)  76.6 us
    pallas_call x1, Pallas kernels, body(): pl.pallas_call(lambda *refs: list_kernel(row_bits, triplets, *refs), out_...  39.3 us
    ppermute x30, starting transfers between devices, send(): return lax.ppermute(value, 'phi', pairs)  37.8 us
    pallas_call x1, Pallas kernels, body(): pl.pallas_call(last_layer_kernel, out_shape=(grads_shape, jax.ShapeDtypeS...  25.2 us
    pallas_call x1, Pallas kernels, body(): pl.pallas_call(lambda *refs: contrast_layer_kernel(row_bits, *refs), out_...  20.7 us
    pallas_call x1, Pallas kernels, body(): pl.pallas_call(first_layer_kernel, out_shape=(blocked,) * 4, in_specs=[sm...  18.1 us
    pallas_call x1, Pallas kernels, body(): pl.pallas_call(next_layer_kernel, out_shape=(blocked,) * 3, in_specs=[sme...  12.8 us
    pallas_call x1, Pallas kernels, body(): pl.pallas_call(lambda *refs: gather_kernel(row_bits, *refs), out_shape=(t...  8.25 us
  transfers between devices with their start and end apart: 30, of which 14 were waited for; matrix products, arithmetic and copies ran while one was open for 7% of the time, Pallas kernels for 23%

profile of v2, /device:TPU:0, one launch (start us, length us, event | category | flops | bytes accessed | tf_op | source)
XLA Modules:
  0.0 276.2 jit_solution(14979974544151144728)
XLA Ops:
  3.9 6.1 %collective-permute-start = (bf16[16,4096]{1,0:T(8,128)(2,1)S(1)}, bf16[16,4096]{1,0:T(8,128)(2,1)S(1)}, u32[]{:S(2)}, u32[]{:S(2)}) collective-permute-start(bf16[16,4096]{1,0:T(8,128)(2,1)S(1)} %maximum_maximum_fusion.p0), channel_id=1, source_target_pairs={{2,0},{15,1},{4,2},{1,3},{6,4},{3,5},{8,6},{5,7},{10,8},{7,9},{12,... | collective-permute-start | bytes 393224 | tf_op jit(solution)/shard_map/ppermute | solution.py:65
  16.1 3.9 %fusion.7 = s32[32,8]{0,1:T(8,128)S(1)} fusion(s32[32,8]{0,1:T(8,128)} %param.20, s32[]{:T(128)} %bitcast.4, s32[]{:T(128)} %bitcast.3, s32[]{:T(128)} %bitcast.2, s32[]{:T(128)} %bitcast.1, s32[]{:T(128)} %bitcast, s32[32]{0:T(128)} %param.21), kind=kLoop, calls=%fused_computation.63 | loop fusion | flops 8448 | bytes 2196 | tf_op jit(solution)/shard_map/jit(_where)/select_n | solution.py:456
  23.1 18.1 %first_layer.1 = (bf16[32,128,128]{2,1,0:T(8,128)(2,1)}, bf16[32,128,128]{2,1,0:T(8,128)(2,1)}, bf16[32,128,128]{2,1,0:T(8,128)(2,1)}, bf16[32,128,128]{2,1,0:T(8,128)(2,1)}) custom-call(s32[256]{0:T(256)} %reshape.115.src.refs_0_, bf16[32,8,128,128]{3,2,1,0:T(8,128)(2,1)} %tiles_hbm.5, bf16[16,4096]{1,0:T(8,128)(2,1)} %copy-done, ...), custom_call_target="tpu_custom_call" | custom-call | bytes 64800000 | tf_op jit(solution)/shard_map/first_layer/pallas_call | solution.py:465
  41.2 4.8 %collective-permute-start.4 = (bf16[32,128,128]{2,1,0:T(8,128)(2,1)}, bf16[32,128,128]{2,1,0:T(8,128)(2,1)S(1)}, u32[]{:S(2)}, u32[]{:S(2)}) collective-permute-start(bf16[32,128,128]{2,1,0:T(8,128)(2,1)} %get-tuple-element.38.l0.refs_13_), channel_id=1, source_target_pairs={{2,0},{15,1},{4,2},{1,3},{6,4},{3,5},{8,6},{5,7},{10,8},{7,9},{12,... | collective-permute-start | bytes 3145736 | tf_op jit(solution)/shard_map/ppermute | solution.py:65
  48.7 39.3 %row_lists.1 = (s32[5136]{0:T(1024)}, s32[5136]{0:T(1024)}, s32[8]{0:T(128)}) custom-call(s32[5]{0:T(128)} %get-tuple-element.100.refs_0_, s32[10240]{0:T(1024)} %bitcast.50), custom_call_target="tpu_custom_call" | custom-call | bytes 140400000 | tf_op jit(solution)/shard_map/row_lists/pallas_call | solution.py:480
  89.7 2.6 collective-permute-done.7.l4
  93.3 12.8 %next_layer.1 = (bf16[32,128,128]{2,1,0:T(8,128)(2,1)}, bf16[32,128,128]{2,1,0:T(8,128)(2,1)}, bf16[32,128,128]{2,1,0:T(8,128)(2,1)}) custom-call(s32[256]{0:T(256)} %reshape.115.src.refs_0_, bf16[32,8,128,128]{3,2,1,0:T(8,128)(2,1)} %tiles_hbm.5, bf16[32,128,128]{2,1,0:T(8,128)(2,1)} %get-tuple-element.38.l0.refs_13_, bf16[32,128,128]{2,1,0:T(8,128)(2,1)} %copy-done.4, ...), custom_call_target="tpu_custom_call" | custom-call | bytes 46800000 | tf_op jit(solution)/shard_map/next_layer/pallas_call | solution.py:495
  106.1 8.2 %gather_rows.1 = (bf16[1024,128]{1,0:T(8,128)(2,1)}, bf16[1024,128]{1,0:T(8,128)(2,1)}, bf16[1024,128]{1,0:T(8,128)(2,1)}, bf16[1024,128]{1,0:T(8,128)(2,1)}, bf...) custom-call(s32[5136]{0:T(1024)} %get-tuple-element.35.refs_0_.refs_1_, s32[5136]{0:T(1024)} %get-tuple-element.36.refs_1_.refs_2_, ...), custom_call_target="tpu_custom_call" | custom-call | bytes 28800000 | tf_op jit(solution)/shard_map/gather_rows/pallas_call | solution.py:510
  114.3 3.0 %collective-permute-start.10 = (bf16[1024,128]{1,0:T(8,128)(2,1)}, bf16[1024,128]{1,0:T(8,128)(2,1)S(1)}, u32[]{:S(2)}, u32[]{:S(2)}) collective-permute-start(bf16[1024,128]{1,0:T(8,128)(2,1)} %get-tuple-element.44), channel_id=1, source_target_pairs={{0,14},{1,3},{2,0},{3,5},{4,2},{5,7},{6,4},{7,9},{8,6},{9,11},{10,... | collective-permute-start | bytes 786440 | tf_op jit(solution)/shard_map/ppermute | solution.py:65
  118.4 5.8 %collective-permute-done.10.near = bf16[1024,128]{1,0:T(8,128)(2,1)S(1)} collective-permute-done((bf16[1024,128]{1,0:T(8,128)(2,1)}, bf16[1024,128]{1,0:T(8,128)(2,1)S(1)}, u32[]{:S(2)}, u32[]{:S(2)}) %collective-permute-start.10) | collective-permute-done | bytes 262176 | tf_op jit(solution)/shard_map/ppermute | solution.py:65
  124.2 3.3 %collective-permute-done.9.far = bf16[1024,128]{1,0:T(8,128)(2,1)S(1)} collective-permute-done((bf16[1024,128]{1,0:T(8,128)(2,1)S(1)}, bf16[1024,128]{1,0:T(8,128)(2,1)S(1)}, u32[]{:S(2)}, u32[]{:S(2)}) %collective-permute-start.9) | collective-permute-done | bytes 262176 | tf_op jit(solution)/shard_map/ppermute | solution.py:65
  128.3 2.9 %scores.1 = (f32[8,128]{1,0:T(8,128)}, f32[1024,128]{1,0:T(8,128)}, bf16[1024,128]{1,0:T(8,128)(2,1)}, f32[1024,128]{1,0:T(8,128)}) custom-call(bf16[1024,128]{1,0:T(8,128)(2,1)} %get-tuple-element.41.own, bf16[1024,128]{1,0:T(8,128)(2,1)} %copy-done.19, bf16[1024,128]{1,0:T(8,128)(2,1)} %copy-done.16, bf16[1024,128]{1,0:T(8,128)(2,1)} %copy-done.17, ...), custom_call_target="tpu_custom_call" | custom-call | bytes 10800000 | tf_op jit(solution)/shard_map/scores/pallas_call | solution.py:528
  131.2 4.6 %collective-permute-start.12 = (bf16[1024,128]{1,0:T(8,128)(2,1)}, bf16[1024,128]{1,0:T(8,128)(2,1)S(1)}, u32[]{:S(2)}, u32[]{:S(2)}) collective-permute-start(bf16[1024,128]{1,0:T(8,128)(2,1)} %get-tuple-element.48), channel_id=1, source_target_pairs={{2,0},{15,1},{4,2},{1,3},{6,4},{3,5},{8,6},{5,7},{10,8},{7,9},{12,... | collective-permute-start | bytes 786440 | tf_op jit(solution)/shard_map/ppermute | solution.py:65
  137.0 8.5 %collective-permute-done.12.refs_7_ = bf16[1024,128]{1,0:T(8,128)(2,1)S(1)} collective-permute-done((bf16[1024,128]{1,0:T(8,128)(2,1)}, bf16[1024,128]{1,0:T(8,128)(2,1)S(1)}, u32[]{:S(2)}, u32[]{:S(2)}) %collective-permute-start.12) | collective-permute-done | bytes 262176 | tf_op jit(solution)/shard_map/ppermute | solution.py:65
  147.8 20.7 %contrast_layer.1 = (f32[32,128,128]{2,1,0:T(8,128)}, bf16[32,128,128]{2,1,0:T(8,128)(2,1)}, bf16[32,128,128]{2,1,0:T(8,128)(2,1)}, bf16[32,128,128]{2,1,0:T(8,1...) custom-call(s32[256]{0:T(256)} %reshape.115.src.refs_0_, s32[5136]{0:T(1024)} %get-tuple-element.35.refs_0_.refs_1_, ...), custom_call_target="tpu_custom_call" | custom-call | bytes 72000000 | tf_op jit(solution)/shard_map/contrast_layer/pallas_call | solution.py:542
  168.6 2.8 %collective-permute-start.23 = (bf16[32,128,128]{2,1,0:T(8,128)(2,1)}, bf16[32,128,128]{2,1,0:T(8,128)(2,1)S(1)}, u32[]{:S(2)}, u32[]{:S(2)}) collective-permute-start(bf16[32,128,128]{2,1,0:T(8,128)(2,1)} %get-tuple-element.57), channel_id=1, source_target_pairs={{0,14},{1,3},{2,0},{3,5},{4,2},{5,7},{6,4},{7,9},{8,6},{9,11},{10,... | collective-permute-start | bytes 3145736 | tf_op jit(solution)/shard_map/ppermute | solution.py:65
  171.4 2.6 add_convert_fusion
  177.5 37.5 %collective-permute-done.23.r2 = bf16[32,128,128]{2,1,0:T(8,128)(2,1)S(1)} collective-permute-done((bf16[32,128,128]{2,1,0:T(8,128)(2,1)}, bf16[32,128,128]{2,1,0:T(8,128)(2,1)S(1)}, u32[]{:S(2)}, u32[]{:S(2)}) %collective-permute-start.23) | collective-permute-done | bytes 1048608 | tf_op jit(solution)/shard_map/ppermute | solution.py:65
  216.7 25.2 %last_layer.1 = (f32[3,128,128]{2,1,0:T(8,128)}, f32[32,128]{1,0:T(8,128)}) custom-call(s32[256]{0:T(256)} %reshape.115.src.refs_0_, bf16[32,8,128,128]{3,2,1,0:T(8,128)(2,1)} %tiles_hbm.5, f32[32,128,128]{2,1,0:T(8,128)} %get-tuple-element.54.own, bf16[32,128,128]{2,1,0:T(8,128)(2,1)} %copy-done.3, bf16[32,128,128]{2,1,0:T(8,128)(2,1)} %copy-done.1, ...), custom_call_target="tpu_custom_call" | custom-call | bytes 90000000 | tf_op jit(solution)/shard_map/last_layer/pallas_call | solution.py:563
  244.5 4.8 %collective-permute-done.17 = f32[196,128]{1,0:T(8,128)S(1)} collective-permute-done((f32[196,128]{1,0:T(8,128)S(1)}, f32[196,128]{1,0:T(8,128)S(1)}, u32[]{:S(2)}, u32[]{:S(2)}) %collective-permute-start.17) | collective-permute-done | bytes 100384 | tf_op jit(solution)/shard_map/ppermute | solution.py:65
  249.3 2.4 collective-permute-start.18
  254.4 3.2 %collective-permute-start.19 = (f32[196,128]{1,0:T(8,128)S(1)}, f32[196,128]{1,0:T(8,128)S(1)}, u32[]{:S(2)}, u32[]{:S(2)}) collective-permute-start(f32[196,128]{1,0:T(8,128)S(1)} %add.89), channel_id=1, source_target_pairs={{0,8},{1,9},{2,10},{3,11},{4,12},{5,13},{6,14},{7,15},{8,0},{9,1},... | collective-permute-start | bytes 301064 | tf_op jit(solution)/shard_map/ppermute | solution.py:65
  262.4 2.5 collective-permute-start.28
  265.0 5.2 %collective-permute-done.28 = f32[208,128]{1,0:T(8,128)S(1)} collective-permute-done((f32[208,128]{1,0:T(8,128)S(1)}, f32[208,128]{1,0:T(8,128)S(1)}, u32[]{:S(2)}, u32[]{:S(2)}) %collective-permute-start.28) | collective-permute-done | bytes 106528 | tf_op jit(solution)/shard_map/ppermute | solution.py:65
  (146 shorter events, 42.6 us)
Async XLA Ops:
  3.9 16.8 %collective-permute-start = (bf16[16,4096]{1,0:T(8,128)(2,1)S(1)}, bf16[16,4096]{1,0:T(8,128)(2,1)S(1)}, u32[]{:S(2)}, u32[]{:S(2)}) collective-permute-start(bf16[16,4096]{1,0:T(8,128)(2,1)S(1)} %maximum_maximum_fusion.p0), channel_id=1, source_target_pairs={{2,0},{15,1},{4,2},{1,3},{6,4},{3,5},{8,6},{5,7},{10,8},{7,9},{12,... | collective-permute-start | bytes 393224 | tf_op jit(solution)/shard_map/ppermute | solution.py:65
  10.0 10.8 %collective-permute-start.1 = (bf16[16,4096]{1,0:T(8,128)(2,1)S(1)}, bf16[16,4096]{1,0:T(8,128)(2,1)S(1)}, u32[]{:S(2)}, u32[]{:S(2)}) collective-permute-start(bf16[16,4096]{1,0:T(8,128)(2,1)S(1)} %maximum_maximum_fusion.p0), channel_id=1, source_target_pairs={{14,0},{3,1},{0,2},{5,3},{2,4},{7,5},{4,6},{9,7},{6,8},{11,9},{8,1... | collective-permute-start | bytes 393224 | tf_op jit(solution)/shard_map/ppermute | solution.py:65
  10.0 11.5 %collective-permute-start.2 = (bf16[16,4096]{1,0:T(8,128)(2,1)S(1)}, bf16[16,4096]{1,0:T(8,128)(2,1)S(1)}, u32[]{:S(2)}, u32[]{:S(2)}) collective-permute-start(bf16[16,4096]{1,0:T(8,128)(2,1)S(1)} %maximum_maximum_fusion.p0), channel_id=1, source_target_pairs={{1,0},{0,1},{3,2},{2,3},{5,4},{4,5},{7,6},{6,7},{9,8},{8,9},{11,10... | collective-permute-start | bytes 393224 | tf_op jit(solution)/shard_map/ppermute | solution.py:65
  41.2 48.5 %collective-permute-start.4 = (bf16[32,128,128]{2,1,0:T(8,128)(2,1)}, bf16[32,128,128]{2,1,0:T(8,128)(2,1)S(1)}, u32[]{:S(2)}, u32[]{:S(2)}) collective-permute-start(bf16[32,128,128]{2,1,0:T(8,128)(2,1)} %get-tuple-element.38.l0.refs_13_), channel_id=1, source_target_pairs={{2,0},{15,1},{4,2},{1,3},{6,4},{3,5},{8,6},{5,7},{10,8},{7,9},{12,... | collective-permute-start | bytes 3145736 | tf_op jit(solution)/shard_map/ppermute | solution.py:65
  46.9 42.8 %collective-permute-start.5 = (bf16[32,128,128]{2,1,0:T(8,128)(2,1)}, bf16[32,128,128]{2,1,0:T(8,128)(2,1)S(1)}, u32[]{:S(2)}, u32[]{:S(2)}) collective-permute-start(bf16[32,128,128]{2,1,0:T(8,128)(2,1)} %get-tuple-element.38.l0.refs_13_), channel_id=1, source_target_pairs={{14,0},{3,1},{0,2},{5,3},{2,4},{7,5},{4,6},{9,7},{6,8},{11,9},{8,1... | collective-permute-start | bytes 3145736 | tf_op jit(solution)/shard_map/ppermute | solution.py:65
  47.0 42.7 %collective-permute-start.6 = (bf16[32,128,128]{2,1,0:T(8,128)(2,1)}, bf16[32,128,128]{2,1,0:T(8,128)(2,1)S(1)}, u32[]{:S(2)}, u32[]{:S(2)}) collective-permute-start(bf16[32,128,128]{2,1,0:T(8,128)(2,1)} %get-tuple-element.38.l0.refs_13_), channel_id=1, source_target_pairs={{1,0},{0,1},{3,2},{2,3},{5,4},{4,5},{7,6},{6,7},{9,8},{8,9},{11,10... | collective-permute-start | bytes 3145736 | tf_op jit(solution)/shard_map/ppermute | solution.py:65
  114.3 9.9 %collective-permute-start.10 = (bf16[1024,128]{1,0:T(8,128)(2,1)}, bf16[1024,128]{1,0:T(8,128)(2,1)S(1)}, u32[]{:S(2)}, u32[]{:S(2)}) collective-permute-start(bf16[1024,128]{1,0:T(8,128)(2,1)} %get-tuple-element.44), channel_id=1, source_target_pairs={{0,14},{1,3},{2,0},{3,5},{4,2},{5,7},{6,4},{7,9},{8,6},{9,11},{10,... | collective-permute-start | bytes 786440 | tf_op jit(solution)/shard_map/ppermute | solution.py:65
  117.3 6.9 %collective-permute-start.11 = (bf16[1024,128]{1,0:T(8,128)(2,1)}, bf16[1024,128]{1,0:T(8,128)(2,1)S(1)}, u32[]{:S(2)}, u32[]{:S(2)}) collective-permute-start(bf16[1024,128]{1,0:T(8,128)(2,1)} %get-tuple-element.45), channel_id=1, source_target_pairs={{1,0},{0,1},{3,2},{2,3},{5,4},{4,5},{7,6},{6,7},{9,8},{8,9},{11,10... | collective-permute-start | bytes 786440 | tf_op jit(solution)/shard_map/ppermute | solution.py:65
  118.3 9.2 %collective-permute-start.9 = (bf16[1024,128]{1,0:T(8,128)(2,1)S(1)}, bf16[1024,128]{1,0:T(8,128)(2,1)S(1)}, u32[]{:S(2)}, u32[]{:S(2)}) collective-permute-start(bf16[1024,128]{1,0:T(8,128)(2,1)S(1)} %add_convert_fusion.1), channel_id=1, source_target_pairs={{0,2},{1,15},{2,4},{3,1},{4,6},{5,3},{6,8},{7,5},{8,10},{9,7},{10,... | collective-permute-start | bytes 786440 | tf_op jit(solution)/shard_map/ppermute | solution.py:65
  131.2 14.3 %collective-permute-start.12 = (bf16[1024,128]{1,0:T(8,128)(2,1)}, bf16[1024,128]{1,0:T(8,128)(2,1)S(1)}, u32[]{:S(2)}, u32[]{:S(2)}) collective-permute-start(bf16[1024,128]{1,0:T(8,128)(2,1)} %get-tuple-element.48), channel_id=1, source_target_pairs={{2,0},{15,1},{4,2},{1,3},{6,4},{3,5},{8,6},{5,7},{10,8},{7,9},{12,... | collective-permute-start | bytes 786440 | tf_op jit(solution)/shard_map/ppermute | solution.py:65
  135.8 9.7 %collective-permute-start.13 = (bf16[1024,128]{1,0:T(8,128)(2,1)}, bf16[1024,128]{1,0:T(8,128)(2,1)S(1)}, u32[]{:S(2)}, u32[]{:S(2)}) collective-permute-start(bf16[1024,128]{1,0:T(8,128)(2,1)} %get-tuple-element.48), channel_id=1, source_target_pairs={{14,0},{3,1},{0,2},{5,3},{2,4},{7,5},{4,6},{9,7},{6,8},{11,9},{8,1... | collective-permute-start | bytes 786440 | tf_op jit(solution)/shard_map/ppermute | solution.py:65
  135.8 9.7 %collective-permute-start.14 = (bf16[1024,128]{1,0:T(8,128)(2,1)}, bf16[1024,128]{1,0:T(8,128)(2,1)S(1)}, u32[]{:S(2)}, u32[]{:S(2)}) collective-permute-start(bf16[1024,128]{1,0:T(8,128)(2,1)} %get-tuple-element.48), channel_id=1, source_target_pairs={{1,0},{0,1},{3,2},{2,3},{5,4},{4,5},{7,6},{6,7},{9,8},{8,9},{11,10... | collective-permute-start | bytes 786440 | tf_op jit(solution)/shard_map/ppermute | solution.py:65
  168.6 46.4 %collective-permute-start.23 = (bf16[32,128,128]{2,1,0:T(8,128)(2,1)}, bf16[32,128,128]{2,1,0:T(8,128)(2,1)S(1)}, u32[]{:S(2)}, u32[]{:S(2)}) collective-permute-start(bf16[32,128,128]{2,1,0:T(8,128)(2,1)} %get-tuple-element.57), channel_id=1, source_target_pairs={{0,14},{1,3},{2,0},{3,5},{4,2},{5,7},{6,4},{7,9},{8,6},{9,11},{10,... | collective-permute-start | bytes 3145736 | tf_op jit(solution)/shard_map/ppermute | solution.py:65
  171.4 43.6 %collective-permute-start.24 = (bf16[32,128,128]{2,1,0:T(8,128)(2,1)}, bf16[32,128,128]{2,1,0:T(8,128)(2,1)S(1)}, u32[]{:S(2)}, u32[]{:S(2)}) collective-permute-start(bf16[32,128,128]{2,1,0:T(8,128)(2,1)} %get-tuple-element.58), channel_id=1, source_target_pairs={{1,0},{0,1},{3,2},{2,3},{5,4},{4,5},{7,6},{6,7},{9,8},{8,9},{11,10... | collective-permute-start | bytes 3145736 | tf_op jit(solution)/shard_map/ppermute | solution.py:65
  174.1 41.0 %collective-permute-start.22 = (bf16[32,128,128]{2,1,0:T(8,128)(2,1)}, bf16[32,128,128]{2,1,0:T(8,128)(2,1)S(1)}, u32[]{:S(2)}, u32[]{:S(2)}) collective-permute-start(bf16[32,128,128]{2,1,0:T(8,128)(2,1)} %add_convert_fusion), channel_id=1, source_target_pairs={{0,2},{1,15},{2,4},{3,1},{4,6},{5,3},{6,8},{7,5},{8,10},{9,7},{10,... | collective-permute-start | bytes 3145736 | tf_op jit(solution)/shard_map/ppermute | solution.py:65
  175.2 69.2 %collective-permute-start.16 = (f32[196,128]{1,0:T(8,128)S(1)}, f32[196,128]{1,0:T(8,128)S(1)}, u32[]{:S(2)}, u32[]{:S(2)}) collective-permute-start(f32[196,128]{1,0:T(8,128)S(1)} %fusion.3), channel_id=1, source_target_pairs={{1,0},{0,1},{3,2},{2,3},{5,4},{4,5},{7,6},{6,7},{9,8},{8,9},{11,10... | collective-permute-start | bytes 301064 | tf_op jit(solution)/shard_map/ppermute | solution.py:65
  242.8 8.9 %collective-permute-start.25 = (f32[208,128]{1,0:T(8,128)S(1)}, f32[208,128]{1,0:T(8,128)S(1)}, u32[]{:S(2)}, u32[]{:S(2)}) collective-permute-start(f32[208,128]{1,0:T(8,128)S(1)} %fusion), channel_id=1, source_target_pairs={{1,0},{0,1},{3,2},{2,3},{5,4},{4,5},{7,6},{6,7},{9,8},{8,9},{11,10... | collective-permute-start | bytes 319496 | tf_op jit(solution)/shard_map/ppermute | solution.py:65
  244.4 4.9 %collective-permute-start.17 = (f32[196,128]{1,0:T(8,128)S(1)}, f32[196,128]{1,0:T(8,128)S(1)}, u32[]{:S(2)}, u32[]{:S(2)}) collective-permute-start(f32[196,128]{1,0:T(8,128)S(1)} %fusion.5), channel_id=1, source_target_pairs={{0,2},{1,3},{2,0},{3,1},{4,6},{5,7},{6,4},{7,5},{8,10},{9,11},{10,... | collective-permute-start | bytes 301064 | tf_op jit(solution)/shard_map/ppermute | solution.py:65
  249.3 5.1 %collective-permute-start.18 = (f32[196,128]{1,0:T(8,128)S(1)}, f32[196,128]{1,0:T(8,128)S(1)}, u32[]{:S(2)}, u32[]{:S(2)}) collective-permute-start(f32[196,128]{1,0:T(8,128)S(1)} %add.88), channel_id=1, source_target_pairs={{0,4},{1,5},{2,6},{3,7},{4,0},{5,1},{6,2},{7,3},{8,12},{9,13},{10,... | collective-permute-start | bytes 301064 | tf_op jit(solution)/shard_map/ppermute | solution.py:65
  252.6 5.0 %collective-permute-start.26 = (f32[208,128]{1,0:T(8,128)S(1)}, f32[208,128]{1,0:T(8,128)S(1)}, u32[]{:S(2)}, u32[]{:S(2)}) collective-permute-start(f32[208,128]{1,0:T(8,128)S(1)} %fusion.2), channel_id=1, source_target_pairs={{0,2},{1,3},{2,0},{3,1},{4,6},{5,7},{6,4},{7,5},{8,10},{9,11},{10,... | collective-permute-start | bytes 319496 | tf_op jit(solution)/shard_map/ppermute | solution.py:65
  254.4 6.3 %collective-permute-start.19 = (f32[196,128]{1,0:T(8,128)S(1)}, f32[196,128]{1,0:T(8,128)S(1)}, u32[]{:S(2)}, u32[]{:S(2)}) collective-permute-start(f32[196,128]{1,0:T(8,128)S(1)} %add.89), channel_id=1, source_target_pairs={{0,8},{1,9},{2,10},{3,11},{4,12},{5,13},{6,14},{7,15},{8,0},{9,1},... | collective-permute-start | bytes 301064 | tf_op jit(solution)/shard_map/ppermute | solution.py:65
  257.7 4.8 %collective-permute-start.27 = (f32[208,128]{1,0:T(8,128)S(1)}, f32[208,128]{1,0:T(8,128)S(1)}, u32[]{:S(2)}, u32[]{:S(2)}) collective-permute-start(f32[208,128]{1,0:T(8,128)S(1)} %add.95), channel_id=1, source_target_pairs={{0,4},{1,5},{2,6},{3,7},{4,0},{5,1},{6,2},{7,3},{8,12},{9,13},{10,... | collective-permute-start | bytes 319496 | tf_op jit(solution)/shard_map/ppermute | solution.py:65
  260.7 4.2 %collective-permute-start.20 = (f32[196,128]{1,0:T(8,128)S(1)}, f32[196,128]{1,0:T(8,128)S(1)}, u32[]{:S(2)}, u32[]{:S(2)}) collective-permute-start(f32[196,128]{1,0:T(8,128)S(1)} %add.90), channel_id=1, source_target_pairs={{1,0},{0,1},{3,2},{2,3},{5,4},{4,5},{7,6},{6,7},{9,8},{8,9},{11,10... | collective-permute-start | bytes 301064 | tf_op jit(solution)/shard_map/ppermute | solution.py:65
  262.4 7.8 %collective-permute-start.28 = (f32[208,128]{1,0:T(8,128)S(1)}, f32[208,128]{1,0:T(8,128)S(1)}, u32[]{:S(2)}, u32[]{:S(2)}) collective-permute-start(f32[208,128]{1,0:T(8,128)S(1)} %add.96), channel_id=1, source_target_pairs={{0,8},{1,9},{2,10},{3,11},{4,12},{5,13},{6,14},{7,15},{8,0},{9,1},... | collective-permute-start | bytes 319496 | tf_op jit(solution)/shard_map/ppermute | solution.py:65
  (28 other events, 81.5 us)

commit v3 on v1

v3 whole, which is shorter than its diff:
```python
import math

import jax
import jax.numpy as jnp
from jax import lax
from jax.experimental import pallas as pl
from jax.experimental.pallas import tpu as pltpu
from jax.sharding import PartitionSpec as P

loss_divisor = 64.0
F32 = jnp.float32
BF16 = jnp.bfloat16
VMEM_LIMIT = 56 * 1024 * 1024
PACK_ROWS = 16
GROUP = 8

PIECES = 5


def vmem():
    return pl.BlockSpec(memory_space=pltpu.VMEM)


def smem():
    return pl.BlockSpec(memory_space=pltpu.SMEM)


def in_hbm():
    return pl.BlockSpec(memory_space=pl.ANY)


def params():
    return pltpu.CompilerParams(vmem_limit_bytes=VMEM_LIMIT)


def cost(microseconds):
    return pl.CostEstimate(flops=0, transcendentals=0, bytes_accessed=int(microseconds * 3.6e6))


def dot_nn(left, right):
    return lax.dot_general(left, right, (((1,), (0,)), ((), ())), preferred_element_type=F32)


def dot_tn(left, right):
    return lax.dot_general(left, right, (((0,), (0,)), ((), ())), preferred_element_type=F32)


def dot_nt(left, right):
    return lax.dot_general(left, right, (((1,), (1,)), ((), ())), preferred_element_type=F32)


def second(p):
    return (p >> 1) & 1


def pair_links(count):
    return [(p, p ^ 2) for p in range(count)]


def cross_links(count):
    return [(p, (p + (2 if second(p) else -2)) % count) for p in range(count)]


def relay_links(count):
    return [(p, (p + (-4 if second(p) else 4)) % count) for p in range(count)]


def core_links(count):
    return [(p, p ^ 1) for p in range(count)]


def extra_links(count, from_pair):
    return [(p ^ 1, p) for p in range(count) if ((p & 1) != second(p)) == from_pair]


def turned(links):
    return [(target, source) for source, target in links]


def place_table():
    rows = []
    for kind in range(4):
        odd, on_second = kind & 1, kind >> 1
        pair, core = (-2 if on_second else 2), (-1 if odd else 1)
        offsets = [0, pair, -pair, core, -core]
        rows.append(
            [odd, on_second]
            + [offsets.index(part - 2) for part in range(PIECES)]
            + [2 - offset for offset in offsets]
            + [0] * 4
        )
    return jnp.array(rows, jnp.int32)


def send(value, links):
    return lax.ppermute(value, "phi", links)


def after(value, *earlier):
    return lax.optimization_barrier((value, *earlier))[0]


def gather_small(value, meanwhile=None):
    count = lax.axis_size("phi")
    pair = send(value, pair_links(count))
    cross = send(value, cross_links(count))
    other = send(value, core_links(count))
    if meanwhile is not None:
        pair = after(pair, meanwhile)
    extra_p = send(pair, extra_links(count, True))
    extra_c = send(cross, extra_links(count, False))
    return (value, pair, cross, other, extra_p, extra_c)


def join_extra(pair, cross, received, sends_pair):
    to_pair = jnp.where(sends_pair, received, jnp.zeros_like(received))
    to_cross = jnp.where(sends_pair, jnp.zeros_like(received), received)
    pair = (pair.astype(F32) + to_pair.astype(F32)).astype(BF16)
    cross = (cross.astype(F32) + to_cross.astype(F32)).astype(BF16)
    return pair, cross


def return_small(pair, cross, other, extra, sends_pair):
    count = lax.axis_size("phi")
    received = send(extra, core_links(count))
    from_other = send(other, core_links(count))
    pair, cross = join_extra(pair, cross, received, sends_pair)
    from_pair = send(pair, pair_links(count))
    from_cross = send(cross, turned(cross_links(count)))
    return (from_pair, from_cross, from_other), (pair, cross)


def first_sums(kept, given):
    count = lax.axis_size("phi")
    part = kept + send(given, core_links(count))
    if count & (count - 1) == 0:
        part = part + send(part, pair_links(count))
    return part


def last_sums(part):
    count = lax.axis_size("phi")
    if count & (count - 1):
        moved = part
        for _ in range(count // 2 - 1):
            moved = send(moved, [(p, (p + 2) % count) for p in range(count)])
            part = part + moved
    else:
        step = 4
        while step < count:
            part = part + send(part, [(p, p ^ step) for p in range(count)])
            step *= 2
    return part, send(part, core_links(count))


def fetch_tiles(tiles_hbm, tiles, sems, groups):
    for g in range(groups):
        pltpu.make_async_copy(
            tiles_hbm.at[pl.ds(g * GROUP, GROUP)], tiles.at[pl.ds(g * GROUP, GROUP)], sems.at[g]
        ).start()


def await_tiles(tiles_hbm, tiles, sems, g):
    first = pl.multiple_of(g * GROUP, GROUP)
    pltpu.make_async_copy(
        tiles_hbm.at[pl.ds(first, GROUP)], tiles.at[pl.ds(first, GROUP)], sems.at[g]
    ).wait()


def encode_operand(*pack_refs):
    rows = sum(pack_ref[...] for pack_ref in pack_refs)
    ids = rows.astype(F32)[12:13, :]
    layers = lax.broadcasted_iota(jnp.int32, rows.shape, 0).astype(F32)
    onehot = (layers == ids).astype(BF16)
    return jnp.concatenate([rows, onehot], axis=0)


def block_of(place, src, live, b, s, blocks):
    bits = blocks.bit_length() - 1
    named = src[b, s]
    block = (place[2 + (named >> bits)] << bits) + (named & (blocks - 1))
    return jnp.where(s < live[b], block, PIECES * blocks)


def forward_group(layer, g, place, src, live, tiles, window, w_self, w_agg, w_out, agg_ref, hidden_t_ref, new_ref):
    blocks, slots = tiles.shape[0], tiles.shape[1]
    sums = []
    for q in range(GROUP):
        b = g * GROUP + q
        left = jnp.concatenate([tiles[b, s] for s in range(slots)], axis=1)
        right = [window[block_of(place, src, live, b, s, blocks)] for s in range(slots)]
        sums.append(dot_nn(left, jnp.concatenate(right, axis=0)))
    first = pl.multiple_of(g * GROUP, GROUP)
    agg = jnp.concatenate(sums, axis=0).astype(BF16)
    rows, width = agg.shape
    here = window[pl.ds(first, GROUP)].reshape(rows, width)
    activation = dot_nn(here, w_self[layer]) + dot_nn(agg, w_agg[layer])
    hidden = jnp.maximum(activation, 0.0)
    hidden_b = hidden.astype(BF16)
    updated = (here.astype(F32) + dot_nn(hidden_b, w_out[layer])).astype(BF16)
    agg_ref[pl.ds(first, GROUP)] = agg.reshape(GROUP, rows // GROUP, width)
    new_ref[pl.ds(first, GROUP)] = updated.reshape(GROUP, rows // GROUP, width)
    for q in range(GROUP):
        block = hidden[q * (rows // GROUP) : (q + 1) * (rows // GROUP)]
        hidden_t_ref[first + q] = block.T.astype(BF16)


def input_weights(w_enc, layer_table):
    feats, width = w_enc.shape
    gap = jnp.zeros((PACK_ROWS - feats, width), F32)
    return jnp.concatenate([w_enc[...].astype(F32), gap, layer_table[...].astype(F32)], axis=0).astype(BF16)


def first_layer_kernel(
    place, src, live, tiles_hbm, p0, p1, p2, p3, p4, p5, w_enc, layer_table, w_self, w_agg, w_out,
    own_ref, agg_ref, hidden_t_ref, new_ref, new_a_ref, new_b_ref, tiles, window, sems,
):
    blocks, block_rows = tiles.shape[0], tiles.shape[2]
    groups = blocks // GROUP
    fetch_tiles(tiles_hbm, tiles, sems, groups)
    w_in = input_weights(w_enc, layer_table)
    for k, pack in enumerate(((p0,), (p1,), (p2,), (p3,), (p4, p5))):
        latents = jnp.tanh(dot_tn(encode_operand(*pack), w_in)).astype(BF16)
        window[pl.ds(k * blocks, blocks)] = latents.reshape(blocks, block_rows, latents.shape[1])
    window[PIECES * blocks] = jnp.zeros(window.shape[1:], BF16)
    own_ref[...] = window[pl.ds(0, blocks)]

    def step(g, carry):
        await_tiles(tiles_hbm, tiles, sems, g)
        forward_group(0, g, place, src, live, tiles, window, w_self, w_agg, w_out, agg_ref, hidden_t_ref, new_ref)
        return carry

    lax.fori_loop(0, groups, step, 0)
    cut = new_a_ref.shape[0]
    new_a_ref[...] = new_ref[pl.ds(0, cut)]
    new_b_ref[...] = new_ref[pl.ds(cut, blocks - cut)]


def next_layer_kernel(
    place, src, live, tiles_hbm, own_a, own_b, pair_a, pair_b, cross_a, cross_b, other_a, other_b,
    extra_pa, extra_pb, extra_ca, extra_cb, w_self, w_agg, w_out,
    agg_ref, hidden_t_ref, new_ref, tiles, window, sems, piece_sems,
):
    blocks, cut = tiles.shape[0], own_a.shape[0]
    groups = blocks // GROUP

    def copies(pieces, first):
        for k, (head, tail) in enumerate(pieces):
            start = (first + k) * blocks
            yield pltpu.make_async_copy(
                head, window.at[pl.ds(start, cut)], piece_sems.at[2 * (first + k)]
            )
            yield pltpu.make_async_copy(
                tail, window.at[pl.ds(start + cut, blocks - cut)], piece_sems.at[2 * (first + k) + 1]
            )

    plain = list(copies([(own_a, own_b), (pair_a, pair_b), (cross_a, cross_b), (other_a, other_b)], 0))
    for copy in plain:
        copy.start()

    def extra_is_pair(do):
        @pl.when(place[0] != place[1])
        def _():
            for copy in copies([(extra_pa, extra_pb)], 4):
                do(copy)

        @pl.when(place[0] == place[1])
        def _():
            for copy in copies([(extra_ca, extra_cb)], 4):
                do(copy)

    extra_is_pair(lambda copy: copy.start())
    fetch_tiles(tiles_hbm, tiles, sems, groups)
    window[PIECES * blocks] = jnp.zeros(window.shape[1:], BF16)
    for copy in plain:
        copy.wait()
    extra_is_pair(lambda copy: copy.wait())

    def step(g, carry):
        await_tiles(tiles_hbm, tiles, sems, g)
        forward_group(1, g, place, src, live, tiles, window, w_self, w_agg, w_out, agg_ref, hidden_t_ref, new_ref)
        return carry

    lax.fori_loop(0, groups, step, 0)


def pair_of_lists(lists, counts, k, triplets):
    longest = jnp.maximum(counts[2 * k], counts[2 * k + 1])
    return 2 * k * triplets, (2 * k + 1) * triplets, (longest + 7) >> 3


def gather_kernel(row_bits, lists, counts, latents, d0, d1, d2, d3, d4, wide, negative, positive):
    low = (1 << row_bits) - 1
    triplets = d0.shape[0]
    blocks, block_rows, width = latents.shape
    wide[...] = latents[...].reshape(blocks * block_rows, width).astype(F32)
    negative[...] = jnp.zeros(negative.shape, F32)
    positive[...] = jnp.zeros(positive.shape, F32)
    for k, out in enumerate((d0, d1, d2, d3, d4)):
        first_p, first_n, eights = pair_of_lists(lists, counts, k, triplets)

        def pick(i, carry, first_p=first_p, first_n=first_n):
            for u in range(8):
                code_n = lists[first_n + i * 8 + u]
                code_p = lists[first_p + i * 8 + u]
                negative[pl.ds(code_n >> row_bits, 1), :] = wide[pl.ds(code_n & low, 1), :]
                positive[pl.ds(code_p >> row_bits, 1), :] = wide[pl.ds(code_p & low, 1), :]
            return carry

        lax.fori_loop(0, eights, pick, 0)
        here = pl.ds(k * triplets, triplets)
        out[...] = (negative[here, :] - positive[here, :]).astype(BF16)


def anchor_kernel(anchors, latents, anchor_ref, wide):
    blocks, block_rows, width = latents.shape
    wide[...] = latents[...].reshape(blocks * block_rows, width).astype(F32)

    def pick(i, carry):
        for u in range(8):
            anchor_ref[pl.ds(i * 8 + u, 1), :] = wide[pl.ds(anchors[i * 8 + u], 1), :]
        return carry

    lax.fori_loop(0, anchor_ref.shape[0] // 8, pick, 0)


def own_rows_kernel(row_bits, lists, counts, anchors, weighted, anchor_grad, rows_ref, rows_b, rows_c, rows_d):
    low = (1 << row_bits) - 1
    triplets = anchor_grad.shape[0]
    held = (rows_ref, rows_b, rows_c, rows_d)
    for rows in held:
        rows[...] = jnp.zeros(rows.shape, F32)

    def put_anchor(i, carry):
        for u in range(8):
            here = pl.ds(anchors[i * 8 + u], 1)
            held[u % 4][here, :] += anchor_grad[pl.ds(i * 8 + u, 1), :]
        return carry

    lax.fori_loop(0, triplets // 8, put_anchor, 0)
    first_p, first_n, eights = pair_of_lists(lists, counts, 0, triplets)

    def put(i, carry):
        for u in range(8):
            code_n = lists[first_n + i * 8 + u]
            code_p = lists[first_p + i * 8 + u]
            from_n = pl.ds(jnp.minimum(code_n >> row_bits, triplets), 1)
            from_p = pl.ds(jnp.minimum(code_p >> row_bits, triplets), 1)
            held[u % 2][pl.ds(code_n & low, 1), :] += weighted[from_n, :]
            held[2 + u % 2][pl.ds(code_p & low, 1), :] -= weighted[from_p, :]
        return carry

    lax.fori_loop(0, eights, put, 0)
    rows_ref[...] = (rows_ref[...] + rows_b[...]) + (rows_c[...] + rows_d[...])


def score_kernel(own, pair, cross, other, anchors, loss_ref, weighted_ref, weighted_b_ref, anchor_grad_ref):
    triplets, width = anchors.shape
    inv_root = 1.0 / math.sqrt(width)
    scale = 1.0 / (loss_divisor * math.sqrt(width))
    chunk = 128
    loss = jnp.zeros((chunk, 1), F32)
    weighted_ref[pl.ds(triplets, 8), :] = jnp.zeros((8, width), F32)
    for c in range(triplets // chunk):
        here = pl.ds(c * chunk, chunk)
        gap = own[here, :].astype(F32) + pair[here, :].astype(F32)
        gap = gap + cross[here, :].astype(F32) + other[here, :].astype(F32)
        anchor = anchors[here, :]
        score = jnp.sum(anchor * gap, axis=1, keepdims=True) * inv_root
        loss = loss + jnp.maximum(score, 0.0) + jnp.log1p(jnp.exp(-jnp.abs(score)))
        coef = scale / (1.0 + jnp.exp(-score))
        weighted = coef * anchor
        weighted_ref[here, :] = weighted
        weighted_b_ref[here, :] = weighted.astype(BF16)
        anchor_grad_ref[here, :] = coef * gap
    loss_ref[...] = jnp.broadcast_to(jnp.sum(loss, axis=0, keepdims=True), loss_ref.shape)


def backward_group(layer, g, place, src, live, tiles, gradient, hidden_t, latents, agg, w_self, w_agg, w_out, grads, spread):
    blocks, slots = tiles.shape[0], tiles.shape[1]
    first = pl.multiple_of(g * GROUP, GROUP)
    rows, width = tiles.shape[2], latents.shape[2]
    upstream = gradient.astype(BF16)
    hidden = jnp.concatenate([hidden_t[first + q] for q in range(GROUP)], axis=1)
    grads[2] += dot_nt(hidden, upstream)
    hidden_grad = dot_nn(w_out[layer], upstream)
    act_grad = jnp.where(hidden > 0, hidden_grad, 0.0).astype(BF16)
    grads[0] += dot_nn(act_grad, latents[pl.ds(first, GROUP)].reshape(GROUP * rows, width))
    grads[1] += dot_nn(act_grad, agg[pl.ds(first, GROUP)].reshape(GROUP * rows, width))
    agg_grad = dot_nn(w_agg[layer], act_grad).astype(BF16)
    direct = gradient + dot_nn(w_self[layer], act_grad)
    for q in range(GROUP):
        b = g * GROUP + q
        spread[b] += direct[:, q * rows : (q + 1) * rows]
        right = jnp.concatenate([tiles[b, s] for s in range(slots)], axis=1)
        parts = dot_nn(agg_grad[:, q * rows : (q + 1) * rows], right)
        for s in range(slots):
            spread[block_of(place, src, live, b, s, blocks)] += parts[:, s * rows : (s + 1) * rows]


def put_halves(place, whole, kept_ref, given_ref):
    half = kept_ref.shape[0]
    kept_ref[...] = whole[pl.ds(pl.multiple_of(place[0] * half, 8), half), :]
    given_ref[...] = whole[pl.ds(pl.multiple_of((1 - place[0]) * half, 8), half), :]


def put_grads(grads, whole):
    width = grads.shape[1]
    whole[pl.ds(0, width), :] = grads[0].T
    whole[pl.ds(width, width), :] = grads[1].T
    whole[pl.ds(2 * width, width), :] = grads[2]


def contrast_layer_kernel(
    row_bits, place, src, live, lists, counts, tiles_hbm,
    own_rows, e1, e2, e3, e4, e5, loss_part, hidden_t, latents, agg, w_self, w_agg, w_out,
    own_ref, pair_a_ref, pair_b_ref, cross_a_ref, cross_b_ref, other_ref, extra_a_ref, extra_b_ref,
    kept_ref, given_ref,
    tiles, spread, grads, whole, weighted, rows_a, rows_b, rows_c, rows_d, sems,
):
    low = (1 << row_bits) - 1
    blocks, block_rows = tiles.shape[0], tiles.shape[2]
    groups = blocks // GROUP
    triplets = e1.shape[0]
    fetch_tiles(tiles_hbm, tiles, sems, groups)
    held = (rows_a, rows_b, rows_c, rows_d)
    rows_a[...] = own_rows[...]
    for rows in held[1:]:
        rows[...] = jnp.zeros(rows.shape, F32)
    spread[...] = jnp.zeros(spread.shape, F32)
    grads[...] = jnp.zeros(grads.shape, F32)
    for k, piece in enumerate((e1, e2, e3)):
        weighted[pl.ds(k * triplets, triplets), :] = piece[...].astype(F32)
    weighted[pl.ds(3 * triplets, triplets), :] = e4[...].astype(F32) + e5[...].astype(F32)
    weighted[pl.ds(4 * triplets, 8), :] = jnp.zeros((8, weighted.shape[1]), F32)
    for k in range(1, PIECES):
        first_p, first_n, eights = pair_of_lists(lists, counts, k, triplets)

        def put(i, carry, first_p=first_p, first_n=first_n):
            for u in range(8):
                code_n = lists[first_n + i * 8 + u]
                code_p = lists[first_p + i * 8 + u]
                from_n = pl.ds((code_n >> row_bits) - triplets, 1)
                from_p = pl.ds((code_p >> row_bits) - triplets, 1)
                held_n, held_p = held[u % 2], held[2 + u % 2]
                held_n[pl.ds(code_n & low, 1), :] += weighted[from_n, :]
                held_p[pl.ds(code_p & low, 1), :] -= weighted[from_p, :]
            return carry

        lax.fori_loop(0, eights, put, 0)

    def step(g, carry):
        pieces = []
        for q in range(GROUP):
            here = pl.ds(pl.multiple_of((g * GROUP + q) * block_rows, block_rows), block_rows)
            block = (rows_a[here, :] + rows_b[here, :]) + (rows_c[here, :] + rows_d[here, :])
            pieces.append(block.T)
        await_tiles(tiles_hbm, tiles, sems, g)
        backward_group(1, g, place, src, live, tiles, jnp.concatenate(pieces, axis=1), hidden_t, latents, agg,
                       w_self, w_agg, w_out, grads, spread)
        return carry

    lax.fori_loop(0, groups, step, 0)
    cut = pair_a_ref.shape[0]
    own_ref[...] = spread[pl.ds(0, blocks)]
    for k, (head, tail) in enumerate(((pair_a_ref, pair_b_ref), (cross_a_ref, cross_b_ref))):
        head[...] = spread[pl.ds((k + 1) * blocks, cut)].astype(BF16)
        tail[...] = spread[pl.ds((k + 1) * blocks + cut, blocks - cut)].astype(BF16)
    other_ref[...] = spread[pl.ds(3 * blocks, blocks)].astype(BF16)
    extra_a_ref[...] = spread[pl.ds(4 * blocks, cut)].astype(BF16)
    extra_b_ref[...] = spread[pl.ds(4 * blocks + cut, blocks - cut)].astype(BF16)
    put_grads(grads, whole)
    top = 3 * grads.shape[1]
    whole[pl.ds(top, 8), :] = loss_part[...]
    whole[pl.ds(top + 8, 8), :] = jnp.zeros((8, whole.shape[1]), F32)
    put_halves(place, whole, kept_ref, given_ref)


def last_layer_kernel(
    place, src, live, tiles_hbm, own, pair_a, pair_b, cross_b, other, hidden_t, latents, agg,
    w_self, w_agg, w_out, w_enc, layer_table, p0, p1, p2, p3, p4, p5,
    kept_ref, given_ref, tiles, spread, grads, whole, received, sems,
):
    blocks = tiles.shape[0]
    groups = blocks // GROUP
    cut = pair_a.shape[0]
    fetch_tiles(tiles_hbm, tiles, sems, groups)
    spread[...] = jnp.zeros(spread.shape, F32)
    grads[...] = jnp.zeros(grads.shape, F32)
    head, tail = pl.ds(0, cut), pl.ds(cut, blocks - cut)
    received[head] = own[head] + other[head].astype(F32) + pair_a[...].astype(F32)
    from_far = pair_b[...].astype(F32) + cross_b[...].astype(F32)
    received[tail] = own[tail] + other[tail].astype(F32) + from_far

    def step(g, carry):
        pieces = [received[g * GROUP + q] for q in range(GROUP)]
        await_tiles(tiles_hbm, tiles, sems, g)
        backward_group(0, g, place, src, live, tiles, jnp.concatenate(pieces, axis=1), hidden_t, latents, agg,
                       w_self, w_agg, w_out, grads, spread)
        return carry

    lax.fori_loop(0, groups, step, 0)
    w_in = input_weights(w_enc, layer_table)
    grad_in = jnp.zeros(w_in.shape, F32)
    for k, pack in enumerate(((p0,), (p1,), (p2,), (p3,), (p4, p5))):
        operand = encode_operand(*pack)
        squashed = jnp.tanh(dot_tn(w_in, operand))
        gradient = jnp.concatenate([spread[k * blocks + q] for q in range(blocks)], axis=1)
        encoded_grad = (gradient * (1.0 - squashed * squashed)).astype(BF16)
        grad_in = grad_in + dot_nt(operand, encoded_grad)
    put_grads(grads, whole)
    whole[pl.ds(3 * grads.shape[1], 2 * PACK_ROWS), :] = grad_in
    put_halves(place, whole, kept_ref, given_ref)


def result_kernel(
    scale, feats, place, part_0, back_0, part_1, back_1,
    loss_ref, enc_ref, table_ref, self_ref, agg_ref, out_ref, whole_0, whole_1,
):
    for whole, part, back in ((whole_0, part_0, back_0), (whole_1, part_1, back_1)):
        half = part.shape[0]
        whole[pl.ds(pl.multiple_of(place[0] * half, 8), half), :] = part[...]
        whole[pl.ds(pl.multiple_of((1 - place[0]) * half, 8), half), :] = back[...]
    width = whole_0.shape[1]
    top = 3 * width
    for layer, whole in enumerate((whole_0, whole_1)):
        for k, out in enumerate((self_ref, agg_ref, out_ref)):
            out[layer] = whole[pl.ds(k * width, width), :]
    enc_ref[...] = whole_0[pl.ds(top, feats), :]
    table_ref[...] = whole_0[pl.ds(top + PACK_ROWS, PACK_ROWS), :]
    loss_ref[0] = jnp.max(whole_1[pl.ds(top, 8), :]) * scale


def body(
    hit_feats, layer_ids, edge_tiles, src_blocks, live_slots,
    anchor_hits, positive_hits, negative_hits, w_enc, layer_table, w_self, w_agg, w_out,
):
    blocks, slots, block_rows = edge_tiles.shape[0], edge_tiles.shape[1], edge_tiles.shape[2]
    feats, width = w_enc.shape
    kinds = layer_table.shape[0]
    hits = blocks * block_rows
    triplets = anchor_hits.shape[0]
    layers = w_self.shape[0]
    row_bits = hits.bit_length() - 1
    count = lax.axis_size("phi")
    assert hits == 1 << row_bits and blocks & (blocks - 1) == 0 and blocks % GROUP == 0
    assert feats < PACK_ROWS - 3 and kinds == PACK_ROWS and layers == 2 and 4 * triplets == hits
    assert count % 4 == 0
    groups = blocks // GROUP
    cut, back_cut = blocks // 2, blocks * 5 // 8
    place = lax.dynamic_slice_in_dim(place_table(), lax.axis_index("phi") & 3, 1, 0).reshape(-1)
    sends_pair = place[0] == place[1]

    codes = jnp.concatenate([positive_hits, negative_hits])
    codes = jnp.concatenate([codes >> 7, codes & 127])
    pack = jnp.concatenate(
        [
            hit_feats,
            layer_ids.astype(BF16)[None, :],
            codes.astype(BF16)[None, :],
            jnp.zeros((PACK_ROWS - feats - 2, hits), BF16),
        ]
    )
    packs = gather_small(pack)

    block_shape = (blocks, block_rows, width)
    tile_scratch = pltpu.VMEM(edge_tiles.shape, BF16)
    group_sems = pltpu.SemaphoreType.DMA((groups,))
    window_scratch = pltpu.VMEM((PIECES * blocks + 1, block_rows, width), BF16)
    blocked = jax.ShapeDtypeStruct(block_shape, BF16)
    head = jax.ShapeDtypeStruct((cut, block_rows, width), BF16)
    tail = jax.ShapeDtypeStruct((blocks - cut, block_rows, width), BF16)
    back_head = jax.ShapeDtypeStruct((back_cut, block_rows, width), BF16)
    back_tail = jax.ShapeDtypeStruct((blocks - back_cut, block_rows, width), BF16)
    slots_in = (place, src_blocks, live_slots)

    latents_0, agg_0, hidden_0, latents_1, new_a, new_b = pl.pallas_call(
        first_layer_kernel,
        out_shape=(blocked,) * 4 + (head, tail),
        in_specs=[smem()] * 3 + [in_hbm()] + [vmem()] * 11,
        out_specs=(vmem(),) * 6,
        scratch_shapes=[tile_scratch, window_scratch, group_sems],
        compiler_params=params(),
        name="first_layer",
    )(*slots_in, edge_tiles, *packs, w_enc, layer_table, w_self, w_agg, w_out)

    held_codes = jnp.stack([packs[1], packs[2], packs[3], packs[4] + packs[5]])[:, feats + 1]
    held_codes = after(held_codes, new_a).astype(jnp.int32).reshape(PIECES - 1, 2, 2 * triplets)
    own_codes = jnp.concatenate([positive_hits, negative_hits]).reshape(1, 2 * triplets)
    named = jnp.concatenate([own_codes, (held_codes[:, 0] << 7) + held_codes[:, 1]]).reshape(PIECES, 2, triplets)
    mine = (named >> row_bits) == place[7 : 7 + PIECES, None, None]
    numbers = jnp.arange(PIECES * triplets, dtype=jnp.int32).reshape(PIECES, 1, triplets)
    coded = jnp.where(mine, (numbers << row_bits) | (named & (hits - 1)), (PIECES * triplets) << row_bits)
    lists = lax.sort(coded.reshape(2 * PIECES, triplets).T, dimension=0, is_stable=False).T.reshape(-1)
    counts = jnp.sum(mine.astype(jnp.int32), axis=2).reshape(-1)

    pair_a = send(new_a, pair_links(count))
    late_b = after(new_b, lists, counts)
    pair_b = send(late_b, pair_links(count))
    cross_b = send(late_b, cross_links(count))
    other_a = send(new_a, core_links(count))
    other_b = send(new_b, core_links(count))
    pair_a = after(pair_a, lists, counts)
    cross_a = send(pair_a, relay_links(count))
    extra_pa = send(pair_a, extra_links(count, True))
    extra_pb = send(pair_b, extra_links(count, True))
    extra_cb = send(cross_b, extra_links(count, False))
    extra_ca = send(cross_a, extra_links(count, False))

    agg_1, hidden_1, latents_2 = pl.pallas_call(
        next_layer_kernel,
        out_shape=(blocked,) * 3,
        in_specs=[smem()] * 3 + [in_hbm()] * 13 + [vmem()] * 3,
        out_specs=(vmem(),) * 3,
        scratch_shapes=[
            tile_scratch, window_scratch, group_sems, pltpu.SemaphoreType.DMA((2 * PIECES,)),
        ],
        compiler_params=params(),
        name="next_layer",
    )(
        *slots_in, edge_tiles, new_a, new_b, pair_a, pair_b, cross_a, cross_b, other_a, other_b,
        extra_pa, extra_pb, extra_ca, extra_cb, w_self, w_agg, w_out,
    )

    triplet_rows = jax.ShapeDtypeStruct((triplets, width), BF16)
    wide_rows = jax.ShapeDtypeStruct((triplets, width), F32)
    hit_rows = pltpu.VMEM((hits, width), F32)
    gap_own, *gap_pieces = pl.pallas_call(
        lambda *refs: gather_kernel(row_bits, *refs),
        out_shape=(triplet_rows,) * 5,
        in_specs=[smem()] * 2 + [vmem()],
        out_specs=(vmem(),) * 5,
        scratch_shapes=[
            hit_rows,
            pltpu.VMEM((PIECES * triplets + 8, width), F32),
            pltpu.VMEM((PIECES * triplets + 8, width), F32),
        ],
        compiler_params=params(),
        name="gather_rows",
    )(lists, counts, latents_2)
    gaps, joined = return_small(*gap_pieces, sends_pair)

    anchor_rows = pl.pallas_call(
        anchor_kernel,
        out_shape=wide_rows,
        in_specs=[smem(), vmem()],
        out_specs=vmem(),
        scratch_shapes=[hit_rows],
        compiler_params=params(),
        name="anchor_rows",
    )(anchor_hits, after(latents_2, *joined))

    loss_part, weighted, weighted_b, anchor_grad = pl.pallas_call(
        score_kernel,
        out_shape=(
            jax.ShapeDtypeStruct((8, width), F32),
            jax.ShapeDtypeStruct((triplets + 8, width), F32),
            triplet_rows,
            wide_rows,
        ),
        in_specs=[vmem()] * 5,
        out_specs=(vmem(),) * 4,
        compiler_params=params(),
        name="scores",
    )(gap_own, *gaps, anchor_rows)

    own_rows = pl.pallas_call(
        lambda *refs: own_rows_kernel(row_bits, *refs),
        out_shape=jax.ShapeDtypeStruct((hits, width), F32),
        in_specs=[smem()] * 3 + [vmem()] * 2,
        out_specs=vmem(),
        scratch_shapes=[hit_rows] * 3,
        compiler_params=params(),
        name="own_rows",
    )(lists, counts, anchor_hits, weighted, anchor_grad)
    weighted_window = gather_small(weighted_b, own_rows)

    wide_blocked = jax.ShapeDtypeStruct(block_shape, F32)
    spread_scratch = pltpu.VMEM((PIECES * blocks + 1, width, block_rows), F32)
    grads_scratch = pltpu.VMEM((3, width, width), F32)
    rows_0, rows_1 = 3 * width + 2 * PACK_ROWS, 3 * width + 16
    half_0 = jax.ShapeDtypeStruct((rows_0 // 2, width), F32)
    half_1 = jax.ShapeDtypeStruct((rows_1 // 2, width), F32)
    own_1, ret_pa, ret_pb, ret_ca, ret_cb, ret_other, ret_ea, ret_eb, kept_1, given_1 = pl.pallas_call(
        lambda *refs: contrast_layer_kernel(row_bits, *refs),
        out_shape=(wide_blocked,)
        + (back_head, back_tail) * 2
        + (blocked, back_head, back_tail, half_1, half_1),
        in_specs=[smem()] * 5 + [in_hbm()] + [vmem()] * 13,
        out_specs=(vmem(),) * 10,
        scratch_shapes=[
            tile_scratch, spread_scratch, grads_scratch, pltpu.VMEM((rows_1, width), F32),
            pltpu.VMEM((4 * triplets + 8, width), F32), hit_rows, hit_rows, hit_rows, hit_rows, group_sems,
        ],
        compiler_params=params(),
        name="contrast_layer",
    )(
        *slots_in, lists, counts, edge_tiles,
        own_rows, *weighted_window[1:], loss_part,
        hidden_1, latents_1, agg_1, w_self, w_agg, w_out,
    )

    got_a = send(ret_ea, core_links(count))
    got_b = send(ret_eb, core_links(count))
    from_other = send(ret_other, core_links(count))
    ret_pa, ret_ca = join_extra(ret_pa, ret_ca, got_a, sends_pair)
    relayed = send(ret_ca, turned(relay_links(count)))
    ret_pb, ret_cb = join_extra(ret_pb, ret_cb, got_b, sends_pair)
    from_pair_b = send(ret_pb, pair_links(count))
    from_cross_b = send(ret_cb, turned(cross_links(count)))
    ret_pa = (ret_pa.astype(F32) + relayed.astype(F32)).astype(BF16)
    part_1 = first_sums(kept_1, given_1)
    from_pair_a = send(after(ret_pa, from_pair_b, from_cross_b, part_1), pair_links(count))
    part_1, back_1 = last_sums(part_1)
    own_1 = after(own_1, part_1, back_1)

    kept_0, given_0 = pl.pallas_call(
        last_layer_kernel,
        out_shape=(half_0, half_0),
        in_specs=[smem()] * 3 + [in_hbm()] + [vmem()] * 19,
        out_specs=(vmem(),) * 2,
        scratch_shapes=[
            tile_scratch, spread_scratch, grads_scratch, pltpu.VMEM((rows_0, width), F32),
            pltpu.VMEM(block_shape, F32), group_sems,
        ],
        compiler_params=params(),
        name="last_layer",
    )(
        *slots_in, edge_tiles, own_1, from_pair_a, from_pair_b, from_cross_b, from_other,
        hidden_0, latents_0, agg_0, w_self, w_agg, w_out, w_enc, layer_table, *packs,
    )
    part_0, back_0 = last_sums(first_sums(kept_0, given_0))

    square = jax.ShapeDtypeStruct((layers, width, width), F32)
    return pl.pallas_call(
        lambda *refs: result_kernel(1.0 / (triplets * count), feats, *refs),
        out_shape=(
            jax.ShapeDtypeStruct((1,), F32),
            jax.ShapeDtypeStruct((feats, width), F32),
            jax.ShapeDtypeStruct((PACK_ROWS, width), F32),
            square, square, square,
        ),
        in_specs=[smem()] + [vmem()] * 4,
        out_specs=(smem(),) + (vmem(),) * 5,
        scratch_shapes=[pltpu.VMEM((rows_0, width), F32), pltpu.VMEM((rows_1, width), F32)],
        compiler_params=params(),
        name="results",
    )(place, part_0, back_0, part_1, back_1)


def solution(mesh):
    both = ("event", "phi")
    in_specs = (
        P(None, both), P(both), P(both, None, None, None), P(both, None), P(both),
        P(both), P(both), P(both), P(), P(), P(), P(), P(),
    )
    out_specs = (
        P("event"), P("event", None), P("event", None),
        P("event", None, None), P("event", None, None), P("event", None, None),
    )
    return jax.shard_map(body, mesh=mesh, in_specs=in_specs, out_specs=out_specs, check_vma=False)
```

time: 316 us -> 241 us (0.76)
  Pallas kernels: 127 us -> 74.2 us
  waiting for transfers between devices: 114 us -> 101 us
  local copies, waits for them, and re-layouts: 17.3 us -> 10.6 us
  other arithmetic: 16.8 us -> 10.2 us
  starting transfers between devices: 37 us -> 41 us
    pallas_call x3 -> x5, Pallas kernels: 82.2 us -> 36.6 us  [the longest x1 15.2 us: body(): pl.pallas_call(last_layer_kernel, out_shape=(half_0, half_0), in_specs=[s...]
    ppermute x30 -> x41, waiting for transfers between devices: 114 us -> 101 us  [send(): return lax.ppermute(value, 'phi', links)]
    select_n x6 -> x0, other arithmetic: 6.56 us -> none  [the longest x1 3.94 us: body(): jnp.where(live, piece * blocks + src_blocks % blocks, PIECES * blocks)]
    slice x10 -> x1, local copies, waits for them, and re-layouts: 5.98 us -> 0.58 us  [body(): sends_pair = place[0] == place[1]]
    ppermute x30 -> x41, starting transfers between devices: 37 us -> 41 us  [send(): return lax.ppermute(value, 'phi', links)]
    sort x0 -> x1, other arithmetic: none -> 3.8 us  [body(): lax.sort(coded.reshape(2 * PIECES, triplets).T, dimension=0, is_stable=Fa...]
    pallas_call x1, Pallas kernels: 20.7 us -> 17.1 us  [body(): pl.pallas_call(lambda *refs: contrast_layer_kernel(row_bits, *refs), out_...]
    unnamed x48 -> x80, local copies, waits for them, and re-layouts: 6.79 us -> 6.38 us
  transfers between devices with their start and end apart: 30 -> 41, of which waited for: 12 -> 23; matrix products, arithmetic and copies ran while one was open for 7% -> 5% of each run, Pallas kernels for 20% -> 4%
where the time goes in v3:
time: 241 us; the launch traced here: 240 us
  waiting for transfers between devices  101 us (42%)
  Pallas kernels  74.2 us (31%)
  starting transfers between devices  41 us (17%)
  local copies, waits for them, and re-layouts  10.6 us (4%)
  other arithmetic  10.2 us (4%)
  between operations  2.8 us (1%)
    ppermute x41, waiting for transfers between devices, send(): return lax.ppermute(value, 'phi', links)  101 us
    ppermute x41, starting transfers between devices, send(): return lax.ppermute(value, 'phi', links)  41 us
    pallas_call x1, Pallas kernels, body(): pl.pallas_call(lambda *refs: contrast_layer_kernel(row_bits, *refs), out_...  17.1 us
    pallas_call x1, Pallas kernels, body(): pl.pallas_call(last_layer_kernel, out_shape=(half_0, half_0), in_specs=[s...  15.2 us
    pallas_call x1, Pallas kernels, body(): pl.pallas_call(next_layer_kernel, out_shape=(blocked,) * 3, in_specs=[sme...  10.4 us
    pallas_call x1, Pallas kernels, body(): pl.pallas_call(first_layer_kernel, out_shape=(blocked,) * 4 + (head, tail...  9.5 us
    pallas_call x1, Pallas kernels, body(): pl.pallas_call(lambda *refs: gather_kernel(row_bits, *refs), out_shape=(t...  7.08 us
    pallas_call x1, Pallas kernels, body(): pl.pallas_call(lambda *refs: own_rows_kernel(row_bits, *refs), out_shape=...  6.45 us
  transfers between devices with their start and end apart: 41, of which 23 were waited for; matrix products, arithmetic and copies ran while one was open for 5% of the time, Pallas kernels for 4%

profile of v3, /device:TPU:0, one launch (start us, length us, event | category | flops | bytes accessed | tf_op | source)
XLA Modules:
  0.0 239.8 jit_solution(8868036826882773814)
XLA Ops:
  4.4 5.6 %collective-permute-start.1 = (bf16[16,4096]{1,0:T(8,128)(2,1)S(1)}, bf16[16,4096]{1,0:T(8,128)(2,1)S(1)}, u32[]{:S(2)}, u32[]{:S(2)}) collective-permute-start(bf16[16,4096]{1,0:T(8,128)(2,1)S(1)} %maximum_maximum_fusion.p0), channel_id=1, source_target_pairs={{0,14},{1,15},{2,4},{3,5},{4,2},{5,3},{6,8},{7,9},{8,6},{9,7},{10,... | collective-permute-start | bytes 393224 | tf_op jit(solution)/shard_map/ppermute | solution.py:96
  21.2 9.5 %first_layer.1 = (bf16[32,128,128]{2,1,0:T(8,128)(2,1)}, bf16[32,128,128]{2,1,0:T(8,128)(2,1)}, bf16[32,128,128]{2,1,0:T(8,128)(2,1)}, bf16[32,128,128]{2,1,0:T(...) custom-call(s32[16]{0:T(128)} %get-tuple-element.90.place.refs_0_, s32[32,8]{1,0:T(8,128)} %copy.27.src.refs_1_, ...), custom_call_target="tpu_custom_call" | custom-call | tf_op jit(solution)/shard_map/first_layer/pallas_call | solution.py:577
  32.0 3.8 %sort.7 = s32[1024,10]{0,1:T(8,128)S(1)} sort(s32[1024,10]{0,1:T(8,128)S(1)} %select_bitcast_fusion), dimensions={0}, to_apply=%region_0.1 | sort | flops 143360 | bytes 81920 | tf_op jit(solution)/shard_map/sort | solution.py:594
  36.5 3.2 %collective-permute-start.8 = (bf16[16,128,128]{2,1,0:T(8,128)(2,1)}, bf16[16,128,128]{2,1,0:T(8,128)(2,1)S(1)}, u32[]{:S(2)}, u32[]{:S(2)}) collective-permute-start(bf16[16,128,128]{2,1,0:T(8,128)(2,1)} %get-tuple-element.47.own_b), channel_id=1, source_target_pairs={{0,14},{1,15},{2,4},{3,5},{4,2},{5,3},{6,8},{7,9},{8,6},{9,7},{10,... | collective-permute-start | bytes 1572872 | tf_op jit(solution)/shard_map/ppermute | solution.py:96
  39.9 17.1 %collective-permute-done.5.pair_a = bf16[16,128,128]{2,1,0:T(8,128)(2,1)S(1)} collective-permute-done((bf16[16,128,128]{2,1,0:T(8,128)(2,1)}, bf16[16,128,128]{2,1,0:T(8,128)(2,1)S(1)}, u32[]{:S(2)}, u32[]{:S(2)}) %collective-permute-start.5) | collective-permute-done | bytes 524320 | tf_op jit(solution)/shard_map/ppermute | solution.py:96
  59.5 7.5 %collective-permute-done.6.pair_b = bf16[16,128,128]{2,1,0:T(8,128)(2,1)S(1)} collective-permute-done((bf16[16,128,128]{2,1,0:T(8,128)(2,1)}, bf16[16,128,128]{2,1,0:T(8,128)(2,1)S(1)}, u32[]{:S(2)}, u32[]{:S(2)}) %collective-permute-start.6) | collective-permute-done | bytes 524320 | tf_op jit(solution)/shard_map/ppermute | solution.py:96
  76.1 10.4 %next_layer.1 = (bf16[32,128,128]{2,1,0:T(8,128)(2,1)}, bf16[32,128,128]{2,1,0:T(8,128)(2,1)}, bf16[32,128,128]{2,1,0:T(8,128)(2,1)}) custom-call(s32[16]{0:T(128)} %get-tuple-element.90.place.refs_0_, s32[32,8]{1,0:T(8,128)} %copy.27.src.refs_1_, s32[32]{0:T(128)} %live.5, bf16[32,8,128,128]{3,2,1,0:T(8,128)(2,1)} %tiles_hbm.5, ...), custom_call_target="tpu_custom_call" | custom-call | tf_op jit(solution)/shard_map/next_layer/pallas_call | solution.py:610
  86.5 7.1 %gather_rows.1 = (bf16[1024,128]{1,0:T(8,128)(2,1)}, bf16[1024,128]{1,0:T(8,128)(2,1)}, bf16[1024,128]{1,0:T(8,128)(2,1)}, bf16[1024,128]{1,0:T(8,128)(2,1)}, bf16[1024,128]{1,0:T(8,128)(2,1)}) custom-call(s32[10240]{0:T(1024)} %reshape.137.refs_0_.refs_3_, s32[10]{0:T(128)} %reshape.138.refs_1_.refs_4_, bf16[32,128,128]{2,1,0:T(8,128)(2,1)} %get-tuple-element.54.refs_2_.latents), custom_call_target="tpu_custom_call" | custom-call | tf_op jit(solution)/shard_map/gather_rows/pallas_call | solution.py:628
  97.2 3.6 %collective-permute-start.17 = (bf16[1024,128]{1,0:T(8,128)(2,1)S(1)}, bf16[1024,128]{1,0:T(8,128)(2,1)S(1)}, u32[]{:S(2)}, u32[]{:S(2)}) collective-permute-start(bf16[1024,128]{1,0:T(8,128)(2,1)S(1)} %get-tuple-element.82), channel_id=1, source_target_pairs={{14,0},{15,1},{4,2},{5,3},{2,4},{3,5},{8,6},{9,7},{6,8},{7,9},{12,... | collective-permute-start | bytes 786440 | tf_op jit(solution)/shard_map/ppermute | solution.py:96
  100.8 3.6 %anchor_rows.1.anchors = f32[1024,128]{1,0:T(8,128)} custom-call(s32[1024]{0:T(1024)} %refs_2_.2, bf16[32,128,128]{2,1,0:T(8,128)(2,1)} %get-tuple-element.54.refs_2_.latents), custom_call_target="tpu_custom_call" | custom-call | tf_op jit(solution)/shard_map/anchor_rows/pallas_call | solution.py:643
  104.4 3.9 %collective-permute-done.17.cross = bf16[1024,128]{1,0:T(8,128)(2,1)S(1)} collective-permute-done((bf16[1024,128]{1,0:T(8,128)(2,1)S(1)}, bf16[1024,128]{1,0:T(8,128)(2,1)S(1)}, u32[]{:S(2)}, u32[]{:S(2)}) %collective-permute-start.17) | collective-permute-done | bytes 262176 | tf_op jit(solution)/shard_map/ppermute | solution.py:96
  108.3 5.5 %collective-permute-done.16.pair = bf16[1024,128]{1,0:T(8,128)(2,1)S(1)} collective-permute-done((bf16[1024,128]{1,0:T(8,128)(2,1)S(1)}, bf16[1024,128]{1,0:T(8,128)(2,1)S(1)}, u32[]{:S(2)}, u32[]{:S(2)}) %collective-permute-start.16) | collective-permute-done | bytes 262176 | tf_op jit(solution)/shard_map/ppermute | solution.py:96
  119.8 6.4 %own_rows.1.refs_6_ = f32[4096,128]{1,0:T(8,128)} custom-call(s32[10240]{0:T(1024)} %reshape.137.refs_0_.refs_3_, s32[10]{0:T(128)} %reshape.138.refs_1_.refs_4_, s32[1024]{0:T(1024)} %refs_2_.2, f32[1032,128]{1,0:T(8,128)} %get-tuple-element.55.refs_3_, f32[1024,128]{1,0:T(8,128)} %get-tuple-element.56.refs_4_), custom_call_target="tpu_custom_call" | custom-call | tf_op jit(solution)/shard_map/own_rows/pallas_call | solution.py:667
  126.3 5.4 %collective-permute-done.19.refs_7_ = bf16[1024,128]{1,0:T(8,128)(2,1)S(1)} collective-permute-done((bf16[1024,128]{1,0:T(8,128)(2,1)}, bf16[1024,128]{1,0:T(8,128)(2,1)S(1)}, u32[]{:S(2)}, u32[]{:S(2)}) %collective-permute-start.19) | collective-permute-done | bytes 262176 | tf_op jit(solution)/shard_map/ppermute | solution.py:96
  133.0 3.2 %collective-permute-start.22 = (bf16[1024,128]{1,0:T(8,128)(2,1)S(1)}, bf16[1024,128]{1,0:T(8,128)(2,1)S(1)}, u32[]{:S(2)}, u32[]{:S(2)}) collective-permute-start(bf16[1024,128]{1,0:T(8,128)(2,1)S(1)} %collective-permute-done.19.refs_7_), channel_id=1, source_target_pairs={{0,1},{3,2},{4,5},{7,6},{8,9},{11,10},{12,13},{15,14},{16,17},{19,... | collective-permute-start | bytes 786440 | tf_op jit(solution)/shard_map/ppermute | solution.py:96
  137.8 17.1 %contrast_layer.1 = (f32[32,128,128]{2,1,0:T(8,128)}, bf16[20,128,128]{2,1,0:T(8,128)(2,1)}, bf16[12,128,128]{2,1,0:T(8,128)(2,1)}, bf16[20,128,128]{2,1,0:T(8,1...) custom-call(s32[16]{0:T(128)} %get-tuple-element.90.place.refs_0_, ...), custom_call_target="tpu_custom_call" | custom-call | tf_op jit(solution)/shard_map/contrast_layer/pallas_call | solution.py:684
  165.4 11.8 %collective-permute-done.25 = f32[200,128]{1,0:T(8,128)S(1)} collective-permute-done((f32[200,128]{1,0:T(8,128)S(1)}, f32[200,128]{1,0:T(8,128)S(1)}, u32[]{:S(2)}, u32[]{:S(2)}) %collective-permute-start.25) | collective-permute-done | bytes 102432 | tf_op jit(solution)/shard_map/ppermute | solution.py:96
  177.6 7.3 %collective-permute-done.33.cross_b = bf16[12,128,128]{2,1,0:T(8,128)(2,1)S(1)} collective-permute-done((bf16[12,128,128]{2,1,0:T(8,128)(2,1)S(1)}, bf16[12,128,128]{2,1,0:T(8,128)(2,1)S(1)}, u32[]{:S(2)}, u32[]{:S(2)}) %collective-permute-start.33) | collective-permute-done | bytes 393248 | tf_op jit(solution)/shard_map/ppermute | solution.py:96
  185.7 4.7 %collective-permute-done.26 = f32[200,128]{1,0:T(8,128)S(1)} collective-permute-done((f32[200,128]{1,0:T(8,128)S(1)}, f32[200,128]{1,0:T(8,128)S(1)}, u32[]{:S(2)}, u32[]{:S(2)}) %collective-permute-start.26) | collective-permute-done | bytes 102432 | tf_op jit(solution)/shard_map/ppermute | solution.py:96
  191.4 5.2 %collective-permute-done.27 = f32[200,128]{1,0:T(8,128)S(1)} collective-permute-done((f32[200,128]{1,0:T(8,128)S(1)}, f32[200,128]{1,0:T(8,128)S(1)}, u32[]{:S(2)}, u32[]{:S(2)}) %collective-permute-start.27) | collective-permute-done | bytes 102432 | tf_op jit(solution)/shard_map/ppermute | solution.py:96
  201.8 15.2 %last_layer.1 = (f32[208,128]{1,0:T(8,128)}, f32[208,128]{1,0:T(8,128)}) custom-call(s32[16]{0:T(128)} %get-tuple-element.90.place.refs_0_, s32[32,8]{1,0:T(8,128)} %copy.27.src.refs_1_, s32[32]{0:T(128)} %live.5, bf16[32,8,128,128]{3,2,1,0:T(8,128)(2,1)} %tiles_hbm.5, f32[32,128,128]{2,1,0:T(8,128)} %get-tuple-element.66.own, ...), custom_call_target="tpu_custom_call" | custom-call | tf_op jit(solution)/shard_map/last_layer/pallas_call | solution.py:717
  220.5 4.1 %collective-permute-done.37 = f32[208,128]{1,0:T(8,128)S(1)} collective-permute-done((f32[208,128]{1,0:T(8,128)S(1)}, f32[208,128]{1,0:T(8,128)S(1)}, u32[]{:S(2)}, u32[]{:S(2)}) %collective-permute-start.37) | collective-permute-done | bytes 106528 | tf_op jit(solution)/shard_map/ppermute | solution.py:96
  224.8 4.7 %collective-permute-done.38 = f32[208,128]{1,0:T(8,128)S(1)} collective-permute-done((f32[208,128]{1,0:T(8,128)S(1)}, f32[208,128]{1,0:T(8,128)S(1)}, u32[]{:S(2)}, u32[]{:S(2)}) %collective-permute-start.38) | collective-permute-done | bytes 106528 | tf_op jit(solution)/shard_map/ppermute | solution.py:96
  229.7 6.0 %collective-permute-done.39 = f32[208,128]{1,0:T(8,128)S(1)} collective-permute-done((f32[208,128]{1,0:T(8,128)S(1)}, f32[208,128]{1,0:T(8,128)S(1)}, u32[]{:S(2)}, u32[]{:S(2)}) %collective-permute-start.39) | collective-permute-done | bytes 106528 | tf_op jit(solution)/shard_map/ppermute | solution.py:96
  (189 shorter events, 65.0 us)
Async XLA Ops:
  3.9 16.6 %collective-permute-start.2 = (bf16[16,4096]{1,0:T(8,128)(2,1)S(1)}, bf16[16,4096]{1,0:T(8,128)(2,1)S(1)}, u32[]{:S(2)}, u32[]{:S(2)}) collective-permute-start(bf16[16,4096]{1,0:T(8,128)(2,1)S(1)} %maximum_maximum_fusion.p0), channel_id=1, source_target_pairs={{0,1},{1,0},{2,3},{3,2},{4,5},{5,4},{6,7},{7,6},{8,9},{9,8},{10,11... | collective-permute-start | bytes 393224 | tf_op jit(solution)/shard_map/ppermute | solution.py:96
  4.4 9.8 %collective-permute-start.1 = (bf16[16,4096]{1,0:T(8,128)(2,1)S(1)}, bf16[16,4096]{1,0:T(8,128)(2,1)S(1)}, u32[]{:S(2)}, u32[]{:S(2)}) collective-permute-start(bf16[16,4096]{1,0:T(8,128)(2,1)S(1)} %maximum_maximum_fusion.p0), channel_id=1, source_target_pairs={{0,14},{1,15},{2,4},{3,5},{4,2},{5,3},{6,8},{7,9},{8,6},{9,7},{10,... | collective-permute-start | bytes 393224 | tf_op jit(solution)/shard_map/ppermute | solution.py:96
  10.0 6.9 %collective-permute-start = (bf16[16,4096]{1,0:T(8,128)(2,1)S(1)}, bf16[16,4096]{1,0:T(8,128)(2,1)S(1)}, u32[]{:S(2)}, u32[]{:S(2)}) collective-permute-start(bf16[16,4096]{1,0:T(8,128)(2,1)S(1)} %maximum_maximum_fusion.p0), channel_id=1, source_target_pairs={{0,2},{1,3},{2,0},{3,1},{4,6},{5,7},{6,4},{7,5},{8,10},{9,11},{10,... | collective-permute-start | bytes 393224 | tf_op jit(solution)/shard_map/ppermute | solution.py:96
  30.7 26.3 %collective-permute-start.5 = (bf16[16,128,128]{2,1,0:T(8,128)(2,1)}, bf16[16,128,128]{2,1,0:T(8,128)(2,1)S(1)}, u32[]{:S(2)}, u32[]{:S(2)}) collective-permute-start(bf16[16,128,128]{2,1,0:T(8,128)(2,1)} %get-tuple-element.43.own_a), channel_id=1, source_target_pairs={{0,2},{1,3},{2,0},{3,1},{4,6},{5,7},{6,4},{7,5},{8,10},{9,11},{10,... | collective-permute-start | bytes 1572872 | tf_op jit(solution)/shard_map/ppermute | solution.py:96
  36.5 20.6 %collective-permute-start.8 = (bf16[16,128,128]{2,1,0:T(8,128)(2,1)}, bf16[16,128,128]{2,1,0:T(8,128)(2,1)S(1)}, u32[]{:S(2)}, u32[]{:S(2)}) collective-permute-start(bf16[16,128,128]{2,1,0:T(8,128)(2,1)} %get-tuple-element.47.own_b), channel_id=1, source_target_pairs={{0,14},{1,15},{2,4},{3,5},{4,2},{5,3},{6,8},{7,9},{8,6},{9,7},{10,... | collective-permute-start | bytes 1572872 | tf_op jit(solution)/shard_map/ppermute | solution.py:96
  39.6 27.4 %collective-permute-start.6 = (bf16[16,128,128]{2,1,0:T(8,128)(2,1)}, bf16[16,128,128]{2,1,0:T(8,128)(2,1)S(1)}, u32[]{:S(2)}, u32[]{:S(2)}) collective-permute-start(bf16[16,128,128]{2,1,0:T(8,128)(2,1)} %get-tuple-element.47.own_b), channel_id=1, source_target_pairs={{0,2},{1,3},{2,0},{3,1},{4,6},{5,7},{6,4},{7,5},{8,10},{9,11},{10,... | collective-permute-start | bytes 1572872 | tf_op jit(solution)/shard_map/ppermute | solution.py:96
  39.6 28.6 %collective-permute-start.10 = (bf16[16,128,128]{2,1,0:T(8,128)(2,1)}, bf16[16,128,128]{2,1,0:T(8,128)(2,1)S(1)}, u32[]{:S(2)}, u32[]{:S(2)}) collective-permute-start(bf16[16,128,128]{2,1,0:T(8,128)(2,1)} %get-tuple-element.47.own_b), channel_id=1, source_target_pairs={{0,1},{1,0},{2,3},{3,2},{4,5},{5,4},{6,7},{7,6},{8,9},{9,8},{10,11... | collective-permute-start | bytes 1572872 | tf_op jit(solution)/shard_map/ppermute | solution.py:96
  57.0 14.4 %collective-permute-start.7 = (bf16[16,128,128]{2,1,0:T(8,128)(2,1)S(1)}, bf16[16,128,128]{2,1,0:T(8,128)(2,1)S(1)}, u32[]{:S(2)}, u32[]{:S(2)}) collective-permute-start(bf16[16,128,128]{2,1,0:T(8,128)(2,1)S(1)} %collective-permute-done.5.pair_a), channel_id=1, source_target_pairs={{0,4},{1,5},{2,14},{3,15},{4,8},{5,9},{6,2},{7,3},{8,12},{9,13},{1... | collective-permute-start | bytes 1572872 | tf_op jit(solution)/shard_map/ppermute | solution.py:96
  57.0 15.7 %collective-permute-start.9 = (bf16[16,128,128]{2,1,0:T(8,128)(2,1)}, bf16[16,128,128]{2,1,0:T(8,128)(2,1)S(1)}, u32[]{:S(2)}, u32[]{:S(2)}) collective-permute-start(bf16[16,128,128]{2,1,0:T(8,128)(2,1)} %get-tuple-element.43.own_a), channel_id=1, source_target_pairs={{0,1},{1,0},{2,3},{3,2},{4,5},{5,4},{6,7},{7,6},{8,9},{9,8},{10,11... | collective-permute-start | bytes 1572872 | tf_op jit(solution)/shard_map/ppermute | solution.py:96
  57.0 15.8 %collective-permute-start.11 = (bf16[16,128,128]{2,1,0:T(8,128)(2,1)S(1)}, bf16[16,128,128]{2,1,0:T(8,128)(2,1)S(1)}, u32[]{:S(2)}, u32[]{:S(2)}) collective-permute-start(bf16[16,128,128]{2,1,0:T(8,128)(2,1)S(1)} %collective-permute-done.5.pair_a), channel_id=1, source_target_pairs={{0,1},{3,2},{4,5},{7,6},{8,9},{11,10},{12,13},{15,14},{16,17},{19,... | collective-permute-start | bytes 1572872 | tf_op jit(solution)/shard_map/ppermute | solution.py:96
  95.5 9.0 %collective-permute-start.18 = (bf16[1024,128]{1,0:T(8,128)(2,1)}, bf16[1024,128]{1,0:T(8,128)(2,1)S(1)}, u32[]{:S(2)}, u32[]{:S(2)}) collective-permute-start(bf16[1024,128]{1,0:T(8,128)(2,1)} %get-tuple-element.53), channel_id=1, source_target_pairs={{0,1},{1,0},{2,3},{3,2},{4,5},{5,4},{6,7},{7,6},{8,9},{9,8},{10,11... | collective-permute-start | bytes 786440 | tf_op jit(solution)/shard_map/ppermute | solution.py:96
  97.2 11.1 %collective-permute-start.17 = (bf16[1024,128]{1,0:T(8,128)(2,1)S(1)}, bf16[1024,128]{1,0:T(8,128)(2,1)S(1)}, u32[]{:S(2)}, u32[]{:S(2)}) collective-permute-start(bf16[1024,128]{1,0:T(8,128)(2,1)S(1)} %get-tuple-element.82), channel_id=1, source_target_pairs={{14,0},{15,1},{4,2},{5,3},{2,4},{3,5},{8,6},{9,7},{6,8},{7,9},{12,... | collective-permute-start | bytes 786440 | tf_op jit(solution)/shard_map/ppermute | solution.py:96
  100.8 13.0 %collective-permute-start.16 = (bf16[1024,128]{1,0:T(8,128)(2,1)S(1)}, bf16[1024,128]{1,0:T(8,128)(2,1)S(1)}, u32[]{:S(2)}, u32[]{:S(2)}) collective-permute-start(bf16[1024,128]{1,0:T(8,128)(2,1)S(1)} %get-tuple-element.83), channel_id=1, source_target_pairs={{0,2},{1,3},{2,0},{3,1},{4,6},{5,7},{6,4},{7,5},{8,10},{9,11},{10,... | collective-permute-start | bytes 786440 | tf_op jit(solution)/shard_map/ppermute | solution.py:96
  117.6 14.1 %collective-permute-start.19 = (bf16[1024,128]{1,0:T(8,128)(2,1)}, bf16[1024,128]{1,0:T(8,128)(2,1)S(1)}, u32[]{:S(2)}, u32[]{:S(2)}) collective-permute-start(bf16[1024,128]{1,0:T(8,128)(2,1)} %get-tuple-element.57), channel_id=1, source_target_pairs={{0,2},{1,3},{2,0},{3,1},{4,6},{5,7},{6,4},{7,5},{8,10},{9,11},{10,... | collective-permute-start | bytes 786440 | tf_op jit(solution)/shard_map/ppermute | solution.py:96
  117.6 14.1 %collective-permute-start.20 = (bf16[1024,128]{1,0:T(8,128)(2,1)}, bf16[1024,128]{1,0:T(8,128)(2,1)S(1)}, u32[]{:S(2)}, u32[]{:S(2)}) collective-permute-start(bf16[1024,128]{1,0:T(8,128)(2,1)} %get-tuple-element.57), channel_id=1, source_target_pairs={{0,14},{1,15},{2,4},{3,5},{4,2},{5,3},{6,8},{7,9},{8,6},{9,7},{10,... | collective-permute-start | bytes 786440 | tf_op jit(solution)/shard_map/ppermute | solution.py:96
  119.8 16.4 %collective-permute-start.21 = (bf16[1024,128]{1,0:T(8,128)(2,1)}, bf16[1024,128]{1,0:T(8,128)(2,1)S(1)}, u32[]{:S(2)}, u32[]{:S(2)}) collective-permute-start(bf16[1024,128]{1,0:T(8,128)(2,1)} %get-tuple-element.57), channel_id=1, source_target_pairs={{0,1},{1,0},{2,3},{3,2},{4,5},{5,4},{6,7},{7,6},{8,9},{9,8},{10,11... | collective-permute-start | bytes 786440 | tf_op jit(solution)/shard_map/ppermute | solution.py:96
  158.7 18.5 %collective-permute-start.30 = (bf16[20,128,128]{2,1,0:T(8,128)(2,1)S(1)}, bf16[20,128,128]{2,1,0:T(8,128)(2,1)S(1)}, u32[]{:S(2)}, u32[]{:S(2)}) collective-permute-start(bf16[20,128,128]{2,1,0:T(8,128)(2,1)S(1)} %add_convert_fusion.1), channel_id=1, source_target_pairs={{4,0},{5,1},{14,2},{15,3},{8,4},{9,5},{2,6},{3,7},{12,8},{13,9},{6... | collective-permute-start | bytes 1966088 | tf_op jit(solution)/shard_map/ppermute | solution.py:96
  161.0 23.9 %collective-permute-start.33 = (bf16[12,128,128]{2,1,0:T(8,128)(2,1)S(1)}, bf16[12,128,128]{2,1,0:T(8,128)(2,1)S(1)}, u32[]{:S(2)}, u32[]{:S(2)}) collective-permute-start(bf16[12,128,128]{2,1,0:T(8,128)(2,1)S(1)} %get-tuple-element.80), channel_id=1, source_target_pairs={{14,0},{15,1},{4,2},{5,3},{2,4},{3,5},{8,6},{9,7},{6,8},{7,9},{12,... | collective-permute-start | bytes 1179656 | tf_op jit(solution)/shard_map/ppermute | solution.py:96
  163.4 21.5 %collective-permute-start.32 = (bf16[12,128,128]{2,1,0:T(8,128)(2,1)S(1)}, bf16[12,128,128]{2,1,0:T(8,128)(2,1)S(1)}, u32[]{:S(2)}, u32[]{:S(2)}) collective-permute-start(bf16[12,128,128]{2,1,0:T(8,128)(2,1)S(1)} %get-tuple-element.81), channel_id=1, source_target_pairs={{0,2},{1,3},{2,0},{3,1},{4,6},{5,7},{6,4},{7,5},{8,10},{9,11},{10,... | collective-permute-start | bytes 1179656 | tf_op jit(solution)/shard_map/ppermute | solution.py:96
  164.0 13.2 %collective-permute-start.25 = (f32[200,128]{1,0:T(8,128)S(1)}, f32[200,128]{1,0:T(8,128)S(1)}, u32[]{:S(2)}, u32[]{:S(2)}) collective-permute-start(f32[200,128]{1,0:T(8,128)S(1)} %add.73), channel_id=1, source_target_pairs={{0,2},{1,3},{2,0},{3,1},{4,6},{5,7},{6,4},{7,5},{8,10},{9,11},{10,... | collective-permute-start | bytes 307208 | tf_op jit(solution)/shard_map/ppermute | solution.py:96
  165.4 32.6 %collective-permute-start.35 = (bf16[32,128,128]{2,1,0:T(8,128)(2,1)S(1)}, bf16[32,128,128]{2,1,0:T(8,128)(2,1)S(1)}, u32[]{:S(2)}, u32[]{:S(2)}) collective-permute-start(bf16[32,128,128]{2,1,0:T(8,128)(2,1)S(1)} %copy-done.36), channel_id=1, source_target_pairs={{0,1},{1,0},{2,3},{3,2},{4,5},{5,4},{6,7},{7,6},{8,9},{9,8},{10,11... | collective-permute-start | bytes 3145736 | tf_op jit(solution)/shard_map/ppermute | solution.py:96
  184.9 16.1 %collective-permute-start.34 = (bf16[20,128,128]{2,1,0:T(8,128)(2,1)S(1)}, bf16[20,128,128]{2,1,0:T(8,128)(2,1)S(1)}, u32[]{:S(2)}, u32[]{:S(2)}) collective-permute-start(bf16[20,128,128]{2,1,0:T(8,128)(2,1)S(1)} %add_convert_fusion), channel_id=1, source_target_pairs={{0,2},{1,3},{2,0},{3,1},{4,6},{5,7},{6,4},{7,5},{8,10},{9,11},{10,... | collective-permute-start | bytes 1966088 | tf_op jit(solution)/shard_map/ppermute | solution.py:96
  190.4 6.2 %collective-permute-start.27 = (f32[200,128]{1,0:T(8,128)S(1)}, f32[200,128]{1,0:T(8,128)S(1)}, u32[]{:S(2)}, u32[]{:S(2)}) collective-permute-start(f32[200,128]{1,0:T(8,128)S(1)} %add.75), channel_id=1, source_target_pairs={{0,8},{1,9},{2,10},{3,11},{4,12},{5,13},{6,14},{7,15},{8,0},{9,1},... | collective-permute-start | bytes 307208 | tf_op jit(solution)/shard_map/ppermute | solution.py:96
  229.5 6.3 %collective-permute-start.39 = (f32[208,128]{1,0:T(8,128)S(1)}, f32[208,128]{1,0:T(8,128)S(1)}, u32[]{:S(2)}, u32[]{:S(2)}) collective-permute-start(f32[208,128]{1,0:T(8,128)S(1)} %add.84), channel_id=1, source_target_pairs={{0,8},{1,9},{2,10},{3,11},{4,12},{5,13},{6,14},{7,15},{8,0},{9,1},... | collective-permute-start | bytes 319496 | tf_op jit(solution)/shard_map/ppermute | solution.py:96
  (55 other events, 311.2 us)

commit v4 on v3

--- a/solution.py
+++ b/solution.py
@@ -10,7 +10,6 @@
 loss_divisor = 64.0
 F32 = jnp.float32
 BF16 = jnp.bfloat16
-VMEM_LIMIT = 56 * 1024 * 1024
 PACK_ROWS = 16
 GROUP = 8
 
@@ -29,8 +28,12 @@
     return pl.BlockSpec(memory_space=pl.ANY)
 
 
-def params():
-    return pltpu.CompilerParams(vmem_limit_bytes=VMEM_LIMIT)
+def kept_in_hbm():
+    return pl.BlockSpec(memory_space=pltpu.HBM)
+
+
+def params(mebibytes):
+    return pltpu.CompilerParams(vmem_limit_bytes=mebibytes * 1024 * 1024)
 
 
 def cost(microseconds):
@@ -67,10 +70,6 @@
 
 def core_links(count):
     return [(p, p ^ 1) for p in range(count)]
-
-
-def extra_links(count, from_pair):
-    return [(p ^ 1, p) for p in range(count) if ((p & 1) != second(p)) == from_pair]
 
 
 def turned(links):
@@ -107,8 +106,8 @@
     other = send(value, core_links(count))
     if meanwhile is not None:
         pair = after(pair, meanwhile)
-    extra_p = send(pair, extra_links(count, True))
-    extra_c = send(cross, extra_links(count, False))
+    extra_p = send(pair, core_links(count))
+    extra_c = send(cross, core_links(count))
     return (value, pair, cross, other, extra_p, extra_c)
 
 
@@ -167,12 +166,17 @@
     ).wait()
 
 
-def encode_operand(*pack_refs):
-    rows = sum(pack_ref[...] for pack_ref in pack_refs)
-    ids = rows.astype(F32)[12:13, :]
+def extra_of(place, from_pair, from_cross):
+    return jnp.where(place[0] != place[1], from_pair, from_cross)
+
+
+def encode_operand(place, *pack_refs):
+    pieces = [pack_ref[...].astype(F32) for pack_ref in pack_refs]
+    rows = pieces[0] if len(pieces) == 1 else extra_of(place, *pieces)
+    ids = rows[12:13, :]
     layers = lax.broadcasted_iota(jnp.int32, rows.shape, 0).astype(F32)
     onehot = (layers == ids).astype(BF16)
-    return jnp.concatenate([rows, onehot], axis=0)
+    return jnp.concatenate([rows.astype(BF16), onehot], axis=0)
 
 
 def block_of(place, src, live, b, s, blocks):
@@ -220,7 +224,7 @@
     fetch_tiles(tiles_hbm, tiles, sems, groups)
     w_in = input_weights(w_enc, layer_table)
     for k, pack in enumerate(((p0,), (p1,), (p2,), (p3,), (p4, p5))):
-        latents = jnp.tanh(dot_tn(encode_operand(*pack), w_in)).astype(BF16)
+        latents = jnp.tanh(dot_tn(encode_operand(place, *pack), w_in)).astype(BF16)
         window[pl.ds(k * blocks, blocks)] = latents.reshape(blocks, block_rows, latents.shape[1])
     window[PIECES * blocks] = jnp.zeros(window.shape[1:], BF16)
     own_ref[...] = window[pl.ds(0, blocks)]
@@ -431,7 +435,7 @@
     grads[...] = jnp.zeros(grads.shape, F32)
     for k, piece in enumerate((e1, e2, e3)):
         weighted[pl.ds(k * triplets, triplets), :] = piece[...].astype(F32)
-    weighted[pl.ds(3 * triplets, triplets), :] = e4[...].astype(F32) + e5[...].astype(F32)
+    weighted[pl.ds(3 * triplets, triplets), :] = extra_of(place, e4[...].astype(F32), e5[...].astype(F32))
     weighted[pl.ds(4 * triplets, 8), :] = jnp.zeros((8, weighted.shape[1]), F32)
     for k in range(1, PIECES):
         first_p, first_n, eights = pair_of_lists(lists, counts, k, triplets)
@@ -503,7 +507,7 @@
     w_in = input_weights(w_enc, layer_table)
     grad_in = jnp.zeros(w_in.shape, F32)
     for k, pack in enumerate(((p0,), (p1,), (p2,), (p3,), (p4, p5))):
-        operand = encode_operand(*pack)
+        operand = encode_operand(place, *pack)
         squashed = jnp.tanh(dot_tn(w_in, operand))
         gradient = jnp.concatenate([spread[k * blocks + q] for q in range(blocks)], axis=1)
         encoded_grad = (gradient * (1.0 - squashed * squashed)).astype(BF16)
@@ -547,7 +551,7 @@
     assert feats < PACK_ROWS - 3 and kinds == PACK_ROWS and layers == 2 and 4 * triplets == hits
     assert count % 4 == 0
     groups = blocks // GROUP
-    cut, back_cut = blocks // 2, blocks * 5 // 8
+    cut, back_cut = blocks // 2, blocks * 11 // 16
     place = lax.dynamic_slice_in_dim(place_table(), lax.axis_index("phi") & 3, 1, 0).reshape(-1)
     sends_pair = place[0] == place[1]
 
@@ -580,11 +584,11 @@
         in_specs=[smem()] * 3 + [in_hbm()] + [vmem()] * 11,
         out_specs=(vmem(),) * 6,
         scratch_shapes=[tile_scratch, window_scratch, group_sems],
-        compiler_params=params(),
+        compiler_params=params(56),
         name="first_layer",
     )(*slots_in, edge_tiles, *packs, w_enc, layer_table, w_self, w_agg, w_out)
 
-    held_codes = jnp.stack([packs[1], packs[2], packs[3], packs[4] + packs[5]])[:, feats + 1]
+    held_codes = jnp.stack([each[feats + 1] for each in (*packs[1:4], jnp.where(sends_pair, packs[5], packs[4]))])
     held_codes = after(held_codes, new_a).astype(jnp.int32).reshape(PIECES - 1, 2, 2 * triplets)
     own_codes = jnp.concatenate([positive_hits, negative_hits]).reshape(1, 2 * triplets)
     named = jnp.concatenate([own_codes, (held_codes[:, 0] << 7) + held_codes[:, 1]]).reshape(PIECES, 2, triplets)
@@ -602,20 +606,20 @@
     other_b = send(new_b, core_links(count))
     pair_a = after(pair_a, lists, counts)
     cross_a = send(pair_a, relay_links(count))
-    extra_pa = send(pair_a, extra_links(count, True))
-    extra_pb = send(pair_b, extra_links(count, True))
-    extra_cb = send(cross_b, extra_links(count, False))
-    extra_ca = send(cross_a, extra_links(count, False))
+    extra_pa = send(pair_a, core_links(count))
+    extra_pb = send(pair_b, core_links(count))
+    extra_cb = send(cross_b, core_links(count))
+    extra_ca = send(cross_a, core_links(count))
 
     agg_1, hidden_1, latents_2 = pl.pallas_call(
         next_layer_kernel,
         out_shape=(blocked,) * 3,
-        in_specs=[smem()] * 3 + [in_hbm()] * 13 + [vmem()] * 3,
+        in_specs=[smem()] * 3 + [kept_in_hbm()] + [in_hbm()] * 12 + [vmem()] * 3,
         out_specs=(vmem(),) * 3,
         scratch_shapes=[
             tile_scratch, window_scratch, group_sems, pltpu.SemaphoreType.DMA((2 * PIECES,)),
         ],
-        compiler_params=params(),
+        compiler_params=params(26),
         name="next_layer",
     )(
         *slots_in, edge_tiles, new_a, new_b, pair_a, pair_b, cross_a, cross_b, other_a, other_b,
@@ -635,7 +639,7 @@
             pltpu.VMEM((PIECES * triplets + 8, width), F32),
             pltpu.VMEM((PIECES * triplets + 8, width), F32),
         ],
-        compiler_params=params(),
+        compiler_params=params(18),
         name="gather_rows",
     )(lists, counts, latents_2)
     gaps, joined = return_small(*gap_pieces, sends_pair)
@@ -646,7 +650,7 @@
         in_specs=[smem(), vmem()],
         out_specs=vmem(),
         scratch_shapes=[hit_rows],
-        compiler_params=params(),
+        compiler_params=params(10),
         name="anchor_rows",
     )(anchor_hits, after(latents_2, *joined))
 
@@ -660,7 +664,7 @@
         ),
         in_specs=[vmem()] * 5,
         out_specs=(vmem(),) * 4,
-        compiler_params=params(),
+        compiler_params=params(10),
         name="scores",
     )(gap_own, *gaps, anchor_rows)
 
@@ -670,7 +674,7 @@
         in_specs=[smem()] * 3 + [vmem()] * 2,
         out_specs=vmem(),
         scratch_shapes=[hit_rows] * 3,
-        compiler_params=params(),
+        compiler_params=params(18),
         name="own_rows",
     )(lists, counts, anchor_hits, weighted, anchor_grad)
     weighted_window = gather_small(weighted_b, own_rows)
@@ -692,7 +696,7 @@
             tile_scratch, spread_scratch, grads_scratch, pltpu.VMEM((rows_1, width), F32),
             pltpu.VMEM((4 * triplets + 8, width), F32), hit_rows, hit_rows, hit_rows, hit_rows, group_sems,
         ],
-        compiler_params=params(),
+        compiler_params=params(52),
         name="contrast_layer",
     )(
         *slots_in, lists, counts, edge_tiles,
@@ -723,7 +727,7 @@
             tile_scratch, spread_scratch, grads_scratch, pltpu.VMEM((rows_0, width), F32),
             pltpu.VMEM(block_shape, F32), group_sems,
         ],
-        compiler_params=params(),
+        compiler_params=params(42),
         name="last_layer",
     )(
         *slots_in, edge_tiles, own_1, from_pair_a, from_pair_b, from_cross_b, from_other,
@@ -743,7 +747,7 @@
         in_specs=[smem()] + [vmem()] * 4,
         out_specs=(smem(),) + (vmem(),) * 5,
         scratch_shapes=[pltpu.VMEM((rows_0, width), F32), pltpu.VMEM((rows_1, width), F32)],
-        compiler_params=params(),
+        compiler_params=params(6),
         name="results",
     )(place, part_0, back_0, part_1, back_1)
 

time: 241 us -> 220 us (0.913)
  Pallas kernels: 74.2 us -> 58.7 us
  starting transfers between devices: 41 us -> 26.5 us
  waiting for transfers between devices: 101 us -> 112 us
    ppermute x41, starting transfers between devices: 41 us -> 26.5 us  [send(): return lax.ppermute(value, 'phi', links)]
    ppermute x41, waiting for transfers between devices: 101 us -> 112 us  [send(): return lax.ppermute(value, 'phi', links)]
    pallas_call x1, Pallas kernels: 10.4 us -> 6.07 us  [body(): pl.pallas_call(next_layer_kernel, out_shape=(blocked,) * 3, in_specs=[sme...]
    pallas_call x1, Pallas kernels: 15.2 us -> 11.9 us  [body(): pl.pallas_call(last_layer_kernel, out_shape=(half_0, half_0), in_specs=[s...]
    pallas_call x1, Pallas kernels: 3.03 us -> 0.6 us  [body(): pl.pallas_call(score_kernel, out_shape=(jax.ShapeDtypeStruct((8, width),...]
    unnamed x80 -> x73, local copies, waits for them, and re-layouts: 6.38 us -> 7.57 us
  transfers between devices with their start and end apart: 41 -> 41, of which waited for: 23 -> 26; matrix products, arithmetic and copies ran while one was open for 5% -> 4% of each run, Pallas kernels for 4% -> 3%
where the time goes in v4:
time: 220 us
  waiting for transfers between devices  112 us (51%)
  Pallas kernels  58.7 us (27%)
  starting transfers between devices  26.5 us (12%)
  local copies, waits for them, and re-layouts  10.7 us (5%)
  other arithmetic  9.39 us (4%)
  between operations  2.85 us (1%)
    ppermute x41, waiting for transfers between devices, send(): return lax.ppermute(value, 'phi', links)  112 us
    ppermute x41, starting transfers between devices, send(): return lax.ppermute(value, 'phi', links)  26.5 us
    pallas_call x1, Pallas kernels, body(): pl.pallas_call(lambda *refs: contrast_layer_kernel(row_bits, *refs), out_...  16.4 us
    pallas_call x1, Pallas kernels, body(): pl.pallas_call(last_layer_kernel, out_shape=(half_0, half_0), in_specs=[s...  11.9 us
    pallas_call x1, Pallas kernels, body(): pl.pallas_call(first_layer_kernel, out_shape=(blocked,) * 4 + (head, tail...  9.52 us
    unnamed x73, local copies, waits for them, and re-layouts  7.57 us
    pallas_call x1, Pallas kernels, body(): pl.pallas_call(next_layer_kernel, out_shape=(blocked,) * 3, in_specs=[sme...  6.07 us
    pallas_call x1, Pallas kernels, body(): pl.pallas_call(lambda *refs: gather_kernel(row_bits, *refs), out_shape=(t...  5.81 us
  transfers between devices with their start and end apart: 41, of which 26 were waited for; matrix products, arithmetic and copies ran while one was open for 4% of the time, Pallas kernels for 3%

profile of v4, /device:TPU:0, one launch (start us, length us, event | category | flops | bytes accessed | tf_op | source)
XLA Modules:
  0.0 220.0 jit_solution(14956220844728118794)
XLA Ops:
  4.4 5.6 %collective-permute-start.1 = (bf16[16,4096]{1,0:T(8,128)(2,1)S(1)}, bf16[16,4096]{1,0:T(8,128)(2,1)S(1)}, u32[]{:S(2)}, u32[]{:S(2)}) collective-permute-start(bf16[16,4096]{1,0:T(8,128)(2,1)S(1)} %maximum_maximum_fusion.p0), channel_id=1, source_target_pairs={{0,14},{1,15},{2,4},{3,5},{4,2},{5,3},{6,8},{7,9},{8,6},{9,7},{10,... | collective-permute-start | bytes 393224 | tf_op jit(solution)/shard_map/ppermute | solution.py:95
  21.2 9.5 %first_layer.1 = (bf16[32,128,128]{2,1,0:T(8,128)(2,1)}, bf16[32,128,128]{2,1,0:T(8,128)(2,1)}, bf16[32,128,128]{2,1,0:T(8,128)(2,1)}, bf16[32,128,128]{2,1,0:T(...) custom-call(s32[16]{0:T(128)} %get-tuple-element.90.place.refs_0_, s32[32,8]{1,0:T(8,128)} %copy.27.src.refs_1_, ...), custom_call_target="tpu_custom_call" | custom-call | tf_op jit(solution)/shard_map/first_layer/pallas_call | solution.py:581
  32.8 3.8 %sort.7 = s32[1024,10]{0,1:T(8,128)S(1)} sort(s32[1024,10]{0,1:T(8,128)S(1)} %select_bitcast_fusion), dimensions={0}, to_apply=%region_0.1 | sort | flops 143360 | bytes 81920 | tf_op jit(solution)/shard_map/sort | solution.py:598
  36.6 3.1 %collective-permute-start.8 = (bf16[16,128,128]{2,1,0:T(8,128)(2,1)}, bf16[16,128,128]{2,1,0:T(8,128)(2,1)S(1)}, u32[]{:S(2)}, u32[]{:S(2)}) collective-permute-start(bf16[16,128,128]{2,1,0:T(8,128)(2,1)} %get-tuple-element.47.own_b), channel_id=1, source_target_pairs={{0,14},{1,15},{2,4},{3,5},{4,2},{5,3},{6,8},{7,9},{8,6},{9,7},{10,... | collective-permute-start | bytes 1572872 | tf_op jit(solution)/shard_map/ppermute | solution.py:95
  39.7 17.3 %collective-permute-done.5.pair_a = bf16[16,128,128]{2,1,0:T(8,128)(2,1)S(1)} collective-permute-done((bf16[16,128,128]{2,1,0:T(8,128)(2,1)}, bf16[16,128,128]{2,1,0:T(8,128)(2,1)S(1)}, u32[]{:S(2)}, u32[]{:S(2)}) %collective-permute-start.5) | collective-permute-done | bytes 524320 | tf_op jit(solution)/shard_map/ppermute | solution.py:95
  57.5 10.3 %collective-permute-done.6.pair_b = bf16[16,128,128]{2,1,0:T(8,128)(2,1)S(1)} collective-permute-done((bf16[16,128,128]{2,1,0:T(8,128)(2,1)}, bf16[16,128,128]{2,1,0:T(8,128)(2,1)S(1)}, u32[]{:S(2)}, u32[]{:S(2)}) %collective-permute-start.6) | collective-permute-done | bytes 524320 | tf_op jit(solution)/shard_map/ppermute | solution.py:95
  68.4 3.6 %collective-permute-done.7.cross_a = bf16[16,128,128]{2,1,0:T(8,128)(2,1)S(1)} collective-permute-done((bf16[16,128,128]{2,1,0:T(8,128)(2,1)S(1)}, bf16[16,128,128]{2,1,0:T(8,128)(2,1)S(1)}, u32[]{:S(2)}, u32[]{:S(2)}) %collective-permute-start.7) | collective-permute-done | bytes 524320 | tf_op jit(solution)/shard_map/ppermute | solution.py:95
  73.9 3.4 %copy-done = bf16[32,8,128,128]{3,2,1,0:T(8,128)(2,1)S(1)} copy-done((bf16[32,8,128,128]{3,2,1,0:T(8,128)(2,1)S(1)}, bf16[32,8,128,128]{3,2,1,0:T(8,128)(2,1)}, u32[]{:S(2)}) %copy-start) | copy-done | bytes 8388632
  77.3 6.1 %next_layer.1 = (bf16[32,128,128]{2,1,0:T(8,128)(2,1)S(1)}, bf16[32,128,128]{2,1,0:T(8,128)(2,1)S(1)}, bf16[32,128,128]{2,1,0:T(8,128)(2,1)S(1)}) custom-call(s32[16]{0:T(128)S(1)} %copy-done.26, s32[32,8]{1,0:T(8,128)S(1)} %copy-done.25, s32[32]{0:T(128)S(1)} %copy-done.30, bf16[32,8,128,128]{3,2,1,0:T(8,128)(2,1)S(1)} %copy-done, ...), custom_call_target="tpu_custom_call" | custom-call | tf_op jit(solution)/shard_map/next_layer/pallas_call | solution.py:614
  83.4 5.8 %gather_rows.1 = (bf16[1024,128]{1,0:T(8,128)(2,1)S(1)}, bf16[1024,128]{1,0:T(8,128)(2,1)S(1)}, bf16[1024,128]{1,0:T(8,128)(2,1)S(1)}, bf16[1024,128]{1,0:T(8,128)(2,1)S(1)}, bf16[1024,128]{1,0:T(8,128)(2,1)S(1)}) custom-call(s32[10240]{0:T(1024)S(1)} %reshape.137.refs_0_.refs_3_, s32[10]{0:T(128)S(1)} %reshape.138.refs_1_.refs_4_, ...), custom_call_target="tpu_custom_call" | custom-call | tf_op jit(solution)/shard_map/gather_rows/pallas_call | solution.py:632
  94.7 7.8 %collective-permute-done.17.cross = bf16[1024,128]{1,0:T(8,128)(2,1)S(1)} collective-permute-done((bf16[1024,128]{1,0:T(8,128)(2,1)S(1)}, bf16[1024,128]{1,0:T(8,128)(2,1)S(1)}, u32[]{:S(2)}, u32[]{:S(2)}) %collective-permute-start.17) | collective-permute-done | bytes 262176 | tf_op jit(solution)/shard_map/ppermute | solution.py:95
  102.5 3.8 %collective-permute-done.16.pair = bf16[1024,128]{1,0:T(8,128)(2,1)S(1)} collective-permute-done((bf16[1024,128]{1,0:T(8,128)(2,1)S(1)}, bf16[1024,128]{1,0:T(8,128)(2,1)S(1)}, u32[]{:S(2)}, u32[]{:S(2)}) %collective-permute-start.16) | collective-permute-done | bytes 262176 | tf_op jit(solution)/shard_map/ppermute | solution.py:95
  110.1 5.0 %own_rows.1.refs_6_ = f32[4096,128]{1,0:T(8,128)S(1)} custom-call(s32[10240]{0:T(1024)S(1)} %reshape.137.refs_0_.refs_3_, s32[10]{0:T(128)S(1)} %reshape.138.refs_1_.refs_4_, s32[1024]{0:T(1024)S(1)} %copy-done.27, f32[1032,128]{1,0:T(8,128)S(1)} %get-tuple-element.55.refs_3_, f32[1024,128]{1,0:T(8,128)S(1)} %get-tuple-element.56.refs_4_), custom_call_target="tpu_custom_call" | custom-call | tf_op jit(solution)/shard_map/own_rows/pallas_call | solution.py:671
  116.4 3.4 %collective-permute-done.19.refs_7_ = bf16[1024,128]{1,0:T(8,128)(2,1)S(1)} collective-permute-done((bf16[1024,128]{1,0:T(8,128)(2,1)S(1)}, bf16[1024,128]{1,0:T(8,128)(2,1)S(1)}, u32[]{:S(2)}, u32[]{:S(2)}) %collective-permute-start.19) | collective-permute-done | bytes 262176 | tf_op jit(solution)/shard_map/ppermute | solution.py:95
  121.7 16.4 %contrast_layer.1 = (f32[32,128,128]{2,1,0:T(8,128)}, bf16[22,128,128]{2,1,0:T(8,128)(2,1)}, bf16[10,128,128]{2,1,0:T(8,128)(2,1)}, bf16[22,128,128]{2,1,0:T(8,1...) custom-call(s32[16]{0:T(128)S(1)} %copy-done.26, ...), custom_call_target="tpu_custom_call" | custom-call | tf_op jit(solution)/shard_map/contrast_layer/pallas_call | solution.py:688
  149.5 3.2 %collective-permute-done.25 = f32[200,128]{1,0:T(8,128)S(1)} collective-permute-done((f32[200,128]{1,0:T(8,128)S(1)}, f32[200,128]{1,0:T(8,128)S(1)}, u32[]{:S(2)}, u32[]{:S(2)}) %collective-permute-start.25) | collective-permute-done | bytes 102432 | tf_op jit(solution)/shard_map/ppermute | solution.py:95
  152.7 8.9 %collective-permute-done.30 = bf16[22,128,128]{2,1,0:T(8,128)(2,1)S(1)} collective-permute-done((bf16[22,128,128]{2,1,0:T(8,128)(2,1)S(1)}, bf16[22,128,128]{2,1,0:T(8,128)(2,1)S(1)}, u32[]{:S(2)}, u32[]{:S(2)}) %collective-permute-start.30) | collective-permute-done | bytes 720928 | tf_op jit(solution)/shard_map/ppermute | solution.py:95
  162.1 7.7 %collective-permute-done.33.cross_b = bf16[10,128,128]{2,1,0:T(8,128)(2,1)S(1)} collective-permute-done((bf16[10,128,128]{2,1,0:T(8,128)(2,1)S(1)}, bf16[10,128,128]{2,1,0:T(8,128)(2,1)S(1)}, u32[]{:S(2)}, u32[]{:S(2)}) %collective-permute-start.33) | collective-permute-done | bytes 327712 | tf_op jit(solution)/shard_map/ppermute | solution.py:95
  169.8 4.7 %collective-permute-done.26 = f32[200,128]{1,0:T(8,128)S(1)} collective-permute-done((f32[200,128]{1,0:T(8,128)S(1)}, f32[200,128]{1,0:T(8,128)S(1)}, u32[]{:S(2)}, u32[]{:S(2)}) %collective-permute-start.26) | collective-permute-done | bytes 102432 | tf_op jit(solution)/shard_map/ppermute | solution.py:95
  181.5 6.0 %collective-permute-done.34.pair_a = bf16[22,128,128]{2,1,0:T(8,128)(2,1)S(1)} collective-permute-done((bf16[22,128,128]{2,1,0:T(8,128)(2,1)S(1)}, bf16[22,128,128]{2,1,0:T(8,128)(2,1)S(1)}, u32[]{:S(2)}, u32[]{:S(2)}) %collective-permute-start.34) | collective-permute-done | bytes 720928 | tf_op jit(solution)/shard_map/ppermute | solution.py:95
  187.6 11.9 %last_layer.1 = (f32[208,128]{1,0:T(8,128)S(1)}, f32[208,128]{1,0:T(8,128)S(1)}) custom-call(s32[16]{0:T(128)S(1)} %copy-done.26, s32[32,8]{1,0:T(8,128)S(1)} %copy-done.25, s32[32]{0:T(128)S(1)} %copy-done.30, bf16[32,8,128,128]{3,2,1,0:T(8,128)(2,1)} %tiles_hbm.5, f32[32,128,128]{2,1,0:T(8,128)S(1)} %copy-done.2, ...), custom_call_target="tpu_custom_call" | custom-call | tf_op jit(solution)/shard_map/last_layer/pallas_call | solution.py:721
  201.3 4.7 %collective-permute-done.37 = f32[208,128]{1,0:T(8,128)S(1)} collective-permute-done((f32[208,128]{1,0:T(8,128)S(1)}, f32[208,128]{1,0:T(8,128)S(1)}, u32[]{:S(2)}, u32[]{:S(2)}) %collective-permute-start.37) | collective-permute-done | bytes 106528 | tf_op jit(solution)/shard_map/ppermute | solution.py:95
  206.1 4.7 %collective-permute-done.38 = f32[208,128]{1,0:T(8,128)S(1)} collective-permute-done((f32[208,128]{1,0:T(8,128)S(1)}, f32[208,128]{1,0:T(8,128)S(1)}, u32[]{:S(2)}, u32[]{:S(2)}) %collective-permute-start.38) | collective-permute-done | bytes 106528 | tf_op jit(solution)/shard_map/ppermute | solution.py:95
  211.7 5.4 %collective-permute-done.39 = f32[208,128]{1,0:T(8,128)S(1)} collective-permute-done((f32[208,128]{1,0:T(8,128)S(1)}, f32[208,128]{1,0:T(8,128)S(1)}, u32[]{:S(2)}, u32[]{:S(2)}) %collective-permute-start.39) | collective-permute-done | bytes 106528 | tf_op jit(solution)/shard_map/ppermute | solution.py:95
  (185 shorter events, 54.8 us)
Async XLA Ops:
  3.9 16.6 %collective-permute-start.2 = (bf16[16,4096]{1,0:T(8,128)(2,1)S(1)}, bf16[16,4096]{1,0:T(8,128)(2,1)S(1)}, u32[]{:S(2)}, u32[]{:S(2)}) collective-permute-start(bf16[16,4096]{1,0:T(8,128)(2,1)S(1)} %maximum_maximum_fusion.p0), channel_id=1, source_target_pairs={{0,1},{1,0},{2,3},{3,2},{4,5},{5,4},{6,7},{7,6},{8,9},{9,8},{10,11... | collective-permute-start | bytes 393224 | tf_op jit(solution)/shard_map/ppermute | solution.py:95
  4.4 9.8 %collective-permute-start.1 = (bf16[16,4096]{1,0:T(8,128)(2,1)S(1)}, bf16[16,4096]{1,0:T(8,128)(2,1)S(1)}, u32[]{:S(2)}, u32[]{:S(2)}) collective-permute-start(bf16[16,4096]{1,0:T(8,128)(2,1)S(1)} %maximum_maximum_fusion.p0), channel_id=1, source_target_pairs={{0,14},{1,15},{2,4},{3,5},{4,2},{5,3},{6,8},{7,9},{8,6},{9,7},{10,... | collective-permute-start | bytes 393224 | tf_op jit(solution)/shard_map/ppermute | solution.py:95
  10.0 6.9 %collective-permute-start = (bf16[16,4096]{1,0:T(8,128)(2,1)S(1)}, bf16[16,4096]{1,0:T(8,128)(2,1)S(1)}, u32[]{:S(2)}, u32[]{:S(2)}) collective-permute-start(bf16[16,4096]{1,0:T(8,128)(2,1)S(1)} %maximum_maximum_fusion.p0), channel_id=1, source_target_pairs={{0,2},{1,3},{2,0},{3,1},{4,6},{5,7},{6,4},{7,5},{8,10},{9,11},{10,... | collective-permute-start | bytes 393224 | tf_op jit(solution)/shard_map/ppermute | solution.py:95
  14.2 6.3 %collective-permute-start.3 = (bf16[16,4096]{1,0:T(8,128)(2,1)S(1)}, bf16[16,4096]{1,0:T(8,128)(2,1)S(1)}, u32[]{:S(2)}, u32[]{:S(2)}) collective-permute-start(bf16[16,4096]{1,0:T(8,128)(2,1)S(1)} %collective-permute-done.1.p2), channel_id=1, source_target_pairs={{0,1},{1,0},{2,3},{3,2},{4,5},{5,4},{6,7},{7,6},{8,9},{9,8},{10,11... | collective-permute-start | bytes 393224 | tf_op jit(solution)/shard_map/ppermute | solution.py:95
  30.8 26.2 %collective-permute-start.5 = (bf16[16,128,128]{2,1,0:T(8,128)(2,1)}, bf16[16,128,128]{2,1,0:T(8,128)(2,1)S(1)}, u32[]{:S(2)}, u32[]{:S(2)}) collective-permute-start(bf16[16,128,128]{2,1,0:T(8,128)(2,1)} %get-tuple-element.43.own_a), channel_id=1, source_target_pairs={{0,2},{1,3},{2,0},{3,1},{4,6},{5,7},{6,4},{7,5},{8,10},{9,11},{10,... | collective-permute-start | bytes 1572872 | tf_op jit(solution)/shard_map/ppermute | solution.py:95
  36.6 20.4 %collective-permute-start.8 = (bf16[16,128,128]{2,1,0:T(8,128)(2,1)}, bf16[16,128,128]{2,1,0:T(8,128)(2,1)S(1)}, u32[]{:S(2)}, u32[]{:S(2)}) collective-permute-start(bf16[16,128,128]{2,1,0:T(8,128)(2,1)} %get-tuple-element.47.own_b), channel_id=1, source_target_pairs={{0,14},{1,15},{2,4},{3,5},{4,2},{5,3},{6,8},{7,9},{8,6},{9,7},{10,... | collective-permute-start | bytes 1572872 | tf_op jit(solution)/shard_map/ppermute | solution.py:95
  39.7 28.1 %collective-permute-start.6 = (bf16[16,128,128]{2,1,0:T(8,128)(2,1)}, bf16[16,128,128]{2,1,0:T(8,128)(2,1)S(1)}, u32[]{:S(2)}, u32[]{:S(2)}) collective-permute-start(bf16[16,128,128]{2,1,0:T(8,128)(2,1)} %get-tuple-element.47.own_b), channel_id=1, source_target_pairs={{0,2},{1,3},{2,0},{3,1},{4,6},{5,7},{6,4},{7,5},{8,10},{9,11},{10,... | collective-permute-start | bytes 1572872 | tf_op jit(solution)/shard_map/ppermute | solution.py:95
  39.7 28.1 %collective-permute-start.10 = (bf16[16,128,128]{2,1,0:T(8,128)(2,1)}, bf16[16,128,128]{2,1,0:T(8,128)(2,1)S(1)}, u32[]{:S(2)}, u32[]{:S(2)}) collective-permute-start(bf16[16,128,128]{2,1,0:T(8,128)(2,1)} %get-tuple-element.47.own_b), channel_id=1, source_target_pairs={{0,1},{1,0},{2,3},{3,2},{4,5},{5,4},{6,7},{7,6},{8,9},{9,8},{10,11... | collective-permute-start | bytes 1572872 | tf_op jit(solution)/shard_map/ppermute | solution.py:95
  57.0 14.9 %collective-permute-start.7 = (bf16[16,128,128]{2,1,0:T(8,128)(2,1)S(1)}, bf16[16,128,128]{2,1,0:T(8,128)(2,1)S(1)}, u32[]{:S(2)}, u32[]{:S(2)}) collective-permute-start(bf16[16,128,128]{2,1,0:T(8,128)(2,1)S(1)} %collective-permute-done.5.pair_a), channel_id=1, source_target_pairs={{0,4},{1,5},{2,14},{3,15},{4,8},{5,9},{6,2},{7,3},{8,12},{9,13},{1... | collective-permute-start | bytes 1572872 | tf_op jit(solution)/shard_map/ppermute | solution.py:95
  57.0 14.9 %collective-permute-start.9 = (bf16[16,128,128]{2,1,0:T(8,128)(2,1)}, bf16[16,128,128]{2,1,0:T(8,128)(2,1)S(1)}, u32[]{:S(2)}, u32[]{:S(2)}) collective-permute-start(bf16[16,128,128]{2,1,0:T(8,128)(2,1)} %get-tuple-element.43.own_a), channel_id=1, source_target_pairs={{0,1},{1,0},{2,3},{3,2},{4,5},{5,4},{6,7},{7,6},{8,9},{9,8},{10,11... | collective-permute-start | bytes 1572872 | tf_op jit(solution)/shard_map/ppermute | solution.py:95
  57.0 14.9 %collective-permute-start.11 = (bf16[16,128,128]{2,1,0:T(8,128)(2,1)S(1)}, bf16[16,128,128]{2,1,0:T(8,128)(2,1)S(1)}, u32[]{:S(2)}, u32[]{:S(2)}) collective-permute-start(bf16[16,128,128]{2,1,0:T(8,128)(2,1)S(1)} %collective-permute-done.5.pair_a), channel_id=1, source_target_pairs={{0,1},{1,0},{2,3},{3,2},{4,5},{5,4},{6,7},{7,6},{8,9},{9,8},{10,11... | collective-permute-start | bytes 1572872 | tf_op jit(solution)/shard_map/ppermute | solution.py:95
  91.1 11.5 %collective-permute-start.17 = (bf16[1024,128]{1,0:T(8,128)(2,1)S(1)}, bf16[1024,128]{1,0:T(8,128)(2,1)S(1)}, u32[]{:S(2)}, u32[]{:S(2)}) collective-permute-start(bf16[1024,128]{1,0:T(8,128)(2,1)S(1)} %get-tuple-element.82), channel_id=1, source_target_pairs={{14,0},{15,1},{4,2},{5,3},{2,4},{3,5},{8,6},{9,7},{6,8},{7,9},{12,... | collective-permute-start | bytes 786440 | tf_op jit(solution)/shard_map/ppermute | solution.py:95
  92.6 13.7 %collective-permute-start.16 = (bf16[1024,128]{1,0:T(8,128)(2,1)S(1)}, bf16[1024,128]{1,0:T(8,128)(2,1)S(1)}, u32[]{:S(2)}, u32[]{:S(2)}) collective-permute-start(bf16[1024,128]{1,0:T(8,128)(2,1)S(1)} %get-tuple-element.83), channel_id=1, source_target_pairs={{0,2},{1,3},{2,0},{3,1},{4,6},{5,7},{6,4},{7,5},{8,10},{9,11},{10,... | collective-permute-start | bytes 786440 | tf_op jit(solution)/shard_map/ppermute | solution.py:95
  106.9 12.9 %collective-permute-start.19 = (bf16[1024,128]{1,0:T(8,128)(2,1)S(1)}, bf16[1024,128]{1,0:T(8,128)(2,1)S(1)}, u32[]{:S(2)}, u32[]{:S(2)}) collective-permute-start(bf16[1024,128]{1,0:T(8,128)(2,1)S(1)} %get-tuple-element.57), channel_id=1, source_target_pairs={{0,2},{1,3},{2,0},{3,1},{4,6},{5,7},{6,4},{7,5},{8,10},{9,11},{10,... | collective-permute-start | bytes 786440 | tf_op jit(solution)/shard_map/ppermute | solution.py:95
  107.0 12.8 %collective-permute-start.20 = (bf16[1024,128]{1,0:T(8,128)(2,1)S(1)}, bf16[1024,128]{1,0:T(8,128)(2,1)S(1)}, u32[]{:S(2)}, u32[]{:S(2)}) collective-permute-start(bf16[1024,128]{1,0:T(8,128)(2,1)S(1)} %get-tuple-element.57), channel_id=1, source_target_pairs={{0,14},{1,15},{2,4},{3,5},{4,2},{5,3},{6,8},{7,9},{8,6},{9,7},{10,... | collective-permute-start | bytes 786440 | tf_op jit(solution)/shard_map/ppermute | solution.py:95
  110.1 10.3 %collective-permute-start.21 = (bf16[1024,128]{1,0:T(8,128)(2,1)S(1)}, bf16[1024,128]{1,0:T(8,128)(2,1)S(1)}, u32[]{:S(2)}, u32[]{:S(2)}) collective-permute-start(bf16[1024,128]{1,0:T(8,128)(2,1)S(1)} %get-tuple-element.57), channel_id=1, source_target_pairs={{0,1},{1,0},{2,3},{3,2},{4,5},{5,4},{6,7},{7,6},{8,9},{9,8},{10,11... | collective-permute-start | bytes 786440 | tf_op jit(solution)/shard_map/ppermute | solution.py:95
  142.2 19.5 %collective-permute-start.30 = (bf16[22,128,128]{2,1,0:T(8,128)(2,1)S(1)}, bf16[22,128,128]{2,1,0:T(8,128)(2,1)S(1)}, u32[]{:S(2)}, u32[]{:S(2)}) collective-permute-start(bf16[22,128,128]{2,1,0:T(8,128)(2,1)S(1)} %add_convert_fusion.1), channel_id=1, source_target_pairs={{4,0},{5,1},{14,2},{15,3},{8,4},{9,5},{2,6},{3,7},{12,8},{13,9},{6... | collective-permute-start | bytes 2162696 | tf_op jit(solution)/shard_map/ppermute | solution.py:95
  147.0 5.7 %collective-permute-start.25 = (f32[200,128]{1,0:T(8,128)S(1)}, f32[200,128]{1,0:T(8,128)S(1)}, u32[]{:S(2)}, u32[]{:S(2)}) collective-permute-start(f32[200,128]{1,0:T(8,128)S(1)} %add.69), channel_id=1, source_target_pairs={{0,2},{1,3},{2,0},{3,1},{4,6},{5,7},{6,4},{7,5},{8,10},{9,11},{10,... | collective-permute-start | bytes 307208 | tf_op jit(solution)/shard_map/ppermute | solution.py:95
  147.3 22.5 %collective-permute-start.33 = (bf16[10,128,128]{2,1,0:T(8,128)(2,1)S(1)}, bf16[10,128,128]{2,1,0:T(8,128)(2,1)S(1)}, u32[]{:S(2)}, u32[]{:S(2)}) collective-permute-start(bf16[10,128,128]{2,1,0:T(8,128)(2,1)S(1)} %get-tuple-element.80), channel_id=1, source_target_pairs={{14,0},{15,1},{4,2},{5,3},{2,4},{3,5},{8,6},{9,7},{6,8},{7,9},{12,... | collective-permute-start | bytes 983048 | tf_op jit(solution)/shard_map/ppermute | solution.py:95
  148.9 20.9 %collective-permute-start.32 = (bf16[10,128,128]{2,1,0:T(8,128)(2,1)S(1)}, bf16[10,128,128]{2,1,0:T(8,128)(2,1)S(1)}, u32[]{:S(2)}, u32[]{:S(2)}) collective-permute-start(bf16[10,128,128]{2,1,0:T(8,128)(2,1)S(1)} %get-tuple-element.81), channel_id=1, source_target_pairs={{0,2},{1,3},{2,0},{3,1},{4,6},{5,7},{6,4},{7,5},{8,10},{9,11},{10,... | collective-permute-start | bytes 983048 | tf_op jit(solution)/shard_map/ppermute | solution.py:95
  149.5 32.1 %collective-permute-start.35 = (bf16[32,128,128]{2,1,0:T(8,128)(2,1)}, bf16[32,128,128]{2,1,0:T(8,128)(2,1)S(1)}, u32[]{:S(2)}, u32[]{:S(2)}) collective-permute-start(bf16[32,128,128]{2,1,0:T(8,128)(2,1)} %get-tuple-element.74), channel_id=1, source_target_pairs={{0,1},{1,0},{2,3},{3,2},{4,5},{5,4},{6,7},{7,6},{8,9},{9,8},{10,11... | collective-permute-start | bytes 3145736 | tf_op jit(solution)/shard_map/ppermute | solution.py:95
  169.8 17.7 %collective-permute-start.34 = (bf16[22,128,128]{2,1,0:T(8,128)(2,1)S(1)}, bf16[22,128,128]{2,1,0:T(8,128)(2,1)S(1)}, u32[]{:S(2)}, u32[]{:S(2)}) collective-permute-start(bf16[22,128,128]{2,1,0:T(8,128)(2,1)S(1)} %add_convert_fusion), channel_id=1, source_target_pairs={{0,2},{1,3},{2,0},{3,1},{4,6},{5,7},{6,4},{7,5},{8,10},{9,11},{10,... | collective-permute-start | bytes 2162696 | tf_op jit(solution)/shard_map/ppermute | solution.py:95
  174.5 5.6 %collective-permute-start.27 = (f32[200,128]{1,0:T(8,128)S(1)}, f32[200,128]{1,0:T(8,128)S(1)}, u32[]{:S(2)}, u32[]{:S(2)}) collective-permute-start(f32[200,128]{1,0:T(8,128)S(1)} %add.71), channel_id=1, source_target_pairs={{0,8},{1,9},{2,10},{3,11},{4,12},{5,13},{6,14},{7,15},{8,0},{9,1},... | collective-permute-start | bytes 307208 | tf_op jit(solution)/shard_map/ppermute | solution.py:95
  210.8 6.3 %collective-permute-start.39 = (f32[208,128]{1,0:T(8,128)S(1)}, f32[208,128]{1,0:T(8,128)S(1)}, u32[]{:S(2)}, u32[]{:S(2)}) collective-permute-start(f32[208,128]{1,0:T(8,128)S(1)} %add.80), channel_id=1, source_target_pairs={{0,8},{1,9},{2,10},{3,11},{4,12},{5,13},{6,14},{7,15},{8,0},{9,1},... | collective-permute-start | bytes 319496 | tf_op jit(solution)/shard_map/ppermute | solution.py:95
  (52 other events, 968.5 us)

commit v5 on v4

--- a/solution.py
+++ b/solution.py
@@ -11,7 +11,7 @@
 F32 = jnp.float32
 BF16 = jnp.bfloat16
 PACK_ROWS = 16
-GROUP = 8
+GROUP = 16
 
 PIECES = 5
 
@@ -179,9 +179,9 @@
     return jnp.concatenate([rows.astype(BF16), onehot], axis=0)
 
 
-def block_of(place, src, live, b, s, blocks):
+def block_of(place, src, live, b, s, blocks, slots):
     bits = blocks.bit_length() - 1
-    named = src[b, s]
+    named = src[b * slots + s]
     block = (place[2 + (named >> bits)] << bits) + (named & (blocks - 1))
     return jnp.where(s < live[b], block, PIECES * blocks)
 
@@ -192,7 +192,7 @@
     for q in range(GROUP):
         b = g * GROUP + q
         left = jnp.concatenate([tiles[b, s] for s in range(slots)], axis=1)
-        right = [window[block_of(place, src, live, b, s, blocks)] for s in range(slots)]
+        right = [window[block_of(place, src, live, b, s, blocks, slots)] for s in range(slots)]
         sums.append(dot_nn(left, jnp.concatenate(right, axis=0)))
     first = pl.multiple_of(g * GROUP, GROUP)
     agg = jnp.concatenate(sums, axis=0).astype(BF16)
@@ -399,7 +399,7 @@
         right = jnp.concatenate([tiles[b, s] for s in range(slots)], axis=1)
         parts = dot_nn(agg_grad[:, q * rows : (q + 1) * rows], right)
         for s in range(slots):
-            spread[block_of(place, src, live, b, s, blocks)] += parts[:, s * rows : (s + 1) * rows]
+            spread[block_of(place, src, live, b, s, blocks, slots)] += parts[:, s * rows : (s + 1) * rows]
 
 
 def put_halves(place, whole, kept_ref, given_ref):
@@ -565,7 +565,8 @@
             jnp.zeros((PACK_ROWS - feats - 2, hits), BF16),
         ]
     )
-    packs = gather_small(pack)
+    src_flat = src_blocks.reshape(-1)
+    packs = gather_small(pack, src_flat)
 
     block_shape = (blocks, block_rows, width)
     tile_scratch = pltpu.VMEM(edge_tiles.shape, BF16)
@@ -576,7 +577,7 @@
     tail = jax.ShapeDtypeStruct((blocks - cut, block_rows, width), BF16)
     back_head = jax.ShapeDtypeStruct((back_cut, block_rows, width), BF16)
     back_tail = jax.ShapeDtypeStruct((blocks - back_cut, block_rows, width), BF16)
-    slots_in = (place, src_blocks, live_slots)
+    slots_in = (place, src_flat, live_slots)
 
     latents_0, agg_0, hidden_0, latents_1, new_a, new_b = pl.pallas_call(
         first_layer_kernel,
@@ -619,7 +620,7 @@
         scratch_shapes=[
             tile_scratch, window_scratch, group_sems, pltpu.SemaphoreType.DMA((2 * PIECES,)),
         ],
-        compiler_params=params(26),
+        compiler_params=params(42),
         name="next_layer",
     )(
         *slots_in, edge_tiles, new_a, new_b, pair_a, pair_b, cross_a, cross_b, other_a, other_b,
@@ -696,7 +697,7 @@
             tile_scratch, spread_scratch, grads_scratch, pltpu.VMEM((rows_1, width), F32),
             pltpu.VMEM((4 * triplets + 8, width), F32), hit_rows, hit_rows, hit_rows, hit_rows, group_sems,
         ],
-        compiler_params=params(52),
+        compiler_params=params(36),
         name="contrast_layer",
     )(
         *slots_in, lists, counts, edge_tiles,
@@ -714,8 +715,8 @@
     from_cross_b = send(ret_cb, turned(cross_links(count)))
     ret_pa = (ret_pa.astype(F32) + relayed.astype(F32)).astype(BF16)
     part_1 = first_sums(kept_1, given_1)
-    from_pair_a = send(after(ret_pa, from_pair_b, from_cross_b, part_1), pair_links(count))
-    part_1, back_1 = last_sums(part_1)
+    from_pair_a = send(after(ret_pa, from_pair_b, part_1), pair_links(count))
+    part_1, back_1 = last_sums(after(part_1, from_cross_b))
     own_1 = after(own_1, part_1, back_1)
 
     kept_0, given_0 = pl.pallas_call(
@@ -727,7 +728,7 @@
             tile_scratch, spread_scratch, grads_scratch, pltpu.VMEM((rows_0, width), F32),
             pltpu.VMEM(block_shape, F32), group_sems,
         ],
-        compiler_params=params(42),
+        compiler_params=params(30),
         name="last_layer",
     )(
         *slots_in, edge_tiles, own_1, from_pair_a, from_pair_b, from_cross_b, from_other,

time: 220 us -> 211 us (0.959)
  local copies, waits for them, and re-layouts: 10.7 us -> 6.02 us
  waiting for transfers between devices: 112 us -> 108 us
  Pallas kernels: 58.7 us -> 55.1 us
  starting transfers between devices: 26.5 us -> 29.5 us
    unnamed x73 -> x61, local copies, waits for them, and re-layouts: 7.57 us -> 2.22 us
    pallas_call x1, Pallas kernels: 16.4 us -> 12.6 us  [body(): pl.pallas_call(lambda *refs: contrast_layer_kernel(row_bits, *refs), out_...]
    ppermute x41, waiting for transfers between devices: 112 us -> 108 us  [send(): return lax.ppermute(value, 'phi', links)]
    ppermute x41, starting transfers between devices: 26.5 us -> 29.5 us  [send(): return lax.ppermute(value, 'phi', links)]
  transfers between devices with their start and end apart: 41 -> 41, of which waited for: 26 -> 24; matrix products, arithmetic and copies ran while one was open for 4% -> 5% of each run, Pallas kernels for 3% -> 3%
where the time goes in v5:
time: 211 us; the launch traced here: 210 us
  waiting for transfers between devices  108 us (51%)
  Pallas kernels  55.1 us (26%)
  starting transfers between devices  29.5 us (14%)
  other arithmetic  8.17 us (4%)
  local copies, waits for them, and re-layouts  6.02 us (3%)
  between operations  2.81 us (1%)
    ppermute x41, waiting for transfers between devices, send(): return lax.ppermute(value, 'phi', links)  108 us
    ppermute x41, starting transfers between devices, send(): return lax.ppermute(value, 'phi', links)  29.5 us
    pallas_call x1, Pallas kernels, body(): pl.pallas_call(lambda *refs: contrast_layer_kernel(row_bits, *refs), out_...  12.6 us
    pallas_call x1, Pallas kernels, body(): pl.pallas_call(last_layer_kernel, out_shape=(half_0, half_0), in_specs=[s...  11.3 us
    pallas_call x1, Pallas kernels, body(): pl.pallas_call(first_layer_kernel, out_shape=(blocked,) * 4 + (head, tail...  8.91 us
    pallas_call x1, Pallas kernels, body(): pl.pallas_call(next_layer_kernel, out_shape=(blocked,) * 3, in_specs=[sme...  6.85 us
    pallas_call x1, Pallas kernels, body(): pl.pallas_call(lambda *refs: gather_kernel(row_bits, *refs), out_shape=(t...  6.32 us
    pallas_call x1, Pallas kernels, body(): pl.pallas_call(lambda *refs: own_rows_kernel(row_bits, *refs), out_shape=...  5.16 us
  transfers between devices with their start and end apart: 41, of which 24 were waited for; matrix products, arithmetic and copies ran while one was open for 5% of the time, Pallas kernels for 3%

profile of v5, /device:TPU:0, one launch (start us, length us, event | category | flops | bytes accessed | tf_op | source)
XLA Modules:
  0.0 209.8 jit_solution(11568783692185469660)
XLA Ops:
  4.4 5.6 %collective-permute-start.1 = (bf16[16,4096]{1,0:T(8,128)(2,1)S(1)}, bf16[16,4096]{1,0:T(8,128)(2,1)S(1)}, u32[]{:S(2)}, u32[]{:S(2)}) collective-permute-start(bf16[16,4096]{1,0:T(8,128)(2,1)S(1)} %maximum_maximum_fusion.p0), channel_id=1, source_target_pairs={{0,14},{1,15},{2,4},{3,5},{4,2},{5,3},{6,8},{7,9},{8,6},{9,7},{10,... | collective-permute-start | bytes 393224 | tf_op jit(solution)/shard_map/ppermute | solution.py:95
  12.7 4.2 %collective-permute-done.p1 = bf16[16,4096]{1,0:T(8,128)(2,1)S(1)} collective-permute-done((bf16[16,4096]{1,0:T(8,128)(2,1)S(1)}, bf16[16,4096]{1,0:T(8,128)(2,1)S(1)}, u32[]{:S(2)}, u32[]{:S(2)}) %collective-permute-start) | collective-permute-done | bytes 131104 | tf_op jit(solution)/shard_map/ppermute | solution.py:95
  20.3 8.9 %first_layer.1 = (bf16[32,128,128]{2,1,0:T(8,128)(2,1)}, bf16[32,128,128]{2,1,0:T(8,128)(2,1)}, bf16[32,128,128]{2,1,0:T(8,128)(2,1)}, bf16[32,128,128]{2,1,0:T(...) custom-call(s32[16]{0:T(128)} %get-tuple-element.94.place.refs_0_, s32[256]{0:T(256)} %reshape.135.src.refs_1_, ...), custom_call_target="tpu_custom_call" | custom-call | tf_op jit(solution)/shard_map/first_layer/pallas_call | solution.py:582
  31.3 3.8 %sort.7 = s32[1024,10]{0,1:T(8,128)S(1)} sort(s32[1024,10]{0,1:T(8,128)S(1)} %select_bitcast_fusion), dimensions={0}, to_apply=%region_0.1 | sort | flops 143360 | bytes 81920 | tf_op jit(solution)/shard_map/sort | solution.py:599
  38.2 17.4 %collective-permute-done.5.pair_a = bf16[16,128,128]{2,1,0:T(8,128)(2,1)S(1)} collective-permute-done((bf16[16,128,128]{2,1,0:T(8,128)(2,1)}, bf16[16,128,128]{2,1,0:T(8,128)(2,1)S(1)}, u32[]{:S(2)}, u32[]{:S(2)}) %collective-permute-start.5) | collective-permute-done | bytes 524320 | tf_op jit(solution)/shard_map/ppermute | solution.py:95
  56.1 9.8 %collective-permute-done.6.pair_b = bf16[16,128,128]{2,1,0:T(8,128)(2,1)S(1)} collective-permute-done((bf16[16,128,128]{2,1,0:T(8,128)(2,1)}, bf16[16,128,128]{2,1,0:T(8,128)(2,1)S(1)}, u32[]{:S(2)}, u32[]{:S(2)}) %collective-permute-start.6) | collective-permute-done | bytes 524320 | tf_op jit(solution)/shard_map/ppermute | solution.py:95
  66.5 3.1 %collective-permute-done.7.cross_a = bf16[16,128,128]{2,1,0:T(8,128)(2,1)S(1)} collective-permute-done((bf16[16,128,128]{2,1,0:T(8,128)(2,1)S(1)}, bf16[16,128,128]{2,1,0:T(8,128)(2,1)S(1)}, u32[]{:S(2)}, u32[]{:S(2)}) %collective-permute-start.7) | collective-permute-done | bytes 524320 | tf_op jit(solution)/shard_map/ppermute | solution.py:95
  71.5 6.9 %next_layer.1 = (bf16[32,128,128]{2,1,0:T(8,128)(2,1)S(1)}, bf16[32,128,128]{2,1,0:T(8,128)(2,1)S(1)}, bf16[32,128,128]{2,1,0:T(8,128)(2,1)S(1)}) custom-call(s32[16]{0:T(128)S(1)} %copy-done.22, s32[256]{0:T(256)S(1)} %copy-done.21, s32[32]{0:T(128)S(1)} %copy-done.26, bf16[32,8,128,128]{3,2,1,0:T(8,128)(2,1)} %tiles_hbm.5, ...), custom_call_target="tpu_custom_call" | custom-call | tf_op jit(solution)/shard_map/next_layer/pallas_call | solution.py:615
  78.4 6.3 %gather_rows.1 = (bf16[1024,128]{1,0:T(8,128)(2,1)S(1)}, bf16[1024,128]{1,0:T(8,128)(2,1)S(1)}, bf16[1024,128]{1,0:T(8,128)(2,1)S(1)}, bf16[1024,128]{1,0:T(8,128)(2,1)S(1)}, bf16[1024,128]{1,0:T(8,128)(2,1)S(1)}) custom-call(s32[10240]{0:T(1024)S(1)} %reshape.141.refs_0_.refs_3_, s32[10]{0:T(128)S(1)} %reshape.142.refs_1_.refs_4_, ...), custom_call_target="tpu_custom_call" | custom-call | tf_op jit(solution)/shard_map/gather_rows/pallas_call | solution.py:633
  90.7 7.0 %collective-permute-done.17.cross = bf16[1024,128]{1,0:T(8,128)(2,1)S(1)} collective-permute-done((bf16[1024,128]{1,0:T(8,128)(2,1)S(1)}, bf16[1024,128]{1,0:T(8,128)(2,1)S(1)}, u32[]{:S(2)}, u32[]{:S(2)}) %collective-permute-start.17) | collective-permute-done | bytes 262176 | tf_op jit(solution)/shard_map/ppermute | solution.py:95
  97.7 4.6 %collective-permute-done.16.pair = bf16[1024,128]{1,0:T(8,128)(2,1)S(1)} collective-permute-done((bf16[1024,128]{1,0:T(8,128)(2,1)S(1)}, bf16[1024,128]{1,0:T(8,128)(2,1)S(1)}, u32[]{:S(2)}, u32[]{:S(2)}) %collective-permute-start.16) | collective-permute-done | bytes 262176 | tf_op jit(solution)/shard_map/ppermute | solution.py:95
  105.7 5.2 %own_rows.1.refs_6_ = f32[4096,128]{1,0:T(8,128)S(1)} custom-call(s32[10240]{0:T(1024)S(1)} %reshape.141.refs_0_.refs_3_, s32[10]{0:T(128)S(1)} %reshape.142.refs_1_.refs_4_, s32[1024]{0:T(1024)S(1)} %copy-done.23, f32[1032,128]{1,0:T(8,128)S(1)} %get-tuple-element.58.refs_3_, f32[1024,128]{1,0:T(8,128)S(1)} %get-tuple-element.59.refs_4_), custom_call_target="tpu_custom_call" | custom-call | tf_op jit(solution)/shard_map/own_rows/pallas_call | solution.py:672
  110.9 5.1 %collective-permute-done.19.refs_7_ = bf16[1024,128]{1,0:T(8,128)(2,1)S(1)} collective-permute-done((bf16[1024,128]{1,0:T(8,128)(2,1)S(1)}, bf16[1024,128]{1,0:T(8,128)(2,1)S(1)}, u32[]{:S(2)}, u32[]{:S(2)}) %collective-permute-start.19) | collective-permute-done | bytes 262176 | tf_op jit(solution)/shard_map/ppermute | solution.py:95
  117.9 12.6 %contrast_layer.1 = (f32[32,128,128]{2,1,0:T(8,128)S(1)}, bf16[22,128,128]{2,1,0:T(8,128)(2,1)S(1)}, bf16[10,128,128]{2,1,0:T(8,128)(2,1)S(1)}, bf16[22,128,128]...) custom-call(s32[16]{0:T(128)S(1)} %copy-done.22, ...), custom_call_target="tpu_custom_call" | custom-call | tf_op jit(solution)/shard_map/contrast_layer/pallas_call | solution.py:689
  139.5 3.4 %collective-permute-done.25 = f32[200,128]{1,0:T(8,128)S(1)} collective-permute-done((f32[200,128]{1,0:T(8,128)S(1)}, f32[200,128]{1,0:T(8,128)S(1)}, u32[]{:S(2)}, u32[]{:S(2)}) %collective-permute-start.25) | collective-permute-done | bytes 102432 | tf_op jit(solution)/shard_map/ppermute | solution.py:95
  142.9 8.5 %collective-permute-done.32 = bf16[22,128,128]{2,1,0:T(8,128)(2,1)S(1)} collective-permute-done((bf16[22,128,128]{2,1,0:T(8,128)(2,1)S(1)}, bf16[22,128,128]{2,1,0:T(8,128)(2,1)S(1)}, u32[]{:S(2)}, u32[]{:S(2)}) %collective-permute-start.32) | collective-permute-done | bytes 720928 | tf_op jit(solution)/shard_map/ppermute | solution.py:95
  154.1 3.2 %collective-permute-start.27 = (bf16[10,128,128]{2,1,0:T(8,128)(2,1)S(1)}, bf16[10,128,128]{2,1,0:T(8,128)(2,1)S(1)}, u32[]{:S(2)}, u32[]{:S(2)}) collective-permute-start(bf16[10,128,128]{2,1,0:T(8,128)(2,1)S(1)} %get-tuple-element.85), channel_id=1, source_target_pairs={{14,0},{15,1},{4,2},{5,3},{2,4},{3,5},{8,6},{9,7},{6,8},{7,9},{12,... | collective-permute-start | bytes 983048 | tf_op jit(solution)/shard_map/ppermute | solution.py:95
  157.3 8.4 %collective-permute-done.27.cross_b = bf16[10,128,128]{2,1,0:T(8,128)(2,1)S(1)} collective-permute-done((bf16[10,128,128]{2,1,0:T(8,128)(2,1)S(1)}, bf16[10,128,128]{2,1,0:T(8,128)(2,1)S(1)}, u32[]{:S(2)}, u32[]{:S(2)}) %collective-permute-start.27) | collective-permute-done | bytes 327712 | tf_op jit(solution)/shard_map/ppermute | solution.py:95
  165.7 4.7 %collective-permute-done.28 = f32[200,128]{1,0:T(8,128)S(1)} collective-permute-done((f32[200,128]{1,0:T(8,128)S(1)}, f32[200,128]{1,0:T(8,128)S(1)}, u32[]{:S(2)}, u32[]{:S(2)}) %collective-permute-start.28) | collective-permute-done | bytes 102432 | tf_op jit(solution)/shard_map/ppermute | solution.py:95
  170.4 6.1 %collective-permute-done.29 = f32[200,128]{1,0:T(8,128)S(1)} collective-permute-done((f32[200,128]{1,0:T(8,128)S(1)}, f32[200,128]{1,0:T(8,128)S(1)}, u32[]{:S(2)}, u32[]{:S(2)}) %collective-permute-start.29) | collective-permute-done | bytes 102432 | tf_op jit(solution)/shard_map/ppermute | solution.py:95
  178.0 11.3 %last_layer.1 = (f32[208,128]{1,0:T(8,128)S(1)}, f32[208,128]{1,0:T(8,128)S(1)}) custom-call(s32[16]{0:T(128)S(1)} %copy-done.22, s32[256]{0:T(256)S(1)} %copy-done.21, s32[32]{0:T(128)S(1)} %copy-done.26, bf16[32,8,128,128]{3,2,1,0:T(8,128)(2,1)S(1)} %bitcast.9, f32[32,128,128]{2,1,0:T(8,128)S(1)} %get-tuple-element.72.own, ...), custom_call_target="tpu_custom_call" | custom-call | tf_op jit(solution)/shard_map/last_layer/pallas_call | solution.py:722
  191.4 4.5 %collective-permute-done.37 = f32[208,128]{1,0:T(8,128)S(1)} collective-permute-done((f32[208,128]{1,0:T(8,128)S(1)}, f32[208,128]{1,0:T(8,128)S(1)}, u32[]{:S(2)}, u32[]{:S(2)}) %collective-permute-start.37) | collective-permute-done | bytes 106528 | tf_op jit(solution)/shard_map/ppermute | solution.py:95
  196.0 4.7 %collective-permute-done.38 = f32[208,128]{1,0:T(8,128)S(1)} collective-permute-done((f32[208,128]{1,0:T(8,128)S(1)}, f32[208,128]{1,0:T(8,128)S(1)}, u32[]{:S(2)}, u32[]{:S(2)}) %collective-permute-start.38) | collective-permute-done | bytes 106528 | tf_op jit(solution)/shard_map/ppermute | solution.py:95
  201.5 5.4 %collective-permute-done.39 = f32[208,128]{1,0:T(8,128)S(1)} collective-permute-done((f32[208,128]{1,0:T(8,128)S(1)}, f32[208,128]{1,0:T(8,128)S(1)}, u32[]{:S(2)}, u32[]{:S(2)}) %collective-permute-start.39) | collective-permute-done | bytes 106528 | tf_op jit(solution)/shard_map/ppermute | solution.py:95
  (175 shorter events, 46.4 us)
Async XLA Ops:
  3.9 15.7 %collective-permute-start.2 = (bf16[16,4096]{1,0:T(8,128)(2,1)S(1)}, bf16[16,4096]{1,0:T(8,128)(2,1)S(1)}, u32[]{:S(2)}, u32[]{:S(2)}) collective-permute-start(bf16[16,4096]{1,0:T(8,128)(2,1)S(1)} %maximum_maximum_fusion.p0), channel_id=1, source_target_pairs={{0,1},{1,0},{2,3},{3,2},{4,5},{5,4},{6,7},{7,6},{8,9},{9,8},{10,11... | collective-permute-start | bytes 393224 | tf_op jit(solution)/shard_map/ppermute | solution.py:95
  4.4 12.6 %collective-permute-start.1 = (bf16[16,4096]{1,0:T(8,128)(2,1)S(1)}, bf16[16,4096]{1,0:T(8,128)(2,1)S(1)}, u32[]{:S(2)}, u32[]{:S(2)}) collective-permute-start(bf16[16,4096]{1,0:T(8,128)(2,1)S(1)} %maximum_maximum_fusion.p0), channel_id=1, source_target_pairs={{0,14},{1,15},{2,4},{3,5},{4,2},{5,3},{6,8},{7,9},{8,6},{9,7},{10,... | collective-permute-start | bytes 393224 | tf_op jit(solution)/shard_map/ppermute | solution.py:95
  10.0 6.9 %collective-permute-start = (bf16[16,4096]{1,0:T(8,128)(2,1)S(1)}, bf16[16,4096]{1,0:T(8,128)(2,1)S(1)}, u32[]{:S(2)}, u32[]{:S(2)}) collective-permute-start(bf16[16,4096]{1,0:T(8,128)(2,1)S(1)} %maximum_maximum_fusion.p0), channel_id=1, source_target_pairs={{0,2},{1,3},{2,0},{3,1},{4,6},{5,7},{6,4},{7,5},{8,10},{9,11},{10,... | collective-permute-start | bytes 393224 | tf_op jit(solution)/shard_map/ppermute | solution.py:95
  29.3 26.3 %collective-permute-start.5 = (bf16[16,128,128]{2,1,0:T(8,128)(2,1)}, bf16[16,128,128]{2,1,0:T(8,128)(2,1)S(1)}, u32[]{:S(2)}, u32[]{:S(2)}) collective-permute-start(bf16[16,128,128]{2,1,0:T(8,128)(2,1)} %get-tuple-element.46.own_a), channel_id=1, source_target_pairs={{0,2},{1,3},{2,0},{3,1},{4,6},{5,7},{6,4},{7,5},{8,10},{9,11},{10,... | collective-permute-start | bytes 1572872 | tf_op jit(solution)/shard_map/ppermute | solution.py:95
  35.1 20.5 %collective-permute-start.8 = (bf16[16,128,128]{2,1,0:T(8,128)(2,1)}, bf16[16,128,128]{2,1,0:T(8,128)(2,1)S(1)}, u32[]{:S(2)}, u32[]{:S(2)}) collective-permute-start(bf16[16,128,128]{2,1,0:T(8,128)(2,1)} %get-tuple-element.50.own_b), channel_id=1, source_target_pairs={{0,14},{1,15},{2,4},{3,5},{4,2},{5,3},{6,8},{7,9},{8,6},{9,7},{10,... | collective-permute-start | bytes 1572872 | tf_op jit(solution)/shard_map/ppermute | solution.py:95
  38.2 27.7 %collective-permute-start.6 = (bf16[16,128,128]{2,1,0:T(8,128)(2,1)}, bf16[16,128,128]{2,1,0:T(8,128)(2,1)S(1)}, u32[]{:S(2)}, u32[]{:S(2)}) collective-permute-start(bf16[16,128,128]{2,1,0:T(8,128)(2,1)} %get-tuple-element.50.own_b), channel_id=1, source_target_pairs={{0,2},{1,3},{2,0},{3,1},{4,6},{5,7},{6,4},{7,5},{8,10},{9,11},{10,... | collective-permute-start | bytes 1572872 | tf_op jit(solution)/shard_map/ppermute | solution.py:95
  38.2 27.7 %collective-permute-start.10 = (bf16[16,128,128]{2,1,0:T(8,128)(2,1)}, bf16[16,128,128]{2,1,0:T(8,128)(2,1)S(1)}, u32[]{:S(2)}, u32[]{:S(2)}) collective-permute-start(bf16[16,128,128]{2,1,0:T(8,128)(2,1)} %get-tuple-element.50.own_b), channel_id=1, source_target_pairs={{0,1},{1,0},{2,3},{3,2},{4,5},{5,4},{6,7},{7,6},{8,9},{9,8},{10,11... | collective-permute-start | bytes 1572872 | tf_op jit(solution)/shard_map/ppermute | solution.py:95
  55.6 14.0 %collective-permute-start.7 = (bf16[16,128,128]{2,1,0:T(8,128)(2,1)S(1)}, bf16[16,128,128]{2,1,0:T(8,128)(2,1)S(1)}, u32[]{:S(2)}, u32[]{:S(2)}) collective-permute-start(bf16[16,128,128]{2,1,0:T(8,128)(2,1)S(1)} %collective-permute-done.5.pair_a), channel_id=1, source_target_pairs={{0,4},{1,5},{2,14},{3,15},{4,8},{5,9},{6,2},{7,3},{8,12},{9,13},{1... | collective-permute-start | bytes 1572872 | tf_op jit(solution)/shard_map/ppermute | solution.py:95
  55.6 14.0 %collective-permute-start.9 = (bf16[16,128,128]{2,1,0:T(8,128)(2,1)}, bf16[16,128,128]{2,1,0:T(8,128)(2,1)S(1)}, u32[]{:S(2)}, u32[]{:S(2)}) collective-permute-start(bf16[16,128,128]{2,1,0:T(8,128)(2,1)} %get-tuple-element.46.own_a), channel_id=1, source_target_pairs={{0,1},{1,0},{2,3},{3,2},{4,5},{5,4},{6,7},{7,6},{8,9},{9,8},{10,11... | collective-permute-start | bytes 1572872 | tf_op jit(solution)/shard_map/ppermute | solution.py:95
  55.6 14.0 %collective-permute-start.11 = (bf16[16,128,128]{2,1,0:T(8,128)(2,1)S(1)}, bf16[16,128,128]{2,1,0:T(8,128)(2,1)S(1)}, u32[]{:S(2)}, u32[]{:S(2)}) collective-permute-start(bf16[16,128,128]{2,1,0:T(8,128)(2,1)S(1)} %collective-permute-done.5.pair_a), channel_id=1, source_target_pairs={{0,1},{1,0},{2,3},{3,2},{4,5},{5,4},{6,7},{7,6},{8,9},{9,8},{10,11... | collective-permute-start | bytes 1572872 | tf_op jit(solution)/shard_map/ppermute | solution.py:95
  84.8 5.9 %collective-permute-start.18 = (bf16[1024,128]{1,0:T(8,128)(2,1)S(1)}, bf16[1024,128]{1,0:T(8,128)(2,1)S(1)}, u32[]{:S(2)}, u32[]{:S(2)}) collective-permute-start(bf16[1024,128]{1,0:T(8,128)(2,1)S(1)} %get-tuple-element.56), channel_id=1, source_target_pairs={{0,1},{1,0},{2,3},{3,2},{4,5},{5,4},{6,7},{7,6},{8,9},{9,8},{10,11... | collective-permute-start | bytes 786440 | tf_op jit(solution)/shard_map/ppermute | solution.py:95
  86.5 11.2 %collective-permute-start.17 = (bf16[1024,128]{1,0:T(8,128)(2,1)S(1)}, bf16[1024,128]{1,0:T(8,128)(2,1)S(1)}, u32[]{:S(2)}, u32[]{:S(2)}) collective-permute-start(bf16[1024,128]{1,0:T(8,128)(2,1)S(1)} %get-tuple-element.86), channel_id=1, source_target_pairs={{14,0},{15,1},{4,2},{5,3},{2,4},{3,5},{8,6},{9,7},{6,8},{7,9},{12,... | collective-permute-start | bytes 786440 | tf_op jit(solution)/shard_map/ppermute | solution.py:95
  88.7 13.7 %collective-permute-start.16 = (bf16[1024,128]{1,0:T(8,128)(2,1)S(1)}, bf16[1024,128]{1,0:T(8,128)(2,1)S(1)}, u32[]{:S(2)}, u32[]{:S(2)}) collective-permute-start(bf16[1024,128]{1,0:T(8,128)(2,1)S(1)} %get-tuple-element.87), channel_id=1, source_target_pairs={{0,2},{1,3},{2,0},{3,1},{4,6},{5,7},{6,4},{7,5},{8,10},{9,11},{10,... | collective-permute-start | bytes 786440 | tf_op jit(solution)/shard_map/ppermute | solution.py:95
  103.0 13.0 %collective-permute-start.19 = (bf16[1024,128]{1,0:T(8,128)(2,1)S(1)}, bf16[1024,128]{1,0:T(8,128)(2,1)S(1)}, u32[]{:S(2)}, u32[]{:S(2)}) collective-permute-start(bf16[1024,128]{1,0:T(8,128)(2,1)S(1)} %get-tuple-element.60), channel_id=1, source_target_pairs={{0,2},{1,3},{2,0},{3,1},{4,6},{5,7},{6,4},{7,5},{8,10},{9,11},{10,... | collective-permute-start | bytes 786440 | tf_op jit(solution)/shard_map/ppermute | solution.py:95
  103.0 12.9 %collective-permute-start.20 = (bf16[1024,128]{1,0:T(8,128)(2,1)S(1)}, bf16[1024,128]{1,0:T(8,128)(2,1)S(1)}, u32[]{:S(2)}, u32[]{:S(2)}) collective-permute-start(bf16[1024,128]{1,0:T(8,128)(2,1)S(1)} %get-tuple-element.60), channel_id=1, source_target_pairs={{0,14},{1,15},{2,4},{3,5},{4,2},{5,3},{6,8},{7,9},{8,6},{9,7},{10,... | collective-permute-start | bytes 786440 | tf_op jit(solution)/shard_map/ppermute | solution.py:95
  105.7 10.8 %collective-permute-start.21 = (bf16[1024,128]{1,0:T(8,128)(2,1)S(1)}, bf16[1024,128]{1,0:T(8,128)(2,1)S(1)}, u32[]{:S(2)}, u32[]{:S(2)}) collective-permute-start(bf16[1024,128]{1,0:T(8,128)(2,1)S(1)} %get-tuple-element.60), channel_id=1, source_target_pairs={{0,1},{1,0},{2,3},{3,2},{4,5},{5,4},{6,7},{7,6},{8,9},{9,8},{10,11... | collective-permute-start | bytes 786440 | tf_op jit(solution)/shard_map/ppermute | solution.py:95
  133.0 18.5 %collective-permute-start.32 = (bf16[22,128,128]{2,1,0:T(8,128)(2,1)S(1)}, bf16[22,128,128]{2,1,0:T(8,128)(2,1)S(1)}, u32[]{:S(2)}, u32[]{:S(2)}) collective-permute-start(bf16[22,128,128]{2,1,0:T(8,128)(2,1)S(1)} %add_convert_fusion.1), channel_id=1, source_target_pairs={{4,0},{5,1},{14,2},{15,3},{8,4},{9,5},{2,6},{3,7},{12,8},{13,9},{6... | collective-permute-start | bytes 2162696 | tf_op jit(solution)/shard_map/ppermute | solution.py:95
  137.1 5.8 %collective-permute-start.25 = (f32[200,128]{1,0:T(8,128)S(1)}, f32[200,128]{1,0:T(8,128)S(1)}, u32[]{:S(2)}, u32[]{:S(2)}) collective-permute-start(f32[200,128]{1,0:T(8,128)S(1)} %add.69), channel_id=1, source_target_pairs={{0,2},{1,3},{2,0},{3,1},{4,6},{5,7},{6,4},{7,5},{8,10},{9,11},{10,... | collective-permute-start | bytes 307208 | tf_op jit(solution)/shard_map/ppermute | solution.py:95
  137.5 14.4 %collective-permute-start.33 = (bf16[10,128,128]{2,1,0:T(8,128)(2,1)S(1)}, bf16[10,128,128]{2,1,0:T(8,128)(2,1)S(1)}, u32[]{:S(2)}, u32[]{:S(2)}) collective-permute-start(bf16[10,128,128]{2,1,0:T(8,128)(2,1)S(1)} %get-tuple-element.84), channel_id=1, source_target_pairs={{0,2},{1,3},{2,0},{3,1},{4,6},{5,7},{6,4},{7,5},{8,10},{9,11},{10,... | collective-permute-start | bytes 983048 | tf_op jit(solution)/shard_map/ppermute | solution.py:95
  139.5 38.4 %collective-permute-start.35 = (bf16[32,128,128]{2,1,0:T(8,128)(2,1)S(1)}, bf16[32,128,128]{2,1,0:T(8,128)(2,1)S(1)}, u32[]{:S(2)}, u32[]{:S(2)}) collective-permute-start(bf16[32,128,128]{2,1,0:T(8,128)(2,1)S(1)} %get-tuple-element.78), channel_id=1, source_target_pairs={{0,1},{1,0},{2,3},{3,2},{4,5},{5,4},{6,7},{7,6},{8,9},{9,8},{10,11... | collective-permute-start | bytes 3145736 | tf_op jit(solution)/shard_map/ppermute | solution.py:95
  151.9 26.0 %collective-permute-start.34 = (bf16[22,128,128]{2,1,0:T(8,128)(2,1)S(1)}, bf16[22,128,128]{2,1,0:T(8,128)(2,1)S(1)}, u32[]{:S(2)}, u32[]{:S(2)}) collective-permute-start(bf16[22,128,128]{2,1,0:T(8,128)(2,1)S(1)} %add_convert_fusion), channel_id=1, source_target_pairs={{0,2},{1,3},{2,0},{3,1},{4,6},{5,7},{6,4},{7,5},{8,10},{9,11},{10,... | collective-permute-start | bytes 2162696 | tf_op jit(solution)/shard_map/ppermute | solution.py:95
  154.1 11.6 %collective-permute-start.27 = (bf16[10,128,128]{2,1,0:T(8,128)(2,1)S(1)}, bf16[10,128,128]{2,1,0:T(8,128)(2,1)S(1)}, u32[]{:S(2)}, u32[]{:S(2)}) collective-permute-start(bf16[10,128,128]{2,1,0:T(8,128)(2,1)S(1)} %get-tuple-element.85), channel_id=1, source_target_pairs={{14,0},{15,1},{4,2},{5,3},{2,4},{3,5},{8,6},{9,7},{6,8},{7,9},{12,... | collective-permute-start | bytes 983048 | tf_op jit(solution)/shard_map/ppermute | solution.py:95
  170.3 6.2 %collective-permute-start.29 = (f32[200,128]{1,0:T(8,128)S(1)}, f32[200,128]{1,0:T(8,128)S(1)}, u32[]{:S(2)}, u32[]{:S(2)}) collective-permute-start(f32[200,128]{1,0:T(8,128)S(1)} %add.72), channel_id=1, source_target_pairs={{0,8},{1,9},{2,10},{3,11},{4,12},{5,13},{6,14},{7,15},{8,0},{9,1},... | collective-permute-start | bytes 307208 | tf_op jit(solution)/shard_map/ppermute | solution.py:95
  200.7 6.3 %collective-permute-start.39 = (f32[208,128]{1,0:T(8,128)S(1)}, f32[208,128]{1,0:T(8,128)S(1)}, u32[]{:S(2)}, u32[]{:S(2)}) collective-permute-start(f32[208,128]{1,0:T(8,128)S(1)} %add.80), channel_id=1, source_target_pairs={{0,8},{1,9},{2,10},{3,11},{4,12},{5,13},{6,14},{7,15},{8,0},{9,1},... | collective-permute-start | bytes 319496 | tf_op jit(solution)/shard_map/ppermute | solution.py:95
  (46 other events, 938.4 us)

commit v6 on v5

--- a/solution.py
+++ b/solution.py
@@ -551,7 +551,7 @@
     assert feats < PACK_ROWS - 3 and kinds == PACK_ROWS and layers == 2 and 4 * triplets == hits
     assert count % 4 == 0
     groups = blocks // GROUP
-    cut, back_cut = blocks // 2, blocks * 11 // 16
+    cut, back_cut = blocks // 2, blocks * 9 // 16
     place = lax.dynamic_slice_in_dim(place_table(), lax.axis_index("phi") & 3, 1, 0).reshape(-1)
     sends_pair = place[0] == place[1]
 
@@ -712,11 +712,11 @@
     relayed = send(ret_ca, turned(relay_links(count)))
     ret_pb, ret_cb = join_extra(ret_pb, ret_cb, got_b, sends_pair)
     from_pair_b = send(ret_pb, pair_links(count))
-    from_cross_b = send(ret_cb, turned(cross_links(count)))
+    from_cross_b = send(after(ret_cb, relayed), turned(cross_links(count)))
     ret_pa = (ret_pa.astype(F32) + relayed.astype(F32)).astype(BF16)
     part_1 = first_sums(kept_1, given_1)
     from_pair_a = send(after(ret_pa, from_pair_b, part_1), pair_links(count))
-    part_1, back_1 = last_sums(after(part_1, from_cross_b))
+    part_1, back_1 = last_sums(part_1)
     own_1 = after(own_1, part_1, back_1)
 
     kept_0, given_0 = pl.pallas_call(

time: 211 us -> 208 us (0.986)
  starting transfers between devices: 29.5 us -> 27.3 us
    ppermute x41, starting transfers between devices: 29.5 us -> 27.3 us  [send(): return lax.ppermute(value, 'phi', links)]
  transfers between devices with their start and end apart: 41 -> 41, of which waited for: 24 -> 23; matrix products, arithmetic and copies ran while one was open for 5% -> 5% of each run, Pallas kernels for 3% -> 3%
where the time goes in v6:
time: 208 us
  waiting for transfers between devices  109 us (52%)
  Pallas kernels  54.8 us (26%)
  starting transfers between devices  27.3 us (13%)
  other arithmetic  8.12 us (4%)
  local copies, waits for them, and re-layouts  6.03 us (3%)
  between operations  2.8 us (1%)
    ppermute x41, waiting for transfers between devices, send(): return lax.ppermute(value, 'phi', links)  109 us
    ppermute x41, starting transfers between devices, send(): return lax.ppermute(value, 'phi', links)  27.3 us
    pallas_call x1, Pallas kernels, body(): pl.pallas_call(lambda *refs: contrast_layer_kernel(row_bits, *refs), out_...  12.5 us
    pallas_call x1, Pallas kernels, body(): pl.pallas_call(last_layer_kernel, out_shape=(half_0, half_0), in_specs=[s...  11.4 us
    pallas_call x1, Pallas kernels, body(): pl.pallas_call(first_layer_kernel, out_shape=(blocked,) * 4 + (head, tail...  8.88 us
    pallas_call x1, Pallas kernels, body(): pl.pallas_call(next_layer_kernel, out_shape=(blocked,) * 3, in_specs=[sme...  6.85 us
    pallas_call x1, Pallas kernels, body(): pl.pallas_call(lambda *refs: gather_kernel(row_bits, *refs), out_shape=(t...  6.14 us
    pallas_call x1, Pallas kernels, body(): pl.pallas_call(lambda *refs: own_rows_kernel(row_bits, *refs), out_shape=...  5.04 us
  transfers between devices with their start and end apart: 41, of which 23 were waited for; matrix products, arithmetic and copies ran while one was open for 5% of the time, Pallas kernels for 3%

profile of v6, /device:TPU:0, one launch (start us, length us, event | category | flops | bytes accessed | tf_op | source)
XLA Modules:
  0.0 207.7 jit_solution(17950900736653164558)
XLA Ops:
  4.4 5.6 %collective-permute-start.1 = (bf16[16,4096]{1,0:T(8,128)(2,1)S(1)}, bf16[16,4096]{1,0:T(8,128)(2,1)S(1)}, u32[]{:S(2)}, u32[]{:S(2)}) collective-permute-start(bf16[16,4096]{1,0:T(8,128)(2,1)S(1)} %maximum_maximum_fusion.p0), channel_id=1, source_target_pairs={{0,14},{1,15},{2,4},{3,5},{4,2},{5,3},{6,8},{7,9},{8,6},{9,7},{10,... | collective-permute-start | bytes 393224 | tf_op jit(solution)/shard_map/ppermute | solution.py:95
  12.7 4.2 %collective-permute-done.p1 = bf16[16,4096]{1,0:T(8,128)(2,1)S(1)} collective-permute-done((bf16[16,4096]{1,0:T(8,128)(2,1)S(1)}, bf16[16,4096]{1,0:T(8,128)(2,1)S(1)}, u32[]{:S(2)}, u32[]{:S(2)}) %collective-permute-start) | collective-permute-done | bytes 131104 | tf_op jit(solution)/shard_map/ppermute | solution.py:95
  20.3 8.9 %first_layer.1 = (bf16[32,128,128]{2,1,0:T(8,128)(2,1)}, bf16[32,128,128]{2,1,0:T(8,128)(2,1)}, bf16[32,128,128]{2,1,0:T(8,128)(2,1)}, bf16[32,128,128]{2,1,0:T(...) custom-call(s32[16]{0:T(128)} %get-tuple-element.94.place.refs_0_, s32[256]{0:T(256)} %reshape.135.src.refs_1_, ...), custom_call_target="tpu_custom_call" | custom-call | tf_op jit(solution)/shard_map/first_layer/pallas_call | solution.py:582
  31.2 3.8 %sort.7 = s32[1024,10]{0,1:T(8,128)S(1)} sort(s32[1024,10]{0,1:T(8,128)S(1)} %select_bitcast_fusion), dimensions={0}, to_apply=%region_0.1 | sort | flops 143360 | bytes 81920 | tf_op jit(solution)/shard_map/sort | solution.py:599
  35.1 3.1 %collective-permute-start.8 = (bf16[16,128,128]{2,1,0:T(8,128)(2,1)S(1)}, bf16[16,128,128]{2,1,0:T(8,128)(2,1)S(1)}, u32[]{:S(2)}, u32[]{:S(2)}) collective-permute-start(bf16[16,128,128]{2,1,0:T(8,128)(2,1)S(1)} %copy-done.20), channel_id=1, source_target_pairs={{0,14},{1,15},{2,4},{3,5},{4,2},{5,3},{6,8},{7,9},{8,6},{9,7},{10,... | collective-permute-start | bytes 1572872 | tf_op jit(solution)/shard_map/ppermute | solution.py:95
  38.2 17.4 %collective-permute-done.5.pair_a = bf16[16,128,128]{2,1,0:T(8,128)(2,1)S(1)} collective-permute-done((bf16[16,128,128]{2,1,0:T(8,128)(2,1)}, bf16[16,128,128]{2,1,0:T(8,128)(2,1)S(1)}, u32[]{:S(2)}, u32[]{:S(2)}) %collective-permute-start.5) | collective-permute-done | bytes 524320 | tf_op jit(solution)/shard_map/ppermute | solution.py:95
  56.1 9.8 %collective-permute-done.6.pair_b = bf16[16,128,128]{2,1,0:T(8,128)(2,1)S(1)} collective-permute-done((bf16[16,128,128]{2,1,0:T(8,128)(2,1)S(1)}, bf16[16,128,128]{2,1,0:T(8,128)(2,1)S(1)}, u32[]{:S(2)}, u32[]{:S(2)}) %collective-permute-start.6) | collective-permute-done | bytes 524320 | tf_op jit(solution)/shard_map/ppermute | solution.py:95
  66.5 3.1 %collective-permute-done.7.cross_a = bf16[16,128,128]{2,1,0:T(8,128)(2,1)S(1)} collective-permute-done((bf16[16,128,128]{2,1,0:T(8,128)(2,1)S(1)}, bf16[16,128,128]{2,1,0:T(8,128)(2,1)S(1)}, u32[]{:S(2)}, u32[]{:S(2)}) %collective-permute-start.7) | collective-permute-done | bytes 524320 | tf_op jit(solution)/shard_map/ppermute | solution.py:95
  71.5 6.9 %next_layer.1 = (bf16[32,128,128]{2,1,0:T(8,128)(2,1)S(1)}, bf16[32,128,128]{2,1,0:T(8,128)(2,1)S(1)}, bf16[32,128,128]{2,1,0:T(8,128)(2,1)S(1)}) custom-call(s32[16]{0:T(128)S(1)} %copy-done.22, s32[256]{0:T(256)S(1)} %copy-done.21, s32[32]{0:T(128)S(1)} %copy-done.26, bf16[32,8,128,128]{3,2,1,0:T(8,128)(2,1)} %tiles_hbm.5, ...), custom_call_target="tpu_custom_call" | custom-call | tf_op jit(solution)/shard_map/next_layer/pallas_call | solution.py:615
  78.4 6.1 %gather_rows.1 = (bf16[1024,128]{1,0:T(8,128)(2,1)S(1)}, bf16[1024,128]{1,0:T(8,128)(2,1)S(1)}, bf16[1024,128]{1,0:T(8,128)(2,1)S(1)}, bf16[1024,128]{1,0:T(8,128)(2,1)S(1)}, bf16[1024,128]{1,0:T(8,128)(2,1)S(1)}) custom-call(s32[10240]{0:T(1024)S(1)} %reshape.141.refs_0_.refs_3_, s32[10]{0:T(128)S(1)} %reshape.142.refs_1_.refs_4_, ...), custom_call_target="tpu_custom_call" | custom-call | tf_op jit(solution)/shard_map/gather_rows/pallas_call | solution.py:633
  90.5 7.1 %collective-permute-done.17.cross = bf16[1024,128]{1,0:T(8,128)(2,1)S(1)} collective-permute-done((bf16[1024,128]{1,0:T(8,128)(2,1)S(1)}, bf16[1024,128]{1,0:T(8,128)(2,1)S(1)}, u32[]{:S(2)}, u32[]{:S(2)}) %collective-permute-start.17) | collective-permute-done | bytes 262176 | tf_op jit(solution)/shard_map/ppermute | solution.py:95
  97.6 4.7 %collective-permute-done.16.pair = bf16[1024,128]{1,0:T(8,128)(2,1)S(1)} collective-permute-done((bf16[1024,128]{1,0:T(8,128)(2,1)S(1)}, bf16[1024,128]{1,0:T(8,128)(2,1)S(1)}, u32[]{:S(2)}, u32[]{:S(2)}) %collective-permute-start.16) | collective-permute-done | bytes 262176 | tf_op jit(solution)/shard_map/ppermute | solution.py:95
  103.0 2.6 %collective-permute-start.20 = (bf16[1024,128]{1,0:T(8,128)(2,1)S(1)}, bf16[1024,128]{1,0:T(8,128)(2,1)S(1)}, u32[]{:S(2)}, u32[]{:S(2)}) collective-permute-start(bf16[1024,128]{1,0:T(8,128)(2,1)S(1)} %get-tuple-element.60), channel_id=1, source_target_pairs={{0,14},{1,15},{2,4},{3,5},{4,2},{5,3},{6,8},{7,9},{8,6},{9,7},{10,... | collective-permute-start | bytes 786440 | tf_op jit(solution)/shard_map/ppermute | solution.py:95
  105.6 5.0 %own_rows.1.refs_6_ = f32[4096,128]{1,0:T(8,128)S(1)} custom-call(s32[10240]{0:T(1024)S(1)} %reshape.141.refs_0_.refs_3_, s32[10]{0:T(128)S(1)} %reshape.142.refs_1_.refs_4_, s32[1024]{0:T(1024)S(1)} %copy-done.23, f32[1032,128]{1,0:T(8,128)S(1)} %get-tuple-element.58.refs_3_, f32[1024,128]{1,0:T(8,128)S(1)} %get-tuple-element.59.refs_4_), custom_call_target="tpu_custom_call" | custom-call | tf_op jit(solution)/shard_map/own_rows/pallas_call | solution.py:672
  110.6 5.4 %collective-permute-done.19.refs_7_ = bf16[1024,128]{1,0:T(8,128)(2,1)S(1)} collective-permute-done((bf16[1024,128]{1,0:T(8,128)(2,1)S(1)}, bf16[1024,128]{1,0:T(8,128)(2,1)S(1)}, u32[]{:S(2)}, u32[]{:S(2)}) %collective-permute-start.19) | collective-permute-done | bytes 262176 | tf_op jit(solution)/shard_map/ppermute | solution.py:95
  118.0 12.5 %contrast_layer.1 = (f32[32,128,128]{2,1,0:T(8,128)S(1)}, bf16[18,128,128]{2,1,0:T(8,128)(2,1)S(1)}, bf16[14,128,128]{2,1,0:T(8,128)(2,1)S(1)}, bf16[18,128,128]...) custom-call(s32[16]{0:T(128)S(1)} %copy-done.22, ...), custom_call_target="tpu_custom_call" | custom-call | tf_op jit(solution)/shard_map/contrast_layer/pallas_call | solution.py:689
  137.4 12.8 %collective-permute-done.25 = f32[200,128]{1,0:T(8,128)S(1)} collective-permute-done((f32[200,128]{1,0:T(8,128)S(1)}, f32[200,128]{1,0:T(8,128)S(1)}, u32[]{:S(2)}, u32[]{:S(2)}) %collective-permute-start.25) | collective-permute-done | bytes 102432 | tf_op jit(solution)/shard_map/ppermute | solution.py:95
  151.0 2.8 %collective-permute-start.34 = (bf16[14,128,128]{2,1,0:T(8,128)(2,1)S(1)}, bf16[14,128,128]{2,1,0:T(8,128)(2,1)S(1)}, u32[]{:S(2)}, u32[]{:S(2)}) collective-permute-start(bf16[14,128,128]{2,1,0:T(8,128)(2,1)S(1)} %get-tuple-element.77), channel_id=1, source_target_pairs={{14,0},{15,1},{4,2},{5,3},{2,4},{3,5},{8,6},{9,7},{6,8},{7,9},{12,... | collective-permute-start | bytes 1376264 | tf_op jit(solution)/shard_map/ppermute | solution.py:95
  154.1 12.1 %collective-permute-done.26 = f32[200,128]{1,0:T(8,128)S(1)} collective-permute-done((f32[200,128]{1,0:T(8,128)S(1)}, f32[200,128]{1,0:T(8,128)S(1)}, u32[]{:S(2)}, u32[]{:S(2)}) %collective-permute-start.26) | collective-permute-done | bytes 102432 | tf_op jit(solution)/shard_map/ppermute | solution.py:95
  166.9 6.0 %collective-permute-done.27 = f32[200,128]{1,0:T(8,128)S(1)} collective-permute-done((f32[200,128]{1,0:T(8,128)S(1)}, f32[200,128]{1,0:T(8,128)S(1)}, u32[]{:S(2)}, u32[]{:S(2)}) %collective-permute-start.27) | collective-permute-done | bytes 102432 | tf_op jit(solution)/shard_map/ppermute | solution.py:95
  175.5 11.4 %last_layer.1 = (f32[208,128]{1,0:T(8,128)S(1)}, f32[208,128]{1,0:T(8,128)S(1)}) custom-call(s32[16]{0:T(128)S(1)} %copy-done.22, s32[256]{0:T(256)S(1)} %copy-done.21, s32[32]{0:T(128)S(1)} %copy-done.26, bf16[32,8,128,128]{3,2,1,0:T(8,128)(2,1)S(1)} %bitcast.9, f32[32,128,128]{2,1,0:T(8,128)S(1)} %get-tuple-element.69.own, ...), custom_call_target="tpu_custom_call" | custom-call | tf_op jit(solution)/shard_map/last_layer/pallas_call | solution.py:722
  188.8 4.6 %collective-permute-done.37 = f32[208,128]{1,0:T(8,128)S(1)} collective-permute-done((f32[208,128]{1,0:T(8,128)S(1)}, f32[208,128]{1,0:T(8,128)S(1)}, u32[]{:S(2)}, u32[]{:S(2)}) %collective-permute-start.37) | collective-permute-done | bytes 106528 | tf_op jit(solution)/shard_map/ppermute | solution.py:95
  193.8 4.3 %collective-permute-done.38 = f32[208,128]{1,0:T(8,128)S(1)} collective-permute-done((f32[208,128]{1,0:T(8,128)S(1)}, f32[208,128]{1,0:T(8,128)S(1)}, u32[]{:S(2)}, u32[]{:S(2)}) %collective-permute-start.38) | collective-permute-done | bytes 106528 | tf_op jit(solution)/shard_map/ppermute | solution.py:95
  198.9 5.9 %collective-permute-done.39 = f32[208,128]{1,0:T(8,128)S(1)} collective-permute-done((f32[208,128]{1,0:T(8,128)S(1)}, f32[208,128]{1,0:T(8,128)S(1)}, u32[]{:S(2)}, u32[]{:S(2)}) %collective-permute-start.39) | collective-permute-done | bytes 106528 | tf_op jit(solution)/shard_map/ppermute | solution.py:95
  (175 shorter events, 38.7 us)
Async XLA Ops:
  3.9 15.7 %collective-permute-start.2 = (bf16[16,4096]{1,0:T(8,128)(2,1)S(1)}, bf16[16,4096]{1,0:T(8,128)(2,1)S(1)}, u32[]{:S(2)}, u32[]{:S(2)}) collective-permute-start(bf16[16,4096]{1,0:T(8,128)(2,1)S(1)} %maximum_maximum_fusion.p0), channel_id=1, source_target_pairs={{0,1},{1,0},{2,3},{3,2},{4,5},{5,4},{6,7},{7,6},{8,9},{9,8},{10,11... | collective-permute-start | bytes 393224 | tf_op jit(solution)/shard_map/ppermute | solution.py:95
  4.4 12.6 %collective-permute-start.1 = (bf16[16,4096]{1,0:T(8,128)(2,1)S(1)}, bf16[16,4096]{1,0:T(8,128)(2,1)S(1)}, u32[]{:S(2)}, u32[]{:S(2)}) collective-permute-start(bf16[16,4096]{1,0:T(8,128)(2,1)S(1)} %maximum_maximum_fusion.p0), channel_id=1, source_target_pairs={{0,14},{1,15},{2,4},{3,5},{4,2},{5,3},{6,8},{7,9},{8,6},{9,7},{10,... | collective-permute-start | bytes 393224 | tf_op jit(solution)/shard_map/ppermute | solution.py:95
  10.0 6.9 %collective-permute-start = (bf16[16,4096]{1,0:T(8,128)(2,1)S(1)}, bf16[16,4096]{1,0:T(8,128)(2,1)S(1)}, u32[]{:S(2)}, u32[]{:S(2)}) collective-permute-start(bf16[16,4096]{1,0:T(8,128)(2,1)S(1)} %maximum_maximum_fusion.p0), channel_id=1, source_target_pairs={{0,2},{1,3},{2,0},{3,1},{4,6},{5,7},{6,4},{7,5},{8,10},{9,11},{10,... | collective-permute-start | bytes 393224 | tf_op jit(solution)/shard_map/ppermute | solution.py:95
  29.3 26.3 %collective-permute-start.5 = (bf16[16,128,128]{2,1,0:T(8,128)(2,1)}, bf16[16,128,128]{2,1,0:T(8,128)(2,1)S(1)}, u32[]{:S(2)}, u32[]{:S(2)}) collective-permute-start(bf16[16,128,128]{2,1,0:T(8,128)(2,1)} %get-tuple-element.46.own_a), channel_id=1, source_target_pairs={{0,2},{1,3},{2,0},{3,1},{4,6},{5,7},{6,4},{7,5},{8,10},{9,11},{10,... | collective-permute-start | bytes 1572872 | tf_op jit(solution)/shard_map/ppermute | solution.py:95
  35.1 20.5 %collective-permute-start.8 = (bf16[16,128,128]{2,1,0:T(8,128)(2,1)S(1)}, bf16[16,128,128]{2,1,0:T(8,128)(2,1)S(1)}, u32[]{:S(2)}, u32[]{:S(2)}) collective-permute-start(bf16[16,128,128]{2,1,0:T(8,128)(2,1)S(1)} %copy-done.20), channel_id=1, source_target_pairs={{0,14},{1,15},{2,4},{3,5},{4,2},{5,3},{6,8},{7,9},{8,6},{9,7},{10,... | collective-permute-start | bytes 1572872 | tf_op jit(solution)/shard_map/ppermute | solution.py:95
  38.2 27.7 %collective-permute-start.6 = (bf16[16,128,128]{2,1,0:T(8,128)(2,1)S(1)}, bf16[16,128,128]{2,1,0:T(8,128)(2,1)S(1)}, u32[]{:S(2)}, u32[]{:S(2)}) collective-permute-start(bf16[16,128,128]{2,1,0:T(8,128)(2,1)S(1)} %copy-done.20), channel_id=1, source_target_pairs={{0,2},{1,3},{2,0},{3,1},{4,6},{5,7},{6,4},{7,5},{8,10},{9,11},{10,... | collective-permute-start | bytes 1572872 | tf_op jit(solution)/shard_map/ppermute | solution.py:95
  38.2 27.7 %collective-permute-start.10 = (bf16[16,128,128]{2,1,0:T(8,128)(2,1)S(1)}, bf16[16,128,128]{2,1,0:T(8,128)(2,1)S(1)}, u32[]{:S(2)}, u32[]{:S(2)}) collective-permute-start(bf16[16,128,128]{2,1,0:T(8,128)(2,1)S(1)} %copy-done.20), channel_id=1, source_target_pairs={{0,1},{1,0},{2,3},{3,2},{4,5},{5,4},{6,7},{7,6},{8,9},{9,8},{10,11... | collective-permute-start | bytes 1572872 | tf_op jit(solution)/shard_map/ppermute | solution.py:95
  55.6 14.0 %collective-permute-start.7 = (bf16[16,128,128]{2,1,0:T(8,128)(2,1)S(1)}, bf16[16,128,128]{2,1,0:T(8,128)(2,1)S(1)}, u32[]{:S(2)}, u32[]{:S(2)}) collective-permute-start(bf16[16,128,128]{2,1,0:T(8,128)(2,1)S(1)} %collective-permute-done.5.pair_a), channel_id=1, source_target_pairs={{0,4},{1,5},{2,14},{3,15},{4,8},{5,9},{6,2},{7,3},{8,12},{9,13},{1... | collective-permute-start | bytes 1572872 | tf_op jit(solution)/shard_map/ppermute | solution.py:95
  55.6 14.0 %collective-permute-start.9 = (bf16[16,128,128]{2,1,0:T(8,128)(2,1)S(1)}, bf16[16,128,128]{2,1,0:T(8,128)(2,1)S(1)}, u32[]{:S(2)}, u32[]{:S(2)}) collective-permute-start(bf16[16,128,128]{2,1,0:T(8,128)(2,1)S(1)} %copy-done.19), channel_id=1, source_target_pairs={{0,1},{1,0},{2,3},{3,2},{4,5},{5,4},{6,7},{7,6},{8,9},{9,8},{10,11... | collective-permute-start | bytes 1572872 | tf_op jit(solution)/shard_map/ppermute | solution.py:95
  55.6 14.0 %collective-permute-start.11 = (bf16[16,128,128]{2,1,0:T(8,128)(2,1)S(1)}, bf16[16,128,128]{2,1,0:T(8,128)(2,1)S(1)}, u32[]{:S(2)}, u32[]{:S(2)}) collective-permute-start(bf16[16,128,128]{2,1,0:T(8,128)(2,1)S(1)} %collective-permute-done.5.pair_a), channel_id=1, source_target_pairs={{0,1},{1,0},{2,3},{3,2},{4,5},{5,4},{6,7},{7,6},{8,9},{9,8},{10,11... | collective-permute-start | bytes 1572872 | tf_op jit(solution)/shard_map/ppermute | solution.py:95
  86.3 11.2 %collective-permute-start.17 = (bf16[1024,128]{1,0:T(8,128)(2,1)S(1)}, bf16[1024,128]{1,0:T(8,128)(2,1)S(1)}, u32[]{:S(2)}, u32[]{:S(2)}) collective-permute-start(bf16[1024,128]{1,0:T(8,128)(2,1)S(1)} %get-tuple-element.86), channel_id=1, source_target_pairs={{14,0},{15,1},{4,2},{5,3},{2,4},{3,5},{8,6},{9,7},{6,8},{7,9},{12,... | collective-permute-start | bytes 786440 | tf_op jit(solution)/shard_map/ppermute | solution.py:95
  88.4 13.9 %collective-permute-start.16 = (bf16[1024,128]{1,0:T(8,128)(2,1)S(1)}, bf16[1024,128]{1,0:T(8,128)(2,1)S(1)}, u32[]{:S(2)}, u32[]{:S(2)}) collective-permute-start(bf16[1024,128]{1,0:T(8,128)(2,1)S(1)} %get-tuple-element.87), channel_id=1, source_target_pairs={{0,2},{1,3},{2,0},{3,1},{4,6},{5,7},{6,4},{7,5},{8,10},{9,11},{10,... | collective-permute-start | bytes 786440 | tf_op jit(solution)/shard_map/ppermute | solution.py:95
  102.9 13.2 %collective-permute-start.19 = (bf16[1024,128]{1,0:T(8,128)(2,1)S(1)}, bf16[1024,128]{1,0:T(8,128)(2,1)S(1)}, u32[]{:S(2)}, u32[]{:S(2)}) collective-permute-start(bf16[1024,128]{1,0:T(8,128)(2,1)S(1)} %get-tuple-element.60), channel_id=1, source_target_pairs={{0,2},{1,3},{2,0},{3,1},{4,6},{5,7},{6,4},{7,5},{8,10},{9,11},{10,... | collective-permute-start | bytes 786440 | tf_op jit(solution)/shard_map/ppermute | solution.py:95
  103.0 13.1 %collective-permute-start.20 = (bf16[1024,128]{1,0:T(8,128)(2,1)S(1)}, bf16[1024,128]{1,0:T(8,128)(2,1)S(1)}, u32[]{:S(2)}, u32[]{:S(2)}) collective-permute-start(bf16[1024,128]{1,0:T(8,128)(2,1)S(1)} %get-tuple-element.60), channel_id=1, source_target_pairs={{0,14},{1,15},{2,4},{3,5},{4,2},{5,3},{6,8},{7,9},{8,6},{9,7},{10,... | collective-permute-start | bytes 786440 | tf_op jit(solution)/shard_map/ppermute | solution.py:95
  105.6 11.0 %collective-permute-start.21 = (bf16[1024,128]{1,0:T(8,128)(2,1)S(1)}, bf16[1024,128]{1,0:T(8,128)(2,1)S(1)}, u32[]{:S(2)}, u32[]{:S(2)}) collective-permute-start(bf16[1024,128]{1,0:T(8,128)(2,1)S(1)} %get-tuple-element.60), channel_id=1, source_target_pairs={{0,1},{1,0},{2,3},{3,2},{4,5},{5,4},{6,7},{7,6},{8,9},{9,8},{10,11... | collective-permute-start | bytes 786440 | tf_op jit(solution)/shard_map/ppermute | solution.py:95
  132.8 17.4 %collective-permute-start.30 = (bf16[18,128,128]{2,1,0:T(8,128)(2,1)S(1)}, bf16[18,128,128]{2,1,0:T(8,128)(2,1)S(1)}, u32[]{:S(2)}, u32[]{:S(2)}) collective-permute-start(bf16[18,128,128]{2,1,0:T(8,128)(2,1)S(1)} %add_convert_fusion.1), channel_id=1, source_target_pairs={{4,0},{5,1},{14,2},{15,3},{8,4},{9,5},{2,6},{3,7},{12,8},{13,9},{6... | collective-permute-start | bytes 1769480 | tf_op jit(solution)/shard_map/ppermute | solution.py:95
  135.0 15.6 %collective-permute-start.32 = (bf16[14,128,128]{2,1,0:T(8,128)(2,1)S(1)}, bf16[14,128,128]{2,1,0:T(8,128)(2,1)S(1)}, u32[]{:S(2)}, u32[]{:S(2)}) collective-permute-start(bf16[14,128,128]{2,1,0:T(8,128)(2,1)S(1)} %get-tuple-element.85), channel_id=1, source_target_pairs={{0,2},{1,3},{2,0},{3,1},{4,6},{5,7},{6,4},{7,5},{8,10},{9,11},{10,... | collective-permute-start | bytes 1376264 | tf_op jit(solution)/shard_map/ppermute | solution.py:95
  135.1 39.2 %collective-permute-start.35 = (bf16[32,128,128]{2,1,0:T(8,128)(2,1)S(1)}, bf16[32,128,128]{2,1,0:T(8,128)(2,1)S(1)}, u32[]{:S(2)}, u32[]{:S(2)}) collective-permute-start(bf16[32,128,128]{2,1,0:T(8,128)(2,1)S(1)} %get-tuple-element.78), channel_id=1, source_target_pairs={{0,1},{1,0},{2,3},{3,2},{4,5},{5,4},{6,7},{7,6},{8,9},{9,8},{10,11... | collective-permute-start | bytes 3145736 | tf_op jit(solution)/shard_map/ppermute | solution.py:95
  136.0 14.2 %collective-permute-start.25 = (f32[200,128]{1,0:T(8,128)S(1)}, f32[200,128]{1,0:T(8,128)S(1)}, u32[]{:S(2)}, u32[]{:S(2)}) collective-permute-start(f32[200,128]{1,0:T(8,128)S(1)} %add.69), channel_id=1, source_target_pairs={{0,2},{1,3},{2,0},{3,1},{4,6},{5,7},{6,4},{7,5},{8,10},{9,11},{10,... | collective-permute-start | bytes 307208 | tf_op jit(solution)/shard_map/ppermute | solution.py:95
  150.6 24.8 %collective-permute-start.33 = (bf16[18,128,128]{2,1,0:T(8,128)(2,1)S(1)}, bf16[18,128,128]{2,1,0:T(8,128)(2,1)S(1)}, u32[]{:S(2)}, u32[]{:S(2)}) collective-permute-start(bf16[18,128,128]{2,1,0:T(8,128)(2,1)S(1)} %add_convert_fusion), channel_id=1, source_target_pairs={{0,2},{1,3},{2,0},{3,1},{4,6},{5,7},{6,4},{7,5},{8,10},{9,11},{10,... | collective-permute-start | bytes 1769480 | tf_op jit(solution)/shard_map/ppermute | solution.py:95
  151.0 23.3 %collective-permute-start.34 = (bf16[14,128,128]{2,1,0:T(8,128)(2,1)S(1)}, bf16[14,128,128]{2,1,0:T(8,128)(2,1)S(1)}, u32[]{:S(2)}, u32[]{:S(2)}) collective-permute-start(bf16[14,128,128]{2,1,0:T(8,128)(2,1)S(1)} %get-tuple-element.77), channel_id=1, source_target_pairs={{14,0},{15,1},{4,2},{5,3},{2,4},{3,5},{8,6},{9,7},{6,8},{7,9},{12,... | collective-permute-start | bytes 1376264 | tf_op jit(solution)/shard_map/ppermute | solution.py:95
  153.8 12.4 %collective-permute-start.26 = (f32[200,128]{1,0:T(8,128)S(1)}, f32[200,128]{1,0:T(8,128)S(1)}, u32[]{:S(2)}, u32[]{:S(2)}) collective-permute-start(f32[200,128]{1,0:T(8,128)S(1)} %add.70), channel_id=1, source_target_pairs={{0,4},{1,5},{2,6},{3,7},{4,0},{5,1},{6,2},{7,3},{8,12},{9,13},{10,... | collective-permute-start | bytes 307208 | tf_op jit(solution)/shard_map/ppermute | solution.py:95
  166.2 6.7 %collective-permute-start.27 = (f32[200,128]{1,0:T(8,128)S(1)}, f32[200,128]{1,0:T(8,128)S(1)}, u32[]{:S(2)}, u32[]{:S(2)}) collective-permute-start(f32[200,128]{1,0:T(8,128)S(1)} %add.71), channel_id=1, source_target_pairs={{0,8},{1,9},{2,10},{3,11},{4,12},{5,13},{6,14},{7,15},{8,0},{9,1},... | collective-permute-start | bytes 307208 | tf_op jit(solution)/shard_map/ppermute | solution.py:95
  198.2 6.6 %collective-permute-start.39 = (f32[208,128]{1,0:T(8,128)S(1)}, f32[208,128]{1,0:T(8,128)S(1)}, u32[]{:S(2)}, u32[]{:S(2)}) collective-permute-start(f32[208,128]{1,0:T(8,128)S(1)} %add.80), channel_id=1, source_target_pairs={{0,8},{1,9},{2,10},{3,11},{4,12},{5,13},{6,14},{7,15},{8,0},{9,1},... | collective-permute-start | bytes 319496 | tf_op jit(solution)/shard_map/ppermute | solution.py:95
  (46 other events, 861.2 us)
